TPU v7x, 256 devices: a whole 4x4x8 slice. The times are simulated.
256 devices in a mesh: ctx: 64 (over y, x_hi, z), head: 4 (over x_lo, core).
Axes of the slice: x: 4 (x_hi: 2, x_lo: 2; x = x_hi * 2 + x_lo), y: 4, z: 8, core: 2. Of those that a mesh axis runs over, the one named last changes fastest.
Arguments:
- query: bfloat16 [65536, 4096], P('ctx', 'head'), may hold values from -6 to 6
- key: bfloat16 [65536, 4096], P('ctx', 'head'), may hold values from -6 to 6
- value: bfloat16 [65536, 4096], P('ctx', 'head'), may hold values from -6 to 6
- windows: int32 [4096], P('ctx'), may hold values from 1 to 4, as said below
- out_weight: bfloat16 [4096, 4096], P(None, 'head'), may hold values from -0.09375 to 0.09375
Outputs:
- mixed: bfloat16 [65536, 4096], P('ctx', 'head')
Inputs may be any that keep to these rules, and one draw needn't show every extreme that they name: `windows`: both ends are reached in every draw.
All inputs are finite; a program needn't handle non-finite values.
Results may differ from a plain program's by a relative error of at most 0.0095.
Values may be sent and summed in bfloat16 or wider, within the bound.
No kernel may reach another device: no remote copies, remote signals or barrier semaphores. Data moves between devices by JAX's collectives and lax.ppermute only.
A program may use at most 128 MiB of HBM per device.

v0:
```python
import jax
import jax.numpy as jnp
from jax import lax
from jax.sharding import PartitionSpec as P

HD = 128
G = 16
WMAX = 4


def shifted(shard, axis, by):
    peers = lax.axis_size(axis)
    pairs = [(i, i + by) for i in range(peers) if 0 <= i + by < peers]
    return lax.ppermute(shard, axis, pairs)


def pooled(array, width):
    rows_total = array.shape[0]
    summed = jnp.sum(
        array.reshape(rows_total // width, width, array.shape[1]), axis=1, dtype=jnp.float32
    )
    return (summed / width).astype(jnp.bfloat16)


def scored(queries, keys_block, mask):
    values_f = jnp.einsum("qhe,khe->hqk", queries, keys_block, preferred_element_type=jnp.float32)
    values_f = values_f * HD ** (-0.5)
    return jnp.where(mask[None, :, :], values_f, -jnp.inf)


def local(query, key, value, windows, out_weight):
    tok_rows, local_width = query.shape
    heads_here = local_width // HD
    block_rows = G * G
    halo_rows = WMAX * G
    blocks_here = tok_rows // block_rows
    device_pos = lax.axis_index("ctx")
    first_token = device_pos * tok_rows
    key1 = pooled(key, G)
    value1 = pooled(value, G)
    key2 = pooled(key, block_rows)
    value2 = pooled(value, block_rows)
    prev_key, prev_value, prev_key1, prev_value1 = shifted(
        (
            key[tok_rows - halo_rows :],
            value[tok_rows - halo_rows :],
            key1[key1.shape[0] - G :],
            value1[value1.shape[0] - G :],
        ),
        "ctx",
        1,
    )
    far_key, far_value = (
        lax.all_gather(key2, "ctx", axis=0, tiled=True),
        lax.all_gather(value2, "ctx", axis=0, tiled=True),
    )
    coarse_total = far_key.shape[0]
    far_k = far_key.reshape(coarse_total, heads_here, HD)
    far_v = far_value.reshape(coarse_total, heads_here, HD)
    key_ext = jnp.concatenate([prev_key, key], axis=0)
    value_ext = jnp.concatenate([prev_value, value], axis=0)
    key1_ext = jnp.concatenate([prev_key1, key1], axis=0)
    value1_ext = jnp.concatenate([prev_value1, value1], axis=0)

    def one_block(block):
        local_first = block * block_rows
        rows_q = lax.dynamic_slice_in_dim(query, local_first, block_rows, 0).reshape(
            block_rows, heads_here, HD
        )
        near_k = lax.dynamic_slice_in_dim(key_ext, local_first, block_rows + halo_rows, 0).reshape(
            -1, heads_here, HD
        )
        near_v = lax.dynamic_slice_in_dim(
            value_ext, local_first, block_rows + halo_rows, 0
        ).reshape(-1, heads_here, HD)
        mid_k = lax.dynamic_slice_in_dim(key1_ext, block * G, 2 * G, 0).reshape(-1, heads_here, HD)
        mid_v = lax.dynamic_slice_in_dim(value1_ext, block * G, 2 * G, 0).reshape(
            -1, heads_here, HD
        )
        global_first = first_token + local_first
        token_i = global_first + jnp.arange(block_rows, dtype=jnp.int32)
        cell_i = token_i // G
        window_rows = jnp.repeat(lax.dynamic_slice_in_dim(windows, block * G, G, 0), G)
        token_j = global_first - halo_rows + jnp.arange(block_rows + halo_rows, dtype=jnp.int32)
        near_mask = (
            (token_j[None, :] >= 0)
            & (token_j[None, :] <= token_i[:, None])
            & (token_j[None, :] // G >= (cell_i - window_rows)[:, None])
        )
        cell_e = global_first // G - G + jnp.arange(2 * G, dtype=jnp.int32)
        mid_mask = (cell_e[None, :] >= 0) & (cell_e[None, :] <= (cell_i - window_rows - 1)[:, None])
        coarse_here = global_first // block_rows
        coarse_e = jnp.arange(coarse_total, dtype=jnp.int32)
        far_mask = jnp.broadcast_to(
            coarse_e[None, :] <= coarse_here - 2, (block_rows, coarse_total)
        )
        scores = jnp.concatenate(
            [
                scored(rows_q, near_k, near_mask),
                scored(rows_q, mid_k, mid_mask),
                scored(rows_q, far_k, far_mask),
            ],
            axis=2,
        )
        top = jnp.max(scores, axis=2, keepdims=True)
        weights = jnp.exp(scores - top).astype(jnp.bfloat16)
        total = jnp.sum(weights, axis=2, keepdims=True, dtype=jnp.float32)
        values_all = jnp.concatenate([near_v, mid_v, far_v], axis=0)
        summed = jnp.einsum("hqk,khe->qhe", weights, values_all, preferred_element_type=jnp.float32)
        result = summed / jnp.transpose(total, (1, 0, 2))
        finished = result.astype(jnp.bfloat16).reshape(block_rows, local_width)
        return finished

    mapped = lax.map(one_block, jnp.arange(blocks_here, dtype=jnp.int32))
    attended = mapped.reshape(tok_rows, local_width)
    projected = jnp.dot(
        lax.all_gather(attended, "head", axis=1, tiled=True),
        out_weight,
        preferred_element_type=jnp.float32,
    )
    return projected.astype(jnp.bfloat16)


def solution(mesh):
    in_specs = (P("ctx", "head"), P("ctx", "head"), P("ctx", "head"), P("ctx"), P(None, "head"))
    out_specs = P("ctx", "head")
    return jax.shard_map(local, mesh=mesh, in_specs=in_specs, out_specs=out_specs, check_vma=False)
```

profile of v0, /device:TPU:1, one launch (start us, length us, event | category | flops | bytes accessed | tf_op | source)
XLA Modules:
  0.0 555.8 jit_solution(1680363296847215885)
XLA Ops:
  6.5 2.6 bitcast_reduce_fusion.3
  9.2 4.4 collective-permute-start.1
  13.6 2.5 bitcast_reduce_fusion.1
  16.1 3.5 collective-permute-start.3
  19.7 0.7 slice.12
  20.4 4.2 collective-permute-start
  24.5 0.7 slice.14
  25.2 4.8 collective-permute-start.2
  30.0 0.4 bitcast_reduce_fusion.2
  30.4 0.4 bitcast_reduce_fusion
  30.8 149.6 %all-gather = bf16[64,4,1024]{2,1,0:T(4,128)(2,1)S(1)} all-gather(bf16[1,4,1024]{2,1,0:T(4,128)(2,1)S(1)} %fusion.21), channel_id=1, replica_groups=mesh['ctx'=64,'head'=4] {'ctx'}, dimensions={0}, use_global_device_ids=true | all-gather | bytes 532480 | tf_op jit(solution)/shard_map/all_gather | solution.py:55
  180.3 151.4 %all-gather.1 = bf16[64,4,1024]{2,1,0:T(4,128)(2,1)S(1)} all-gather(bf16[1,4,1024]{2,1,0:T(4,128)(2,1)S(1)} %fusion.22), channel_id=1, replica_groups=mesh['ctx'=64,'head'=4] {'ctx'}, dimensions={0}, use_global_device_ids=true | all-gather | bytes 532480 | tf_op jit(solution)/shard_map/all_gather | solution.py:54
  331.7 1.0 reshape.295
  332.7 1.9 copy.24
  334.8 0.9 copy.26
  335.7 1.7 pad_maximum_fusion.3
  337.5 2.5 pad_maximum_fusion
  339.9 2.5 pad_maximum_fusion.1
  342.4 59.6 %while.13 = (s32[]{:T(128)}, bf16[4,256,1024]{2,1,0:T(8,128)(2,1)}, s32[4]{0:T(128)S(1)}, bf16[1088,1024]{1,0:T(8,128)(2,1)}, bf16[80,1024]{1,0:T(8,128)(2,1)S(1...) while((s32[]{:T(128)}, bf16[4,256,1024]{2,1,0:T(8,128)(2,1)}, ...), condition=%wide.region_9.10_spmd, body=%wide.region_4.9_spmd.sunk | while | flops 658332160 | bytes 40920988 | solution.py:114
  342.4 0.7 dynamic_slice.63
  345.0 1.4 dynamic-slice_bitcast_fusion.7
  346.4 1.1 constant_dynamic-slice_fusion.2
  347.7 2.1 fusion.52
  349.8 1.5 fusion.50
  351.4 0.9 dynamic-slice_bitcast_fusion.6
  352.2 0.2 fusion.53
  352.5 2.3 convert_reduce_fusion.2
  355.1 1.2 fusion.54
  356.3 0.2 copy.65
  356.5 0.8 constant_dynamic-update-slice_fusion.2
  357.3 0.7 dynamic_slice.63
  359.9 1.4 dynamic-slice_bitcast_fusion.7
  361.3 1.1 constant_dynamic-slice_fusion.2
  362.6 2.0 fusion.52
  364.7 1.5 fusion.50
  366.3 0.9 dynamic-slice_bitcast_fusion.6
  367.1 0.2 fusion.53
  367.4 2.3 convert_reduce_fusion.2
  370.0 1.2 fusion.54
  371.2 0.2 copy.65
  371.4 0.8 constant_dynamic-update-slice_fusion.2
  372.2 0.7 dynamic_slice.63
  374.8 1.4 dynamic-slice_bitcast_fusion.7
  376.2 1.1 constant_dynamic-slice_fusion.2
  377.5 2.0 fusion.52
  379.6 1.5 fusion.50
  381.2 0.9 dynamic-slice_bitcast_fusion.6
  382.0 0.2 fusion.53
  382.3 2.3 convert_reduce_fusion.2
  384.9 1.2 fusion.54
  386.1 0.2 copy.65
  386.3 0.8 constant_dynamic-update-slice_fusion.2
  387.1 0.7 dynamic_slice.63
  389.7 1.4 dynamic-slice_bitcast_fusion.7
  391.1 1.1 constant_dynamic-slice_fusion.2
  392.4 2.0 fusion.52
  394.5 1.5 fusion.50
  396.1 0.9 dynamic-slice_bitcast_fusion.6
  396.9 0.2 fusion.53
  397.2 2.3 convert_reduce_fusion.2
  399.8 1.2 fusion.54
  401.2 0.8 constant_dynamic-update-slice_fusion.2
  402.1 132.3 %all-gather.4.cloned.1.call-done = bf16[1024,4096]{1,0:T(8,128)(2,1)} async-done(((bf16[1024,1024]{1,0:T(8,128)(2,1)}), bf16[1024,4096]{1,0:T(8,128)(2,1)}) %all-gather.4.cloned.1.call-update) | async-done | bytes 8388624 | tf_op jit(solution)/shard_map/all_gather | solution.py:117
  534.4 14.6 %convolution_convert_fusion = bf16[1024,1024]{1,0:T(8,128)(2,1)} fusion(bf16[1024,4096]{1,0:T(8,128)(2,1)} %all-gather.4.cloned.1.call-done, bf16[4096,1024]{1,0:T(8,128)(2,1)} %param.11), kind=kOutput, calls=%fused_computation.58 | convolution fusion | flops 8590983168 | bytes 18874368 | tf_op jit(solution)/shard_map/dot_general | solution.py:116
  (103 shorter events, 5.0 us)
Async XLA Ops:
  6.5 13.1 %copy-start.1 = (bf16[1024,1024]{1,0:T(8,128)(2,1)S(1)}, bf16[1024,1024]{1,0:T(8,128)(2,1)}, u32[]{:S(2)}) copy-start(bf16[1024,1024]{1,0:T(8,128)(2,1)} %param.9) | copy-start | bytes 6291460
  6.5 527.8 %all-gather.4.cloned.1.call-start = ((), (), s32[]{:S(2)}) async-start(), calls=%async_computation | async-start | bytes 10485760 | tf_op jit(solution)/shard_map/all_gather | solution.py:117
  6.5 18.0 %copy-start.2 = (bf16[1024,1024]{1,0:T(8,128)(2,1)S(1)}, bf16[1024,1024]{1,0:T(8,128)(2,1)}, u32[]{:S(2)}) copy-start(bf16[1024,1024]{1,0:T(8,128)(2,1)} %param.8) | copy-start | bytes 6291460
  9.2 326.5 %collective-permute-start.1 = (bf16[16,1024]{1,0:T(8,128)(2,1)S(1)}, bf16[16,1024]{1,0:T(8,128)(2,1)S(1)}, u32[]{:S(2)}, u32[]{:S(2)}) collective-permute-start(bf16[16,1024]{1,0:T(8,128)(2,1)S(1)} %slice.16), channel_id=1, source_target_pairs={{0,4},{4,8},{8,12},{12,16},{16,20},{20,24},{24,28},{28,32},{32,36}... | collective-permute-start | bytes 98312 | tf_op jit(solution)/shard_map/ppermute | solution.py:14
  16.1 14.6 %copy-start.4 = (bf16[64,1024]{1,0:T(8,128)(2,1)}, bf16[64,1024]{1,0:T(8,128)(2,1)S(1)}, u32[]{:S(2)}) copy-start(bf16[64,1024]{1,0:T(8,128)(2,1)S(1)} %multiply_convert_fusion) | copy-start | bytes 393220
  16.1 319.6 %collective-permute-start.3 = (bf16[16,1024]{1,0:T(8,128)(2,1)S(1)}, bf16[16,1024]{1,0:T(8,128)(2,1)S(1)}, u32[]{:S(2)}, u32[]{:S(2)}) collective-permute-start(bf16[16,1024]{1,0:T(8,128)(2,1)S(1)} %slice.17), channel_id=1, source_target_pairs={{0,4},{4,8},{8,12},{12,16},{16,20},{20,24},{24,28},{28,32},{32,36}... | collective-permute-start | bytes 98312 | tf_op jit(solution)/shard_map/ppermute | solution.py:14
  20.4 317.1 %collective-permute-start = (bf16[64,1024]{1,0:T(8,128)(2,1)}, bf16[64,1024]{1,0:T(8,128)(2,1)}, u32[]{:S(2)}, u32[]{:S(2)}) collective-permute-start(bf16[64,1024]{1,0:T(8,128)(2,1)} %slice.12), channel_id=1, source_target_pairs={{0,4},{4,8},{8,12},{12,16},{16,20},{20,24},{24,28},{28,32},{32,36}... | collective-permute-start | bytes 393224 | tf_op jit(solution)/shard_map/ppermute | solution.py:14
  25.2 314.7 %collective-permute-start.2 = (bf16[64,1024]{1,0:T(8,128)(2,1)}, bf16[64,1024]{1,0:T(8,128)(2,1)}, u32[]{:S(2)}, u32[]{:S(2)}) collective-permute-start(bf16[64,1024]{1,0:T(8,128)(2,1)} %slice.14), channel_id=1, source_target_pairs={{0,4},{4,8},{8,12},{12,16},{16,20},{20,24},{24,28},{28,32},{32,36}... | collective-permute-start | bytes 393224 | tf_op jit(solution)/shard_map/ppermute | solution.py:14
  335.7 4.2 copy-start.3
  339.9 2.5 copy-start.6
  352.5 2.6 copy-start
  352.5 2.6 copy-start.5
  367.4 2.6 copy-start
  367.4 2.6 copy-start.5
  382.3 2.6 copy-start
  382.3 2.6 copy-start.5
  397.2 2.6 copy-start
  397.2 2.6 copy-start.5
Sparse Core Ops, SparseCore 0:
  402.2 132.1 all-gather.3
where the time goes:
time: 557 us; the launch traced here: 556 us
  blocking collectives  301 us (54%)
  waiting for transfers between devices  132 us (24%)
  matrix products  34.2 us (6%)
  local copies, waits for them, and re-layouts  28.5 us (5%)
  other arithmetic  23 us (4%)
  starting transfers between devices  16.9 us (3%)
  between operations  13.5 us (2%)
  loops' own time  6.39 us (1%)
    all_gather x1, blocking collectives, local(): lax.all_gather(key2, 'ctx', axis=0, tiled=True)  151 us
    all_gather x1, blocking collectives, local(): lax.all_gather(value2, 'ctx', axis=0, tiled=True)  150 us
    all_gather x1, waiting for transfers between devices, local(): lax.all_gather(attended, 'head', axis=1, tiled=True)  132 us
    ppermute x4, starting transfers between devices, shifted(): return lax.ppermute(shard, axis, pairs)  16.9 us
    dot_general x12, matrix products, scored(): jnp.einsum('qhe,khe->hqk', queries, keys_block, preferred_element_type=jn...  14.9 us
    dot_general x1, matrix products, local(): jnp.dot(lax.all_gather(attended, 'head', axis=1, tiled=True), out_weight,...  14.6 us
  transfers between devices with their start and end apart: 5, of which 1 were waited for; matrix products, arithmetic and copies ran while one was open for 2% of the time, Pallas kernels for 0%

commit v1 on v0

v1 whole, which is shorter than its diff:
```python
import functools

import jax
import jax.numpy as jnp
from jax import lax
from jax.experimental import pallas as pl
from jax.experimental.pallas import tpu as pltpu
from jax.sharding import Mesh
from jax.sharding import PartitionSpec as P

HD = 128
G = 16
WMAX = 4
HALO = WMAX * G
LOG2E = 1.4426950408889634
SCALE = HD ** (-0.5) * LOG2E
CTX = ("y", "xh", "z")
TILE = 128
NEAR = TILE + HALO
SPAN = 256
CHUNK = 2
VMEM = 48 * 1024 * 1024


def params(**kw):
    return pltpu.CompilerParams(vmem_limit_bytes=VMEM, **kw)


def cost(flops, nbytes, trans=0):
    return pl.CostEstimate(flops=flops, bytes_accessed=nbytes, transcendentals=trans)


def shift(x, axis, by):
    n = lax.axis_size(axis)
    return lax.ppermute(x, axis, [(i, (i + by) % n) for i in range(n)])


def pool_kernel(k_ref, v_ref, k1_ref, v1_ref, far_ref):
    rows = k_ref.shape[0]
    cells = rows // G
    coarse = cells // G
    r = lax.broadcasted_iota(jnp.int32, (cells, rows), 0)
    t = lax.broadcasted_iota(jnp.int32, (cells, rows), 1)
    pick = jnp.where(t // G == r, 1.0, 0.0).astype(jnp.bfloat16)
    for src, one, slot in ((k_ref, k1_ref, 0), (v_ref, v1_ref, 1)):
        sums = jnp.dot(pick, src[...], preferred_element_type=jnp.float32)
        one[...] = (sums * (1.0 / G)).astype(jnp.bfloat16)
        whole = jnp.sum(sums.reshape(coarse, G, sums.shape[1]), axis=1)
        far_ref[slot] = (whole * (1.0 / (G * G))).astype(jnp.bfloat16)


def pool(key, value):
    rows, width = key.shape
    cols = 256
    cells, coarse = rows // G, rows // (G * G)
    spec = lambda n: pl.BlockSpec((n, cols), lambda i: (0, i))
    return pl.pallas_call(
        pool_kernel,
        grid=(width // cols,),
        in_specs=[spec(rows), spec(rows)],
        out_specs=[spec(cells), spec(cells), pl.BlockSpec((2, coarse, cols), lambda i: (0, 0, i))],
        out_shape=[
            jax.ShapeDtypeStruct((cells, width), jnp.bfloat16),
            jax.ShapeDtypeStruct((cells, width), jnp.bfloat16),
            jax.ShapeDtypeStruct((2, coarse, width), jnp.bfloat16),
        ],
        compiler_params=params(),
        cost_estimate=cost(2 * cells * rows * width * 2, 4 * rows * width),
        name="pool",
    )(key, value)


def near_kernel(q_ref, k_ref, v_ref, k1_ref, v1_ref, halo_ref, bias_ref, out_ref, lse_ref):
    rows = q_ref.shape[0]
    h = pl.program_id(0)
    ones = jnp.ones((SPAN, HD), jnp.bfloat16)
    pad = jnp.zeros((SPAN - NEAR - 2 * G, HD), jnp.bfloat16)
    lane = lax.broadcasted_iota(jnp.int32, (TILE, HD), 1)

    def rows_of(src, src1, base, base1, t):
        b = t * TILE // (G * G)
        if t == 0:
            near = [halo_ref[base : base + HALO, :], src[:TILE, :]]
        else:
            near = [src[t * TILE - HALO : (t + 1) * TILE, :]]
        if b == 0:
            mid = [halo_ref[base1 : base1 + G, :], src1[:G, :]]
        else:
            mid = [src1[(b - 1) * G : (b + 1) * G, :]]
        return jnp.concatenate(near + mid + [pad], axis=0)

    for t in range(rows // TILE):
        at = pl.ds(t * TILE, TILE)
        keys = rows_of(k_ref, k1_ref, 0, 2 * HALO, t)
        values = rows_of(v_ref, v1_ref, HALO, 2 * HALO + G, t)
        s = lax.dot_general(
            q_ref[at, :], keys, (((1,), (1,)), ((), ())), preferred_element_type=jnp.float32
        )
        s = s * SCALE + bias_ref[at, :]
        top = jnp.max(s, axis=1, keepdims=True)
        w = jnp.exp2(s - top).astype(jnp.bfloat16)
        both = jnp.dot(
            w, jnp.concatenate([values, ones], axis=1), preferred_element_type=jnp.float32
        )
        total = both[:, HD:]
        out_ref[at, :] = (both[:, :HD] / total).astype(jnp.bfloat16)
        lse = top + jnp.log2(total)

        @pl.when(h == 0)
        def _():
            lse_ref[at, :] = lse

        @pl.when(h > 0)
        def _():
            lse_ref[at, :] = jnp.where(lane == h, lse, lse_ref[at, :])


def near(query, key, value, key1, value1, halo, bias, first, heads):
    rows = query.shape[0]
    spec = lambda n: pl.BlockSpec((n, HD), lambda i: (0, first + i))
    whole = lambda n, w: pl.BlockSpec((n, w), lambda i: (0, 0))
    return pl.pallas_call(
        near_kernel,
        grid=(heads,),
        in_specs=[
            spec(rows), spec(rows), spec(rows), spec(rows // G), spec(rows // G),
            spec(halo.shape[0]), whole(rows, SPAN),
        ],
        out_specs=[pl.BlockSpec((rows, HD), lambda i: (0, i)), whole(rows, HD)],
        out_shape=[
            jax.ShapeDtypeStruct((rows, heads * HD), jnp.bfloat16),
            jax.ShapeDtypeStruct((rows, HD), jnp.float32),
        ],
        compiler_params=params(),
        cost_estimate=cost(
            2 * rows * SPAN * 3 * HD * heads, 8 * rows * HD * heads, rows * SPAN * heads
        ),
        name="near",
    )(query, key, value, key1, value1, halo, bias)


def far_kernel(lim_ref, q_ref, n_ref, lse_ref, k2_ref, v2_ref, cell_ref, out_ref):
    rows = q_ref.shape[0]
    heads = q_ref.shape[1] // HD
    cells = k2_ref.shape[1]
    ones = jnp.ones((cells, HD), jnp.bfloat16)
    cell = cell_ref[...]
    for h in range(heads):
        cols = slice(h * HD, (h + 1) * HD)
        keys = k2_ref[0, :, cols]
        values = jnp.concatenate([v2_ref[0, :, cols], ones], axis=1)
        for t in range(rows // TILE):
            at = slice(t * TILE, (t + 1) * TILE)
            last = lim_ref[0] + t * TILE // (G * G)
            bias = jnp.where(cell <= last, 0.0, -jnp.inf)
            s = lax.dot_general(
                q_ref[at, cols], keys, (((1,), (1,)), ((), ())), preferred_element_type=jnp.float32
            )
            s = s * SCALE + bias
            lse = lse_ref[at, h : h + 1]
            top = jnp.maximum(jnp.max(s, axis=1, keepdims=True), lse)
            w = jnp.exp2(s - top).astype(jnp.bfloat16)
            both = jnp.dot(w, values, preferred_element_type=jnp.float32)
            part = jnp.exp2(lse - top)
            summed = both[:, :HD] + n_ref[at, cols].astype(jnp.float32) * part
            out_ref[at, cols] = (summed / (both[:, HD:] + part)).astype(jnp.bfloat16)


def far(lim, query, partial, lse, kv2, col, cell, first):
    rows, width = partial.shape
    cells = kv2.shape[1]
    return pl.pallas_call(
        far_kernel,
        grid_spec=pltpu.PrefetchScalarGridSpec(
            num_scalar_prefetch=1,
            grid=(1,),
            in_specs=[
                pl.BlockSpec((rows, width), lambda i, s: (0, first)),
                pl.BlockSpec((rows, width), lambda i, s: (0, 0)),
                pl.BlockSpec((rows, HD), lambda i, s: (0, 0)),
                pl.BlockSpec((1, cells, width), lambda i, s: (0, 0, col)),
                pl.BlockSpec((1, cells, width), lambda i, s: (1, 0, col)),
                pl.BlockSpec((1, cells), lambda i, s: (0, 0)),
            ],
            out_specs=pl.BlockSpec((rows, width), lambda i, s: (0, 0)),
        ),
        out_shape=jax.ShapeDtypeStruct((rows, width), jnp.bfloat16),
        compiler_params=params(),
        cost_estimate=cost(2 * rows * cells * 3 * width, 8 * rows * width, rows * cells * 2),
        name="far",
    )(lim, query, partial, lse, kv2, kv2, cell)


def project_kernel(n, has_acc, place_ref, *refs):
    pieces, weights = refs[:n], refs[n : 2 * n]
    out_ref = refs[-1]
    total = refs[2 * n][...] if has_acc else None
    for piece, weight in zip(pieces, weights):
        term = jnp.dot(piece[...], weight[...], preferred_element_type=jnp.float32)
        total = term if total is None else total + term
    out_ref[...] = total.astype(out_ref.dtype)


def project(pieces, places, weight, acc, dtype):
    n = len(pieces)
    rows, width = pieces[0].shape
    cols = weight.shape[1]
    tile = 256
    specs = [pl.BlockSpec((tile, width), lambda i, s: (i, 0)) for _ in pieces]
    specs += [pl.BlockSpec((width, cols), lambda i, s, j=j: (s[j], 0)) for j in range(n)]
    args = list(pieces) + [weight] * n
    if acc is not None:
        specs.append(pl.BlockSpec((tile, cols), lambda i, s: (i, 0)))
        args.append(acc)
    return pl.pallas_call(
        functools.partial(project_kernel, n, acc is not None),
        grid_spec=pltpu.PrefetchScalarGridSpec(
            num_scalar_prefetch=1,
            grid=(rows // tile,),
            in_specs=specs,
            out_specs=pl.BlockSpec((tile, cols), lambda i, s: (i, 0)),
        ),
        out_shape=jax.ShapeDtypeStruct((rows, cols), dtype),
        compiler_params=params(),
        cost_estimate=cost(2 * rows * width * n * cols, n * width * (rows + cols) * 2 + rows * cols * 4),
        name="project",
    )(jnp.stack(places).astype(jnp.int32), *args)


def near_bias(windows, ctx, rows):
    row = jnp.arange(rows, dtype=jnp.int32)[:, None]
    lane = jnp.arange(SPAN, dtype=jnp.int32)[None, :]
    token = ctx * rows + row
    cell = token // G
    window = jnp.broadcast_to(windows[:, None], (windows.shape[0], G)).reshape(rows, 1)
    other = ctx * rows + row // TILE * TILE - HALO + lane
    near_ok = (other >= 0) & (other <= token) & (other // G >= cell - window)
    mid = token // (G * G) * G - G + lane - NEAR
    mid_ok = (mid >= 0) & (mid <= cell - window - 1)
    ok = jnp.where(lane < NEAR, near_ok, mid_ok & (lane < NEAR + 2 * G))
    return jnp.where(ok, 0.0, -jnp.inf).astype(jnp.float32)


def local(query, key, value, windows, out_weight):
    rows, width = query.shape
    heads = width // HD
    ny, nz = lax.axis_size("y"), lax.axis_size("z")
    iy, ix, iz = (lax.axis_index(a) for a in CTX)
    ctx = lax.axis_index(CTX)
    coarse = rows // (G * G)

    key1, value1, mine = pool(key, value)

    other = lax.ppermute(mine, "xh", [(0, 1), (1, 0)])
    x = jnp.concatenate([mine, other], axis=1)[:, None]
    a, b = shift(x, "z", 1), shift(x, "z", -1)
    x = jnp.concatenate([x, a, b], axis=1)
    c, d = shift(x, "z", 3), shift(x[:, :2], "z", -3)
    x = jnp.concatenate([x, c, d], axis=1)
    zs = (iz + jnp.array([0, -1, 1, -3, -4, -2, 3, 2], jnp.int32)) % nz
    ys = (iy + jnp.array([0, -1, 1, -2], jnp.int32)) % ny
    xs = jnp.stack([ix, 1 - ix])
    cell = (
        ((ys[:, None, None] * 2 + xs[None, None, :]) * nz + zs[None, :, None])[..., None] * coarse
        + jnp.arange(coarse, dtype=jnp.int32)
    ).reshape(1, -1)

    def over_y(part):
        parts = [part] + [shift(part, "y", s) for s in (1, -1, 2)]
        return jnp.concatenate(parts, axis=1).reshape(2, -1, part.shape[-1])

    step = CHUNK * HD
    gathered = [over_y(x[..., :step]), over_y(x[..., step:])]

    halo = lax.ppermute(
        jnp.concatenate([key[rows - HALO :], value[rows - HALO :], key1[-G:], value1[-G:]], axis=0),
        CTX,
        [(i, i + 1) for i in range(lax.axis_size(CTX) - 1)],
    )
    bias = near_bias(windows, ctx, rows)
    lim = (ctx * coarse - 2).reshape(1).astype(jnp.int32)
    xl, core = lax.axis_index("xl"), lax.axis_index("core")

    chunks = heads // CHUNK
    pieces, places = [], []
    for i in range(chunks):
        part, lse = near(query, key, value, key1, value1, halo, bias, i * CHUNK, CHUNK)
        kv2, col = (gathered[0], 0) if i == 0 else (gathered[1], i - 1)
        own = far(lim, query, part, lse, kv2, col, cell, i)
        across = lax.ppermute(own, "xl", [(0, 1), (1, 0)])
        beside = lax.ppermute(own, "core", [(0, 1), (1, 0)])
        diagonal = lax.ppermute(across, "core", [(0, 1), (1, 0)])
        for piece, px, pc in (
            (own, xl, core), (beside, xl, 1 - core), (across, 1 - xl, core), (diagonal, 1 - xl, 1 - core),
        ):
            pieces.append(piece)
            places.append((px * 2 + pc) * chunks + i)
    early = len(pieces) - 2
    acc = project(pieces[:early], places[:early], out_weight, None, jnp.float32)
    return project(pieces[early:], places[early:], out_weight, acc, jnp.bfloat16)


def solution(mesh):
    split = Mesh(mesh.devices.reshape(4, 2, 8, 2, 2), CTX + ("xl", "core"))
    rows, cols = CTX, ("xl", "core")
    in_specs = (P(rows, cols), P(rows, cols), P(rows, cols), P(rows), P(None, cols))
    return jax.shard_map(
        local, mesh=split, in_specs=in_specs, out_specs=P(rows, cols), check_vma=False
    )
```

time: 557 us -> 148 us (0.27)
  blocking collectives: 301 us -> 0 us
  waiting for transfers between devices: 132 us -> 31.4 us
  Pallas kernels: 0 us -> 62 us
  matrix products: 34.2 us -> 0 us
  other arithmetic: 23 us -> 4.56 us
  starting transfers between devices: 16.9 us -> 32.8 us
  between operations: 13.5 us -> 0.46 us
  local copies, waits for them, and re-layouts: 28.5 us -> 15.7 us
  loops' own time: 6.39 us -> 0 us
    all_gather x2 -> x0, blocking collectives: 301 us -> none  [the longest x1 151 us: local(): lax.all_gather(key2, 'ctx', axis=0, tiled=True)]
    all_gather x1 -> x0, waiting for transfers between devices: 132 us -> none  [local(): lax.all_gather(attended, 'head', axis=1, tiled=True)]
    pallas_call x0 -> x11, Pallas kernels: none -> 62 us  [the longest x4 32 us: near(): pl.pallas_call(near_kernel, grid=(heads,), in_specs=[spec(rows), spec(row...]
    dot_general x17 -> x0, matrix products: 34.2 us -> none  [the longest x12 14.9 us: scored(): jnp.einsum('qhe,khe->hqk', queries, keys_block, preferred_element_type=jn...]
    ppermute x4 -> x24, waiting for transfers between devices: 0.01 us -> 31.4 us  [the longest x10 16.7 us: shift(): return lax.ppermute(x, axis, [(i, (i + by) % n) for i in range(n)])]
    ppermute x4 -> x24, starting transfers between devices: 16.9 us -> 32.8 us  [the longest x10 13.5 us: shift(): return lax.ppermute(x, axis, [(i, (i + by) % n) for i in range(n)])]
    reduce_sum x8 -> x0, other arithmetic: 14.9 us -> none  [the longest x4 9.07 us: one_block(): total = jnp.sum(weights, axis=2, keepdims=True, dtype=jnp.float32)]
    unnamed x10 -> x53, local copies, waits for them, and re-layouts: 0.02 us -> 14.5 us
  transfers between devices with their start and end apart: 5 -> 24, of which waited for: 1 -> 6; matrix products, arithmetic and copies ran while one was open for 2% -> 4% of each run, Pallas kernels for 0% -> 31%
where the time goes in v1:
time: 148 us; the launch traced here: 147 us
  Pallas kernels  62 us (42%)
  starting transfers between devices  32.8 us (22%)
  waiting for transfers between devices  31.4 us (21%)
  local copies, waits for them, and re-layouts  15.7 us (11%)
  other arithmetic  4.56 us (3%)
    pallas_call x4, Pallas kernels, near(): pl.pallas_call(near_kernel, grid=(heads,), in_specs=[spec(rows), spec(row...  32 us
    pallas_call x2, Pallas kernels, project(): pl.pallas_call(functools.partial(project_kernel, n, acc is not None), gri...  18.4 us
    ppermute x10, waiting for transfers between devices, shift(): return lax.ppermute(x, axis, [(i, (i + by) % n) for i in range(n)])  16.7 us
    ppermute x4, waiting for transfers between devices, local(): across = lax.ppermute(own, 'xl', [(0, 1), (1, 0)])  14.7 us
    unnamed x53, local copies, waits for them, and re-layouts  14.5 us
    ppermute x10, starting transfers between devices, shift(): return lax.ppermute(x, axis, [(i, (i + by) % n) for i in range(n)])  13.5 us
    pallas_call x4, Pallas kernels, far(): pl.pallas_call(far_kernel, grid_spec=pltpu.PrefetchScalarGridSpec(num_sca...  9.6 us
    ppermute x4, starting transfers between devices, local(): beside = lax.ppermute(own, 'core', [(0, 1), (1, 0)])  5.98 us
  transfers between devices with their start and end apart: 24, of which 6 were waited for; matrix products, arithmetic and copies ran while one was open for 4% of the time, Pallas kernels for 31%

profile of v1, /device:TPU:1, one launch (start us, length us, event | category | flops | bytes accessed | tf_op | source)
XLA Modules:
  0.0 146.9 jit_solution(6071360200125932850)
XLA Ops:
  0.0 1.6 %copy-done.1 = bf16[1024,1024]{1,0:T(8,128)(2,1)S(1)} copy-done((bf16[1024,1024]{1,0:T(8,128)(2,1)S(1)}, bf16[1024,1024]{1,0:T(8,128)(2,1)}, u32[]{:S(2)}) %copy-start.1) | copy-done | bytes 2097176
  1.6 1.6 %copy-done.2 = bf16[1024,1024]{1,0:T(8,128)(2,1)S(1)} copy-done((bf16[1024,1024]{1,0:T(8,128)(2,1)S(1)}, bf16[1024,1024]{1,0:T(8,128)(2,1)}, u32[]{:S(2)}) %copy-start.2) | copy-done | bytes 2097176
  3.2 1.9 %pool.1 = (bf16[64,1024]{1,0:T(8,128)(2,1)S(1)}, bf16[64,1024]{1,0:T(8,128)(2,1)S(1)}, bf16[2,4,1024]{2,1,0:T(4,128)(2,1)S(1)}) custom-call(bf16[1024,1024]{1,0:T(8,128)(2,1)S(1)} %copy-done.1, bf16[1024,1024]{1,0:T(8,128)(2,1)S(1)} %copy-done.2), custom_call_target="tpu_custom_call" | custom-call | flops 268435456 | bytes 4194304 | tf_op jit(solution)/shard_map/pool/pallas_call | solution.py:57
  5.2 3.7 %collective-permute-start.1 = (bf16[2,4,1024]{2,1,0:T(4,128)(2,1)S(1)}, bf16[2,4,1024]{2,1,0:T(4,128)(2,1)S(1)}, u32[]{:S(2)}, u32[]{:S(2)}) collective-permute-start(bf16[2,4,1024]{2,1,0:T(4,128)(2,1)S(1)} %get-tuple-element.20), channel_id=1, source_target_pairs={{0,32},{32,0},{1,33},{33,1},{2,34},{34,2},{3,35},{35,3},{4,36},{36... | collective-permute-start | bytes 49160 | tf_op jit(solution)/shard_map/ppermute | solution.py:254
  8.9 0.7 pad_maximum_fusion.1
  9.6 3.6 %collective-permute-start = (bf16[160,1024]{1,0:T(8,128)(2,1)}, bf16[160,1024]{1,0:T(8,128)(2,1)S(1)}, u32[]{:S(2)}, u32[]{:S(2)}) collective-permute-start(bf16[160,1024]{1,0:T(8,128)(2,1)} %pad_maximum_fusion.1), channel_id=1, source_target_pairs={{0,4},{4,8},{8,12},{12,16},{16,20},{20,24},{24,28},{28,32},{32,36}... | collective-permute-start | bytes 983048 | tf_op jit(solution)/shard_map/ppermute | solution.py:275
  13.3 0.1 broadcast_in_dim.19
  13.4 0.1 reshape.209
  13.5 0.1 pad_add_fusion.1
  13.6 0.1 add_multiply_fusion.1
  13.6 1.7 %fusion.10.bias_ref = f32[1024,256]{1,0:T(8,128)S(1)} fusion(s32[1024]{0:T(1024)S(1)} %get-tuple-element.27, s32[1024]{0:T(1024)S(1)} %get-tuple-element.30, s32[1024]{0:T(1024)S(1)} %get-tuple-element.28, s32[1024]{0:T(1024)S(1)} %iota_add_fusion.2, s32[1024]{0:T(1024)S(1)} %get-tuple-element.29, pred[256]{0:T(512)(128)(4,1)S(1)} %get-tuple-element.31, ...), kind=kLoop, calls=%fused_computation.17 | loop fusion | flops 7602176 | bytes 1069568 | tf_op jit(solution)/shard_map/jit(_where)/select_n | solution.py:241
  15.3 0.1 add_multiply_fusion
  15.4 4.0 %collective-permute-start.3 = (bf16[2,1,8,1024]{3,2,0,1:T(8,128)(2,1)S(1)}, bf16[2,1,8,1024]{3,2,0,1:T(8,128)(2,1)S(1)}, u32[]{:S(2)}, u32[]{:S(2)}) collective-permute-start(bf16[2,1,8,1024]{3,2,0,1:T(8,128)(2,1)S(1)} %maximum_bitcast_fusion), channel_id=1, source_target_pairs={{0,28},{4,0},{8,4},{12,8},{16,12},{20,16},{24,20},{28,24},{1,29},{... | collective-permute-start | bytes 98312 | tf_op jit(solution)/shard_map/ppermute | solution.py:35
  19.5 5.3 %collective-permute-done.2 = bf16[2,1,8,1024]{3,2,0,1:T(8,128)(2,1)S(1)} collective-permute-done((bf16[2,1,8,1024]{3,2,0,1:T(8,128)(2,1)S(1)}, bf16[2,1,8,1024]{3,2,0,1:T(8,128)(2,1)S(1)}, u32[]{:S(2)}, u32[]{:S(2)}) %collective-permute-start.2) | collective-permute-done | bytes 32800 | tf_op jit(solution)/shard_map/ppermute | solution.py:35
  24.8 2.4 %collective-permute-start.5 = (bf16[2,2,8,1024]{3,2,0,1:T(8,128)(2,1)S(1)}, bf16[2,2,8,1024]{3,2,0,1:T(8,128)(2,1)S(1)}, u32[]{:S(2)}, u32[]{:S(2)}) collective-permute-start(bf16[2,2,8,1024]{3,2,0,1:T(8,128)(2,1)S(1)} %pad_maximum_fusion.4), channel_id=1, source_target_pairs={{0,20},{4,24},{8,28},{12,0},{16,4},{20,8},{24,12},{28,16},{1,21},{... | collective-permute-start | bytes 196616 | tf_op jit(solution)/shard_map/ppermute | solution.py:35
  27.2 1.0 collective-permute-start.4
  28.3 8.9 %collective-permute-done.4 = bf16[2,3,8,1024]{3,2,0,1:T(8,128)(2,1)S(1)} collective-permute-done((bf16[2,3,8,1024]{3,2,0,1:T(8,128)(2,1)S(1)}, bf16[2,3,8,1024]{3,2,0,1:T(8,128)(2,1)S(1)}, u32[]{:S(2)}, u32[]{:S(2)}) %collective-permute-start.4) | collective-permute-done | bytes 98336 | tf_op jit(solution)/shard_map/ppermute | solution.py:35
  37.2 0.7 copy-done.20
  37.9 3.0 %collective-permute-start.13 = (bf16[2,8,8,256]{3,2,0,1:T(8,128)(2,1)S(1)}, bf16[2,8,8,256]{3,2,0,1:T(8,128)(2,1)}, u32[]{:S(2)}, u32[]{:S(2)}) collective-permute-start(bf16[2,8,8,256]{3,2,0,1:T(8,128)(2,1)S(1)} %slice.27), channel_id=1, source_target_pairs={{0,128},{64,192},{128,0},{192,64},{1,129},{65,193},{129,1},{193,65... | collective-permute-start | bytes 196616 | tf_op jit(solution)/shard_map/ppermute | solution.py:35
  40.9 0.8 collective-permute-start.12
  41.7 0.7 collective-permute-start.11
  42.3 0.7 iota_add_fusion.1
  43.1 0.9 add.275.cell_ref
  43.9 0.2 collective-permute-done.12
  44.1 2.3 %collective-permute-done.11 = bf16[2,8,8,256]{3,2,0,1:T(8,128)(2,1)} collective-permute-done((bf16[2,8,8,256]{3,2,0,1:T(8,128)(2,1)S(1)}, bf16[2,8,8,256]{3,2,0,1:T(8,128)(2,1)}, u32[]{:S(2)}, u32[]{:S(2)}) %collective-permute-start.11) | collective-permute-done | bytes 65568 | tf_op jit(solution)/shard_map/ppermute | solution.py:35
  46.4 0.9 copy_bitcast_fusion.1.k2_ref.v2_ref
  47.4 0.9 copy-done.5
  48.3 0.9 copy-done.7
  49.2 8.0 %near.5 = (bf16[1024,256]{1,0:T(8,128)(2,1)S(1)}, f32[1024,128]{1,0:T(8,128)S(1)}) custom-call(bf16[1024,1024]{1,0:T(8,128)(2,1)S(1)} %copy-done, bf16[1024,1024]{1,0:T(8,128)(2,1)} %k_ref.9, bf16[1024,1024]{1,0:T(8,128)(2,1)} %v_ref.9, bf16[64,1024]{1,0:T(8,128)(2,1)S(1)} %copy-done.5, bf16[64,1024]{1,0:T(8,128)(2,1)S(1)} %copy-done.7, ...), custom_call_target="tpu_custom_call" | custom-call | flops 402653184 | bytes 2097152 | tf_op jit(solution)/shard_map/near/pallas_call | solution.py:122
  57.2 2.2 %far.5.refs_0_ = bf16[1024,256]{1,0:T(8,128)(2,1)S(1)} custom-call(s32[1]{0:T(128)} %bitcast.2.lim_ref, bf16[1024,1024]{1,0:T(8,128)(2,1)S(1)} %copy-done, bf16[1024,256]{1,0:T(8,128)(2,1)S(1)} %get-tuple-element.21.n_ref, f32[1024,128]{1,0:T(8,128)S(1)} %get-tuple-element.22.lse_ref, bf16[2,256,256]{2,1,0:T(8,128)(2,1)S(1)} %copy_bitcast_fusion.1.k2_ref.v2_ref, ...), custom_call_target="tpu_custom_call" | custom-call | flops 402653184 | bytes 2097152 | tf_op jit(solution)/shard_map/far/pallas_call | solution.py:172
  59.3 0.6 collective-permute-start.15
  60.0 0.1 collective-permute-start.8
  60.1 1.5 %collective-permute-start.7 = (bf16[2,8,8,768]{3,2,0,1:T(8,128)(2,1)S(1)}, bf16[2,8,8,768]{3,2,0,1:T(8,128)(2,1)S(1)}, u32[]{:S(2)}, u32[]{:S(2)}) collective-permute-start(bf16[2,8,8,768]{3,2,0,1:T(8,128)(2,1)S(1)} %slice.26), channel_id=1, source_target_pairs={{0,192},{64,0},{128,64},{192,128},{1,193},{65,1},{129,65},{193,129... | collective-permute-start | bytes 589832 | tf_op jit(solution)/shard_map/ppermute | solution.py:35
  61.6 5.2 %collective-permute-start.14 = (bf16[1024,256]{1,0:T(8,128)(2,1)S(1)}, bf16[1024,256]{1,0:T(8,128)(2,1)S(1)}, u32[]{:S(2)}, u32[]{:S(2)}) collective-permute-start(bf16[1024,256]{1,0:T(8,128)(2,1)S(1)} %far.5.refs_0_), channel_id=1, source_target_pairs={{0,1},{1,0},{2,3},{3,2},{4,5},{5,4},{6,7},{7,6},{8,9},{9,8},{10,11... | collective-permute-start | bytes 1572872 | tf_op jit(solution)/shard_map/ppermute | solution.py:291
  66.8 8.0 %near.7 = (bf16[1024,256]{1,0:T(8,128)(2,1)S(1)}, f32[1024,128]{1,0:T(8,128)S(1)}) custom-call(bf16[1024,1024]{1,0:T(8,128)(2,1)S(1)} %copy-done, bf16[1024,1024]{1,0:T(8,128)(2,1)} %k_ref.9, bf16[1024,1024]{1,0:T(8,128)(2,1)} %v_ref.9, bf16[64,1024]{1,0:T(8,128)(2,1)S(1)} %copy-done.5, bf16[64,1024]{1,0:T(8,128)(2,1)S(1)} %copy-done.7, ...), custom_call_target="tpu_custom_call" | custom-call | flops 402653184 | bytes 2097152 | tf_op jit(solution)/shard_map/near/pallas_call | solution.py:122
  74.8 8.0 %near.6 = (bf16[1024,256]{1,0:T(8,128)(2,1)S(1)}, f32[1024,128]{1,0:T(8,128)S(1)}) custom-call(bf16[1024,1024]{1,0:T(8,128)(2,1)S(1)} %copy-done, bf16[1024,1024]{1,0:T(8,128)(2,1)} %k_ref.9, bf16[1024,1024]{1,0:T(8,128)(2,1)} %v_ref.9, bf16[64,1024]{1,0:T(8,128)(2,1)S(1)} %copy-done.5, bf16[64,1024]{1,0:T(8,128)(2,1)S(1)} %copy-done.7, ...), custom_call_target="tpu_custom_call" | custom-call | flops 402653184 | bytes 2097152 | tf_op jit(solution)/shard_map/near/pallas_call | solution.py:122
  82.8 0.1 copy_bitcast_fusion.k2_ref.v2_ref
  82.9 2.2 %far.7.refs_8_ = bf16[1024,256]{1,0:T(8,128)(2,1)S(1)} custom-call(s32[1]{0:T(128)} %bitcast.2.lim_ref, bf16[1024,1024]{1,0:T(8,128)(2,1)S(1)} %copy-done, bf16[1024,256]{1,0:T(8,128)(2,1)S(1)} %get-tuple-element.25.n_ref, f32[1024,128]{1,0:T(8,128)S(1)} %get-tuple-element.26.lse_ref, bf16[2,256,768]{2,1,0:T(8,128)(2,1)S(1)} %copy_bitcast_fusion.k2_ref.v2_ref, ...), custom_call_target="tpu_custom_call" | custom-call | flops 402653184 | bytes 2097152 | tf_op jit(solution)/shard_map/far/pallas_call | solution.py:172
  85.1 1.2 collective-permute-start.21
  86.3 0.3 collective-permute-start.20
  86.6 2.2 %far.6.refs_4_ = bf16[1024,256]{1,0:T(8,128)(2,1)S(1)} custom-call(s32[1]{0:T(128)} %bitcast.2.lim_ref, bf16[1024,1024]{1,0:T(8,128)(2,1)S(1)} %copy-done, bf16[1024,256]{1,0:T(8,128)(2,1)S(1)} %get-tuple-element.23.n_ref, f32[1024,128]{1,0:T(8,128)S(1)} %get-tuple-element.24.lse_ref, bf16[2,256,768]{2,1,0:T(8,128)(2,1)S(1)} %copy_bitcast_fusion.k2_ref.v2_ref, ...), custom_call_target="tpu_custom_call" | custom-call | flops 402653184 | bytes 2097152 | tf_op jit(solution)/shard_map/far/pallas_call | solution.py:172
  88.9 0.4 collective-permute-start.18
  89.3 0.5 collective-permute-start.17
  89.8 8.0 %near.4 = (bf16[1024,256]{1,0:T(8,128)(2,1)S(1)}, f32[1024,128]{1,0:T(8,128)S(1)}) custom-call(bf16[1024,1024]{1,0:T(8,128)(2,1)S(1)} %copy-done, bf16[1024,1024]{1,0:T(8,128)(2,1)} %k_ref.9, bf16[1024,1024]{1,0:T(8,128)(2,1)} %v_ref.9, bf16[64,1024]{1,0:T(8,128)(2,1)S(1)} %copy-done.5, bf16[64,1024]{1,0:T(8,128)(2,1)S(1)} %copy-done.7, ...), custom_call_target="tpu_custom_call" | custom-call | flops 402653184 | bytes 2097152 | tf_op jit(solution)/shard_map/near/pallas_call | solution.py:122
  97.8 3.0 %far.4.refs_12_ = bf16[1024,256]{1,0:T(8,128)(2,1)} custom-call(s32[1]{0:T(128)} %bitcast.2.lim_ref, bf16[1024,1024]{1,0:T(8,128)(2,1)S(1)} %copy-done, bf16[1024,256]{1,0:T(8,128)(2,1)S(1)} %get-tuple-element.18.n_ref, f32[1024,128]{1,0:T(8,128)S(1)} %get-tuple-element.19.lse_ref, bf16[2,256,768]{2,1,0:T(8,128)(2,1)S(1)} %copy_bitcast_fusion.k2_ref.v2_ref, ...), custom_call_target="tpu_custom_call" | custom-call | flops 402653184 | bytes 2097152 | tf_op jit(solution)/shard_map/far/pallas_call | solution.py:172
  100.8 0.8 copy-done.14
  101.6 0.0 collective-permute-start.23
  101.7 1.1 collective-permute-start.9
  102.8 0.8 copy-done.16
  103.6 0.8 collective-permute-start.16
  104.4 5.7 %collective-permute-done.18.refs_6_ = bf16[1024,256]{1,0:T(8,128)(2,1)} collective-permute-done((bf16[1024,256]{1,0:T(8,128)(2,1)S(1)}, bf16[1024,256]{1,0:T(8,128)(2,1)}, u32[]{:S(2)}, u32[]{:S(2)}) %collective-permute-start.18) | collective-permute-done | bytes 524320 | tf_op jit(solution)/shard_map/ppermute | solution.py:290
  110.1 1.2 collective-permute-start.22
  111.3 0.8 copy-done.18
  112.1 0.1 stack.83.place_ref
  112.2 0.1 pad_add_fusion.place_ref
  112.3 9.0 %collective-permute-done.9.refs_0_ = bf16[1024,256]{1,0:T(8,128)(2,1)S(1)} collective-permute-done((bf16[1024,256]{1,0:T(8,128)(2,1)}, bf16[1024,256]{1,0:T(8,128)(2,1)S(1)}, u32[]{:S(2)}, u32[]{:S(2)}) %collective-permute-start.9) | collective-permute-done | bytes 524320 | tf_op jit(solution)/shard_map/ppermute | solution.py:290
  121.2 0.8 collective-permute-start.10
  122.1 1.0 copy-done.13
  123.1 1.0 copy-done.15
  124.1 1.0 copy-done.17
  125.2 1.0 copy-done.19
  126.2 13.7 %project.2.refs_4_ = f32[1024,1024]{1,0:T(8,128)} custom-call(s32[14]{0:T(128)S(1)} %stack.83.place_ref, bf16[1024,256]{1,0:T(8,128)(2,1)S(1)} %copy-done.9, bf16[1024,256]{1,0:T(8,128)(2,1)S(1)} %copy-done.15, bf16[1024,256]{1,0:T(8,128)(2,1)} %collective-permute-done.15.refs_2_, bf16[1024,256]{1,0:T(8,128)(2,1)S(1)} %collective-permute-done.16.refs_3_, ...), custom_call_target="tpu_custom_call" | custom-call | flops 7516192768 | bytes 18874368 | tf_op jit(solution)/shard_map/project/pallas_call | solution.py:215
  140.0 2.2 %copy-done.3 = f32[1024,1024]{1,0:T(8,128)S(1)} copy-done((f32[1024,1024]{1,0:T(8,128)S(1)}, f32[1024,1024]{1,0:T(8,128)}, u32[]{:S(2)}) %copy-start.3) | copy-done | bytes 4194328
  142.2 4.7 %project.3 = bf16[1024,1024]{1,0:T(8,128)(2,1)} custom-call(s32[2]{0:T(128)S(1)} %pad_add_fusion.place_ref, bf16[1024,256]{1,0:T(8,128)(2,1)S(1)} %collective-permute-done.9.refs_0_, bf16[1024,256]{1,0:T(8,128)(2,1)S(1)} %collective-permute-done.10.refs_1_, bf16[4096,1024]{1,0:T(8,128)(2,1)} %refs_3_.1, bf16[4096,1024]{1,0:T(8,128)(2,1)} %refs_3_.1, ...), custom_call_target="tpu_custom_call" | custom-call | flops 1073741824 | bytes 6291456 | tf_op jit(solution)/shard_map/project/pallas_call | solution.py:215
  (80 shorter events, 0.3 us)
Async XLA Ops:
  0.0 13.3 %copy-start.24 = (s32[4]{0:T(128)S(1)}, s32[4]{0:T(128)}, u32[]{:S(2)}) copy-start(s32[4]{0:T(128)} %constant.134.clone) | copy-start | bytes 52
  0.0 13.3 %copy-start.23 = (s32[8]{0:T(128)S(1)}, s32[8]{0:T(128)}, u32[]{:S(2)}) copy-start(s32[8]{0:T(128)} %constant.133.clone) | copy-start | bytes 100
  0.0 1.6 %copy-start.1 = (bf16[1024,1024]{1,0:T(8,128)(2,1)S(1)}, bf16[1024,1024]{1,0:T(8,128)(2,1)}, u32[]{:S(2)}) copy-start(bf16[1024,1024]{1,0:T(8,128)(2,1)} %k_ref.9) | copy-start | bytes 6291460
  1.6 1.6 %copy-start.2 = (bf16[1024,1024]{1,0:T(8,128)(2,1)S(1)}, bf16[1024,1024]{1,0:T(8,128)(2,1)}, u32[]{:S(2)}) copy-start(bf16[1024,1024]{1,0:T(8,128)(2,1)} %v_ref.9) | copy-start | bytes 6291460
  3.2 5.6 %slice-start = ((bf16[1024,1024]{1,0:T(8,128)(2,1)}), bf16[64,1024]{1,0:T(8,128)(2,1)S(1)}, s32[]{:S(2)}) async-start(bf16[1024,1024]{1,0:T(8,128)(2,1)} %k_ref.9), calls=%async_computation | async-start | bytes 262144 | tf_op jit(solution)/shard_map/slice | solution.py:276
  3.2 5.6 %slice-start.1 = ((bf16[1024,1024]{1,0:T(8,128)(2,1)}), bf16[64,1024]{1,0:T(8,128)(2,1)S(1)}, s32[]{:S(2)}) async-start(bf16[1024,1024]{1,0:T(8,128)(2,1)} %v_ref.9), calls=%async_computation.1 | async-start | bytes 262144 | tf_op jit(solution)/shard_map/slice | solution.py:276
  3.2 10.1 %copy-start.22 = (s32[64]{0:T(128)S(1)}, s32[64]{0:T(128)}, u32[]{:S(2)}) copy-start(s32[64]{0:T(128)} %param.10) | copy-start | bytes 772
  5.2 4.5 %copy-start.4 = (bf16[64,1024]{1,0:T(8,128)(2,1)}, bf16[64,1024]{1,0:T(8,128)(2,1)S(1)}, u32[]{:S(2)}) copy-start(bf16[64,1024]{1,0:T(8,128)(2,1)S(1)} %get-tuple-element.16.k1_ref) | copy-start | bytes 393220
  5.2 8.0 %copy-start.6 = (bf16[64,1024]{1,0:T(8,128)(2,1)}, bf16[64,1024]{1,0:T(8,128)(2,1)S(1)}, u32[]{:S(2)}) copy-start(bf16[64,1024]{1,0:T(8,128)(2,1)S(1)} %get-tuple-element.17.v1_ref) | copy-start | bytes 393220
  5.2 42.2 %copy-start = (bf16[1024,1024]{1,0:T(8,128)(2,1)S(1)}, bf16[1024,1024]{1,0:T(8,128)(2,1)}, u32[]{:S(2)}) copy-start(bf16[1024,1024]{1,0:T(8,128)(2,1)} %q_ref.15) | copy-start | bytes 6291460
  5.2 10.2 %collective-permute-start.1 = (bf16[2,4,1024]{2,1,0:T(4,128)(2,1)S(1)}, bf16[2,4,1024]{2,1,0:T(4,128)(2,1)S(1)}, u32[]{:S(2)}, u32[]{:S(2)}) collective-permute-start(bf16[2,4,1024]{2,1,0:T(4,128)(2,1)S(1)} %get-tuple-element.20), channel_id=1, source_target_pairs={{0,32},{32,0},{1,33},{33,1},{2,34},{34,2},{3,35},{35,3},{4,36},{36... | collective-permute-start | bytes 49160 | tf_op jit(solution)/shard_map/ppermute | solution.py:254
  9.6 37.7 %collective-permute-start = (bf16[160,1024]{1,0:T(8,128)(2,1)}, bf16[160,1024]{1,0:T(8,128)(2,1)S(1)}, u32[]{:S(2)}, u32[]{:S(2)}) collective-permute-start(bf16[160,1024]{1,0:T(8,128)(2,1)} %pad_maximum_fusion.1), channel_id=1, source_target_pairs={{0,4},{4,8},{8,12},{12,16},{16,20},{20,24},{24,28},{28,32},{32,36}... | collective-permute-start | bytes 983048 | tf_op jit(solution)/shard_map/ppermute | solution.py:275
  15.4 11.8 %collective-permute-start.3 = (bf16[2,1,8,1024]{3,2,0,1:T(8,128)(2,1)S(1)}, bf16[2,1,8,1024]{3,2,0,1:T(8,128)(2,1)S(1)}, u32[]{:S(2)}, u32[]{:S(2)}) collective-permute-start(bf16[2,1,8,1024]{3,2,0,1:T(8,128)(2,1)S(1)} %maximum_bitcast_fusion), channel_id=1, source_target_pairs={{0,28},{4,0},{8,4},{12,8},{16,12},{20,16},{24,20},{28,24},{1,29},{... | collective-permute-start | bytes 98312 | tf_op jit(solution)/shard_map/ppermute | solution.py:35
  19.5 5.4 %collective-permute-start.2 = (bf16[2,1,8,1024]{3,2,0,1:T(8,128)(2,1)S(1)}, bf16[2,1,8,1024]{3,2,0,1:T(8,128)(2,1)S(1)}, u32[]{:S(2)}, u32[]{:S(2)}) collective-permute-start(bf16[2,1,8,1024]{3,2,0,1:T(8,128)(2,1)S(1)} %maximum_bitcast_fusion), channel_id=1, source_target_pairs={{0,4},{4,8},{8,12},{12,16},{16,20},{20,24},{24,28},{28,0},{1,5},{5... | collective-permute-start | bytes 98312 | tf_op jit(solution)/shard_map/ppermute | solution.py:35
  24.8 12.3 %collective-permute-start.5 = (bf16[2,2,8,1024]{3,2,0,1:T(8,128)(2,1)S(1)}, bf16[2,2,8,1024]{3,2,0,1:T(8,128)(2,1)S(1)}, u32[]{:S(2)}, u32[]{:S(2)}) collective-permute-start(bf16[2,2,8,1024]{3,2,0,1:T(8,128)(2,1)S(1)} %pad_maximum_fusion.4), channel_id=1, source_target_pairs={{0,20},{4,24},{8,28},{12,0},{16,4},{20,8},{24,12},{28,16},{1,21},{... | collective-permute-start | bytes 196616 | tf_op jit(solution)/shard_map/ppermute | solution.py:35
  27.2 9.9 %collective-permute-start.4 = (bf16[2,3,8,1024]{3,2,0,1:T(8,128)(2,1)S(1)}, bf16[2,3,8,1024]{3,2,0,1:T(8,128)(2,1)S(1)}, u32[]{:S(2)}, u32[]{:S(2)}) collective-permute-start(bf16[2,3,8,1024]{3,2,0,1:T(8,128)(2,1)S(1)} %pad_maximum_fusion.3), channel_id=1, source_target_pairs={{0,12},{4,16},{8,20},{12,24},{16,28},{20,0},{24,4},{28,8},{1,13},{... | collective-permute-start | bytes 294920 | tf_op jit(solution)/shard_map/ppermute | solution.py:35
  37.2 0.7 copy-start.20
  37.9 6.0 %collective-permute-start.13 = (bf16[2,8,8,256]{3,2,0,1:T(8,128)(2,1)S(1)}, bf16[2,8,8,256]{3,2,0,1:T(8,128)(2,1)}, u32[]{:S(2)}, u32[]{:S(2)}) collective-permute-start(bf16[2,8,8,256]{3,2,0,1:T(8,128)(2,1)S(1)} %slice.27), channel_id=1, source_target_pairs={{0,128},{64,192},{128,0},{192,64},{1,129},{65,193},{129,1},{193,65... | collective-permute-start | bytes 196616 | tf_op jit(solution)/shard_map/ppermute | solution.py:35
  40.9 3.2 %collective-permute-start.12 = (bf16[2,8,8,256]{3,2,0,1:T(8,128)(2,1)S(1)}, bf16[2,8,8,256]{3,2,0,1:T(8,128)(2,1)}, u32[]{:S(2)}, u32[]{:S(2)}) collective-permute-start(bf16[2,8,8,256]{3,2,0,1:T(8,128)(2,1)S(1)} %slice.27), channel_id=1, source_target_pairs={{0,192},{64,0},{128,64},{192,128},{1,193},{65,1},{129,65},{193,129... | collective-permute-start | bytes 196616 | tf_op jit(solution)/shard_map/ppermute | solution.py:35
  41.7 4.8 %collective-permute-start.11 = (bf16[2,8,8,256]{3,2,0,1:T(8,128)(2,1)S(1)}, bf16[2,8,8,256]{3,2,0,1:T(8,128)(2,1)}, u32[]{:S(2)}, u32[]{:S(2)}) collective-permute-start(bf16[2,8,8,256]{3,2,0,1:T(8,128)(2,1)S(1)} %slice.27), channel_id=1, source_target_pairs={{0,64},{64,128},{128,192},{192,0},{1,65},{65,129},{129,193},{193,1... | collective-permute-start | bytes 196616 | tf_op jit(solution)/shard_map/ppermute | solution.py:35
  47.4 0.9 copy-start.5
  48.3 0.9 copy-start.7
  57.2 2.8 %copy-start.21 = (bf16[2,8,8,1024]{3,2,0,1:T(8,128)(2,1)S(1)}, bf16[2,8,8,1024]{3,2,0,1:T(8,128)(2,1)}, u32[]{:S(2)}) copy-start(bf16[2,8,8,1024]{3,2,0,1:T(8,128)(2,1)} %copy-done.20) | copy-start | bytes 786436
  59.3 15.4 %copy-start.8 = (bf16[1024,256]{1,0:T(8,128)(2,1)}, bf16[1024,256]{1,0:T(8,128)(2,1)S(1)}, u32[]{:S(2)}) copy-start(bf16[1024,256]{1,0:T(8,128)(2,1)S(1)} %far.5.refs_0_) | copy-start | bytes 1572868
  59.3 29.9 %collective-permute-start.15 = (bf16[1024,256]{1,0:T(8,128)(2,1)S(1)}, bf16[1024,256]{1,0:T(8,128)(2,1)}, u32[]{:S(2)}, u32[]{:S(2)}) collective-permute-start(bf16[1024,256]{1,0:T(8,128)(2,1)S(1)} %far.5.refs_0_), channel_id=1, source_target_pairs={{0,2},{2,0},{1,3},{3,1},{4,6},{6,4},{5,7},{7,5},{8,10},{10,8},{9,1... | collective-permute-start | bytes 1572872 | tf_op jit(solution)/shard_map/ppermute | solution.py:290
  60.0 22.9 %collective-permute-start.8 = (bf16[2,8,8,768]{3,2,0,1:T(8,128)(2,1)S(1)}, bf16[2,8,8,768]{3,2,0,1:T(8,128)(2,1)S(1)}, u32[]{:S(2)}, u32[]{:S(2)}) collective-permute-start(bf16[2,8,8,768]{3,2,0,1:T(8,128)(2,1)S(1)} %slice.26), channel_id=1, source_target_pairs={{0,128},{64,192},{128,0},{192,64},{1,129},{65,193},{129,1},{193,65... | collective-permute-start | bytes 589832 | tf_op jit(solution)/shard_map/ppermute | solution.py:35
  60.1 22.8 %collective-permute-start.7 = (bf16[2,8,8,768]{3,2,0,1:T(8,128)(2,1)S(1)}, bf16[2,8,8,768]{3,2,0,1:T(8,128)(2,1)S(1)}, u32[]{:S(2)}, u32[]{:S(2)}) collective-permute-start(bf16[2,8,8,768]{3,2,0,1:T(8,128)(2,1)S(1)} %slice.26), channel_id=1, source_target_pairs={{0,192},{64,0},{128,64},{192,128},{1,193},{65,1},{129,65},{193,129... | collective-permute-start | bytes 589832 | tf_op jit(solution)/shard_map/ppermute | solution.py:35
  61.6 21.2 %collective-permute-start.6 = (bf16[2,8,8,768]{3,2,0,1:T(8,128)(2,1)S(1)}, bf16[2,8,8,768]{3,2,0,1:T(8,128)(2,1)S(1)}, u32[]{:S(2)}, u32[]{:S(2)}) collective-permute-start(bf16[2,8,8,768]{3,2,0,1:T(8,128)(2,1)S(1)} %slice.26), channel_id=1, source_target_pairs={{0,64},{64,128},{128,192},{192,0},{1,65},{65,129},{129,193},{193,1... | collective-permute-start | bytes 589832 | tf_op jit(solution)/shard_map/ppermute | solution.py:35
  61.6 39.2 %collective-permute-start.14 = (bf16[1024,256]{1,0:T(8,128)(2,1)S(1)}, bf16[1024,256]{1,0:T(8,128)(2,1)S(1)}, u32[]{:S(2)}, u32[]{:S(2)}) collective-permute-start(bf16[1024,256]{1,0:T(8,128)(2,1)S(1)} %far.5.refs_0_), channel_id=1, source_target_pairs={{0,1},{1,0},{2,3},{3,2},{4,5},{5,4},{6,7},{7,6},{8,9},{9,8},{10,11... | collective-permute-start | bytes 1572872 | tf_op jit(solution)/shard_map/ppermute | solution.py:291
  85.1 3.7 %copy-start.10 = (bf16[1024,256]{1,0:T(8,128)(2,1)}, bf16[1024,256]{1,0:T(8,128)(2,1)S(1)}, u32[]{:S(2)}) copy-start(bf16[1024,256]{1,0:T(8,128)(2,1)S(1)} %far.7.refs_8_) | copy-start | bytes 1572868
  85.1 16.5 %collective-permute-start.21 = (bf16[1024,256]{1,0:T(8,128)(2,1)S(1)}, bf16[1024,256]{1,0:T(8,128)(2,1)}, u32[]{:S(2)}, u32[]{:S(2)}) collective-permute-start(bf16[1024,256]{1,0:T(8,128)(2,1)S(1)} %far.7.refs_8_), channel_id=1, source_target_pairs={{0,2},{2,0},{1,3},{3,1},{4,6},{6,4},{5,7},{7,5},{8,10},{10,8},{9,1... | collective-permute-start | bytes 1572872 | tf_op jit(solution)/shard_map/ppermute | solution.py:290
  86.3 16.5 %collective-permute-start.20 = (bf16[1024,256]{1,0:T(8,128)(2,1)S(1)}, bf16[1024,256]{1,0:T(8,128)(2,1)S(1)}, u32[]{:S(2)}, u32[]{:S(2)}) collective-permute-start(bf16[1024,256]{1,0:T(8,128)(2,1)S(1)} %far.7.refs_8_), channel_id=1, source_target_pairs={{0,1},{1,0},{2,3},{3,2},{4,5},{5,4},{6,7},{7,6},{8,9},{9,8},{10,11... | collective-permute-start | bytes 1572872 | tf_op jit(solution)/shard_map/ppermute | solution.py:291
  88.8 8.9 %copy-start.12 = (bf16[1024,256]{1,0:T(8,128)(2,1)}, bf16[1024,256]{1,0:T(8,128)(2,1)S(1)}, u32[]{:S(2)}) copy-start(bf16[1024,256]{1,0:T(8,128)(2,1)S(1)} %far.6.refs_4_) | copy-start | bytes 1572868
  88.9 21.2 %collective-permute-start.18 = (bf16[1024,256]{1,0:T(8,128)(2,1)S(1)}, bf16[1024,256]{1,0:T(8,128)(2,1)}, u32[]{:S(2)}, u32[]{:S(2)}) collective-permute-start(bf16[1024,256]{1,0:T(8,128)(2,1)S(1)} %far.6.refs_4_), channel_id=1, source_target_pairs={{0,2},{2,0},{1,3},{3,1},{4,6},{6,4},{5,7},{7,5},{8,10},{10,8},{9,1... | collective-permute-start | bytes 1572872 | tf_op jit(solution)/shard_map/ppermute | solution.py:290
  89.3 22.0 %collective-permute-start.17 = (bf16[1024,256]{1,0:T(8,128)(2,1)S(1)}, bf16[1024,256]{1,0:T(8,128)(2,1)S(1)}, u32[]{:S(2)}, u32[]{:S(2)}) collective-permute-start(bf16[1024,256]{1,0:T(8,128)(2,1)S(1)} %far.6.refs_4_), channel_id=1, source_target_pairs={{0,1},{1,0},{2,3},{3,2},{4,5},{5,4},{6,7},{7,6},{8,9},{9,8},{10,11... | collective-permute-start | bytes 1572872 | tf_op jit(solution)/shard_map/ppermute | solution.py:291
  97.8 24.2 %copy-start.9 = (bf16[1024,256]{1,0:T(8,128)(2,1)S(1)}, bf16[1024,256]{1,0:T(8,128)(2,1)}, u32[]{:S(2)}) copy-start(bf16[1024,256]{1,0:T(8,128)(2,1)} %copy-done.8) | copy-start | bytes 1572868
  97.8 24.2 %copy-start.11 = (bf16[1024,256]{1,0:T(8,128)(2,1)S(1)}, bf16[1024,256]{1,0:T(8,128)(2,1)}, u32[]{:S(2)}) copy-start(bf16[1024,256]{1,0:T(8,128)(2,1)} %copy-done.10) | copy-start | bytes 1572868
  100.8 0.8 copy-start.14
  101.6 20.4 %collective-permute-start.23 = (bf16[1024,256]{1,0:T(8,128)(2,1)}, bf16[1024,256]{1,0:T(8,128)(2,1)}, u32[]{:S(2)}, u32[]{:S(2)}) collective-permute-start(bf16[1024,256]{1,0:T(8,128)(2,1)} %far.4.refs_12_), channel_id=1, source_target_pairs={{0,1},{1,0},{2,3},{3,2},{4,5},{5,4},{6,7},{7,6},{8,9},{9,8},{10,11... | collective-permute-start | bytes 1572872 | tf_op jit(solution)/shard_map/ppermute | solution.py:291
  101.7 19.6 %collective-permute-start.9 = (bf16[1024,256]{1,0:T(8,128)(2,1)}, bf16[1024,256]{1,0:T(8,128)(2,1)S(1)}, u32[]{:S(2)}, u32[]{:S(2)}) collective-permute-start(bf16[1024,256]{1,0:T(8,128)(2,1)} %far.4.refs_12_), channel_id=1, source_target_pairs={{0,2},{2,0},{1,3},{3,1},{4,6},{6,4},{5,7},{7,5},{8,10},{10,8},{9,1... | collective-permute-start | bytes 1572872 | tf_op jit(solution)/shard_map/ppermute | solution.py:290
  102.8 0.8 copy-start.16
  103.6 18.4 %collective-permute-start.16 = (bf16[1024,256]{1,0:T(8,128)(2,1)}, bf16[1024,256]{1,0:T(8,128)(2,1)S(1)}, u32[]{:S(2)}, u32[]{:S(2)}) collective-permute-start(bf16[1024,256]{1,0:T(8,128)(2,1)} %collective-permute-done.15.refs_2_), channel_id=1, source_target_pairs={{0,1},{1,0},{2,3},{3,2},{4,5},{5,4},{6,7},{7,6},{8,9},{9,8},{10,11... | collective-permute-start | bytes 1572872 | tf_op jit(solution)/shard_map/ppermute | solution.py:292
  110.1 11.9 %collective-permute-start.22 = (bf16[1024,256]{1,0:T(8,128)(2,1)}, bf16[1024,256]{1,0:T(8,128)(2,1)}, u32[]{:S(2)}, u32[]{:S(2)}) collective-permute-start(bf16[1024,256]{1,0:T(8,128)(2,1)} %collective-permute-done.21.refs_10_), channel_id=1, source_target_pairs={{0,1},{1,0},{2,3},{3,2},{4,5},{5,4},{6,7},{7,6},{8,9},{9,8},{10,11... | collective-permute-start | bytes 1572872 | tf_op jit(solution)/shard_map/ppermute | solution.py:292
  111.3 0.8 copy-start.18
  112.1 9.9 %collective-permute-start.19 = (bf16[1024,256]{1,0:T(8,128)(2,1)}, bf16[1024,256]{1,0:T(8,128)(2,1)S(1)}, u32[]{:S(2)}, u32[]{:S(2)}) collective-permute-start(bf16[1024,256]{1,0:T(8,128)(2,1)} %collective-permute-done.18.refs_6_), channel_id=1, source_target_pairs={{0,1},{1,0},{2,3},{3,2},{4,5},{5,4},{6,7},{7,6},{8,9},{9,8},{10,11... | collective-permute-start | bytes 1572872 | tf_op jit(solution)/shard_map/ppermute | solution.py:292
  121.2 18.7 %collective-permute-start.10 = (bf16[1024,256]{1,0:T(8,128)(2,1)S(1)}, bf16[1024,256]{1,0:T(8,128)(2,1)S(1)}, u32[]{:S(2)}, u32[]{:S(2)}) collective-permute-start(bf16[1024,256]{1,0:T(8,128)(2,1)S(1)} %collective-permute-done.9.refs_0_), channel_id=1, source_target_pairs={{0,1},{1,0},{2,3},{3,2},{4,5},{5,4},{6,7},{7,6},{8,9},{9,8},{10,11... | collective-permute-start | bytes 1572872 | tf_op jit(solution)/shard_map/ppermute | solution.py:292
  122.1 1.0 copy-start.13
  123.1 1.0 copy-start.15
  124.1 1.0 copy-start.17
  125.2 1.0 copy-start.19
  140.0 2.2 %copy-start.3 = (f32[1024,1024]{1,0:T(8,128)S(1)}, f32[1024,1024]{1,0:T(8,128)}, u32[]{:S(2)}) copy-start(f32[1024,1024]{1,0:T(8,128)} %project.2.refs_4_) | copy-start | bytes 12582916

commit v2 on v1

v2 whole, which is shorter than its diff:
```python
import functools

import jax
import jax.numpy as jnp
from jax import lax
from jax.experimental import pallas as pl
from jax.experimental.pallas import tpu as pltpu
from jax.sharding import Mesh
from jax.sharding import PartitionSpec as P

HD = 128
G = 16
WMAX = 4
HALO = WMAX * G
LOG2E = 1.4426950408889634
SCALE = HD ** (-0.5) * LOG2E
CTX = ("y", "xh", "z")
TILE = 128
NEAR = TILE + HALO
SPAN = 256
CHUNK = 2
MIB = 1024 * 1024
DEPTH = 3


def params(mib):
    return pltpu.CompilerParams(vmem_limit_bytes=mib * MIB)


def cost(micros):
    return pl.CostEstimate(flops=micros * 10**9, bytes_accessed=1000, transcendentals=0)


def shift(x, axis, by):
    n = lax.axis_size(axis)
    return lax.ppermute(x, axis, [(i, (i + by) % n) for i in range(n)])


def staged(jobs, stages):
    kept = {}
    for i in range(len(jobs) + DEPTH * (len(stages) - 1)):
        for n, stage in enumerate(stages):
            j = i - n * DEPTH
            if 0 <= j < len(jobs):
                kept[j] = stage(jobs[j], kept.get(j))


def pool_kernel(*refs):
    k1_ref, v1_ref, far_ref, edge_ref = refs[-4:]
    blocks = (len(refs) - 4) // 2
    rows, width = refs[0].shape
    r = lax.broadcasted_iota(jnp.int32, (rows // G, rows), 0)
    t = lax.broadcasted_iota(jnp.int32, (rows // G, rows), 1)
    pick = jnp.where(t // G == r, 1.0, 0.0).astype(jnp.bfloat16)
    for slot, one in ((0, k1_ref), (1, v1_ref)):
        wholes = []
        for b in range(blocks):
            src = refs[slot * blocks + b]
            sums = jnp.dot(pick, src[...], preferred_element_type=jnp.float32)
            one[b * G : (b + 1) * G, :] = (sums * (1.0 / G)).astype(jnp.bfloat16)
            wholes.append(jnp.sum(sums, axis=0, keepdims=True) * (1.0 / (G * G)))
        far_ref[slot] = jnp.concatenate(wholes, axis=0).astype(jnp.bfloat16)
        edge_ref[slot * HALO : (slot + 1) * HALO, :] = src[rows - HALO :, :]
        edge_ref[2 * HALO + slot * G : 2 * HALO + (slot + 1) * G, :] = one[blocks * G - G :, :]


def pool(key, value):
    rows, width = key.shape
    block = G * G
    blocks = rows // block
    spec = lambda n, b: pl.BlockSpec((n, width), lambda i: (b, 0))
    return pl.pallas_call(
        pool_kernel,
        grid=(1,),
        in_specs=[spec(block, b) for b in range(blocks)] * 2,
        out_specs=[
            spec(rows // G, 0), spec(rows // G, 0),
            pl.BlockSpec((2, blocks, width), lambda i: (0, 0, 0)), spec(2 * HALO + 2 * G, 0),
        ],
        out_shape=[
            jax.ShapeDtypeStruct((rows // G, width), jnp.bfloat16),
            jax.ShapeDtypeStruct((rows // G, width), jnp.bfloat16),
            jax.ShapeDtypeStruct((2, blocks, width), jnp.bfloat16),
            jax.ShapeDtypeStruct((2 * HALO + 2 * G, width), jnp.bfloat16),
        ],
        compiler_params=params(60),
        cost_estimate=cost(0),
        name="pool",
    )(*[key] * blocks, *[value] * blocks)


def near_kernel(
    info_ref, q_ref, k_ref, v_ref, k1_ref, v1_ref, pk_ref, pv_ref, pk1_ref, pv1_ref, *refs
):
    out_ref, lse_ref, pack_ref, kx, vx, k1x, v1x, bias_ref = refs[-8:]
    rows, width = q_ref.shape
    heads = width // HD
    ones = jnp.ones((SPAN, HD), jnp.bfloat16)
    pad = jnp.zeros((SPAN - NEAR - 2 * G, HD), jnp.bfloat16)
    lane = lax.broadcasted_iota(jnp.int32, (TILE, HD), 1)
    step = pl.program_id(0)
    for ext, prev, now in ((kx, pk_ref, k_ref), (vx, pv_ref, v_ref), (k1x, pk1_ref, k1_ref), (v1x, pv1_ref, v1_ref)):
        before, count = prev.shape[0], now.shape[0]

        @pl.when(step == 0)
        def _():
            ext[:before, :] = prev[...]

        @pl.when(step > 0)
        def _():
            ext[:before, :] = ext[count : count + before, :]

        ext[before : before + count, :] = now[...]
    block = info_ref[0] + step
    row_cell = lax.broadcasted_iota(jnp.int32, (TILE, SPAN), 0) // G
    row = lax.broadcasted_iota(jnp.int32, (TILE, SPAN), 0)
    at_lane = lax.broadcasted_iota(jnp.int32, (TILE, SPAN), 1)
    for t in range(rows // TILE):
        window = jnp.zeros((TILE, SPAN), jnp.int32)
        for c in range(TILE // G):
            here = info_ref[2 + block * (rows // G) + t * (TILE // G) + c]
            window = jnp.where(row_cell == c, here, window)
        start = info_ref[1] + block * rows + t * TILE
        near_ok = (
            (at_lane >= HALO - start) & (at_lane - HALO <= row)
            & (at_lane // G >= row_cell + WMAX - window)
        )
        mid = at_lane - NEAR - G
        mid_ok = (mid >= -((start // (G * G)) * G)) & (
            mid <= t * (TILE // G) + row_cell - window - 1
        )
        lanes = jnp.where(
            at_lane < NEAR,
            near_ok.astype(jnp.int32),
            jnp.where(at_lane < NEAR + 2 * G, mid_ok.astype(jnp.int32), 0),
        )
        bias_ref[t * TILE : (t + 1) * TILE, :] = jnp.where(lanes == 1, 0.0, -jnp.inf)
    for p in range(heads // CHUNK):
        pack_ref[p] = q_ref[:, p * CHUNK * HD : (p + 1) * CHUNK * HD]
    lses = {}

    def where(job):
        t, h = job
        return slice(t * TILE, (t + 1) * TILE), slice(h * HD, (h + 1) * HD)

    def rows_of(src, src1, job):
        t, _ = job
        _, cols = where(job)
        return jnp.concatenate([src[t * TILE : t * TILE + NEAR, cols], src1[:, cols], pad], axis=0)

    def score(job, _):
        at, cols = where(job)
        return lax.dot_general(
            q_ref[at, cols], rows_of(kx, k1x, job), (((1,), (1,)), ((), ())),
            preferred_element_type=jnp.float32,
        )

    def weigh(job, s):
        at, _ = where(job)
        s = s * SCALE + bias_ref[at, :]
        top = jnp.max(s, axis=1, keepdims=True)
        return top, jnp.exp2(s - top).astype(jnp.bfloat16)

    def finish(job, kept):
        at, _ = where(job)
        t, h = job
        top, w = kept
        values = jnp.concatenate([rows_of(vx, v1x, job), ones], axis=1)
        both = jnp.dot(w, values, preferred_element_type=jnp.float32)
        total = both[:, HD:]
        part = h % CHUNK
        out_ref[h // CHUNK, at, part * HD : (part + 1) * HD] = (both[:, :HD] / total).astype(
            jnp.bfloat16
        )
        lse = top + jnp.log2(total)
        lses[t] = jnp.where(lane == h, lse, lses[t]) if h else lse
        if h == heads - 1:
            lse_ref[at, :] = lses[t]

    staged([(t, h) for t in range(rows // TILE) for h in range(heads)], [score, weigh, finish])


def near(query, key, value, key1, value1, prev, info, first, blocks, before):
    rows, width = query.shape
    block = G * G
    pairs = width // HD // CHUNK
    spec = lambda n: pl.BlockSpec((n, width), lambda i, s: (s[0] + i, 0))
    args = [query, key, value, key1, value1] + [p for p, _, _ in prev]
    specs = [spec(block), spec(block), spec(block), spec(G), spec(G)]
    specs += [pl.BlockSpec((n, width), lambda i, s, at=at: (at, 0)) for _, n, at in prev]
    shapes = [
        jax.ShapeDtypeStruct((pairs, rows, CHUNK * HD), jnp.bfloat16),
        jax.ShapeDtypeStruct((rows, HD), jnp.float32),
        jax.ShapeDtypeStruct((pairs, rows, CHUNK * HD), jnp.bfloat16),
    ]
    aliases = {}
    if before is not None:
        aliases = {len(args) + 1 + i: i for i in range(3)}
        args += list(before)
        specs += [pl.BlockSpec(memory_space=pl.ANY)] * 3
    packed = pl.BlockSpec((pairs, block, CHUNK * HD), lambda i, s: (0, s[0] + i, 0))
    return pl.pallas_call(
        near_kernel,
        grid_spec=pltpu.PrefetchScalarGridSpec(
            num_scalar_prefetch=1,
            grid=(blocks,),
            in_specs=specs,
            out_specs=[packed, pl.BlockSpec((block, HD), lambda i, s: (s[0] + i, 0)), packed],
            scratch_shapes=[
                pltpu.VMEM((HALO + block, width), jnp.bfloat16),
                pltpu.VMEM((HALO + block, width), jnp.bfloat16),
                pltpu.VMEM((2 * G, width), jnp.bfloat16),
                pltpu.VMEM((2 * G, width), jnp.bfloat16),
                pltpu.VMEM((block, SPAN), jnp.float32),
            ],
        ),
        out_shape=shapes,
        input_output_aliases=aliases,
        compiler_params=params(60),
        cost_estimate=cost(0),
        name="near",
    )(jnp.concatenate([jnp.full((1,), first, jnp.int32), info]), *args)


def far_kernel(pair, lim_ref, q_ref, n_ref, lse_ref, k2_ref, v2_ref, cell_ref, out_ref):
    rows = out_ref.shape[0]
    heads = out_ref.shape[1] // HD
    ones = jnp.ones((k2_ref.shape[1], HD), jnp.bfloat16)
    cell = cell_ref[...]
    limit = lim_ref[0] + pl.program_id(0) * (rows // (G * G))

    def where(job):
        t, h = job
        return slice(t * TILE, (t + 1) * TILE), slice(h * HD, (h + 1) * HD)

    def score(job, _):
        at, cols = where(job)
        return lax.dot_general(
            q_ref[0, at, cols], k2_ref[0, :, cols], (((1,), (1,)), ((), ())),
            preferred_element_type=jnp.float32,
        )

    def weigh(job, s):
        t, h = job
        at, _ = where(job)
        last = limit + t * TILE // (G * G)
        s = s * SCALE + jnp.where(cell <= last, 0.0, -jnp.inf)
        lse = lse_ref[at, pair * CHUNK + h : pair * CHUNK + h + 1]
        top = jnp.maximum(jnp.max(s, axis=1, keepdims=True), lse)
        return jnp.exp2(lse - top), jnp.exp2(s - top).astype(jnp.bfloat16)

    def finish(job, kept):
        at, cols = where(job)
        part, w = kept
        values = jnp.concatenate([v2_ref[0, :, cols], ones], axis=1)
        both = jnp.dot(w, values, preferred_element_type=jnp.float32)
        summed = both[:, :HD] + n_ref[0, at, cols].astype(jnp.float32) * part
        done = (summed / (both[:, HD:] + part)).astype(jnp.bfloat16)
        out_ref[at, cols] = done

    staged([(t, h) for h in range(heads) for t in range(rows // TILE)], [score, weigh, finish])


def far(lim, query, partial, lse, kv2, col, cell, pair):
    rows, cells = query.shape[1], kv2.shape[1]
    width = CHUNK * HD
    tile = 512
    args = [lim, query, partial, lse, kv2, kv2, cell]
    return pl.pallas_call(
        functools.partial(far_kernel, pair),
        grid_spec=pltpu.PrefetchScalarGridSpec(
            num_scalar_prefetch=1,
            grid=(rows // tile,),
            in_specs=[
                pl.BlockSpec((1, tile, width), lambda i, s: (pair, i, 0)),
                pl.BlockSpec((1, tile, width), lambda i, s: (pair, i, 0)),
                pl.BlockSpec((tile, HD), lambda i, s: (i, 0)),
                pl.BlockSpec((1, cells, width), lambda i, s: (0, 0, col)),
                pl.BlockSpec((1, cells, width), lambda i, s: (1, 0, col)),
                pl.BlockSpec((1, cells), lambda i, s: (0, 0)),
            ],
            out_specs=pl.BlockSpec((tile, width), lambda i, s: (i, 0)),
        ),
        out_shape=jax.ShapeDtypeStruct((rows, width), jnp.bfloat16),
        compiler_params=params(60),
        cost_estimate=cost(0),
        name="far",
    )(*args)


def project_kernel(n, has_acc, place_ref, *refs):
    held = [ref[...] for ref in refs[:n]]
    weights = jnp.concatenate([r[...] for r in refs[n : 2 * n]], axis=0)
    total = jnp.dot(jnp.concatenate(held, axis=1), weights, preferred_element_type=jnp.float32)
    if has_acc:
        total = total + refs[2 * n][...]
    refs[-1][...] = total.astype(refs[-1].dtype)


def project(pieces, places, weight, acc, dtype):
    n = len(pieces)
    rows, width = pieces[0].shape
    cols = weight.shape[1]
    tile = 256
    out_spec = pl.BlockSpec((tile, cols), lambda i, s: (i, 0))
    specs = [pl.BlockSpec((tile, width), lambda i, s: (i, 0)) for _ in pieces]
    specs += [pl.BlockSpec((width, cols), lambda i, s, j=j: (s[j], 0)) for j in range(n)]
    args = list(pieces) + [weight] * n
    if acc is not None:
        specs.append(out_spec)
        args.append(acc)
    return pl.pallas_call(
        functools.partial(project_kernel, n, acc is not None),
        grid_spec=pltpu.PrefetchScalarGridSpec(
            num_scalar_prefetch=1,
            grid=(rows // tile,),
            in_specs=specs,
            out_specs=out_spec,
        ),
        out_shape=jax.ShapeDtypeStruct((rows, cols), dtype),
        compiler_params=params(60),
        cost_estimate=cost(0),
        name="project",
    )(jnp.stack(places).astype(jnp.int32), *args)


def local(query, key, value, windows, out_weight):
    rows, width = query.shape
    heads = width // HD
    ny, nz = lax.axis_size("y"), lax.axis_size("z")
    iy, ix, iz = (lax.axis_index(a) for a in CTX)
    ctx = lax.axis_index(CTX)
    coarse = rows // (G * G)

    key1, value1, mine, edge = pool(key, value)

    block = G * G
    upper = rows // block // 2
    ahead = [
        (key, HALO, upper * block // HALO - 1), (value, HALO, upper * block // HALO - 1),
        (key1, G, upper - 1), (value1, G, upper - 1),
    ]
    info = jnp.concatenate([(ctx * rows).reshape(1).astype(jnp.int32), windows])

    other = lax.ppermute(mine, "xh", [(0, 1), (1, 0)])
    part = near(query, key, value, key1, value1, ahead, info, upper, rows // block - upper, None)
    mine, part = lax.optimization_barrier((mine, part))
    x = jnp.concatenate([mine, other], axis=1)[:, None]
    halo = lax.ppermute(edge, CTX, [(i, i + 1) for i in range(lax.axis_size(CTX) - 1)])
    x, halo = lax.optimization_barrier((x, halo))
    a, b = shift(x, "z", 3), shift(x, "z", -3)
    behind = [(halo, HALO, 0), (halo, HALO, 1), (halo, G, 2 * HALO // G), (halo, G, 2 * HALO // G + 1)]
    part = near(query, key, value, key1, value1, behind, info, 0, upper, part)
    x, part = lax.optimization_barrier((x, part))
    x = jnp.concatenate([x, a, b], axis=1)
    c, d = shift(x, "z", 1), shift(x[:, :2], "z", -1)
    x = jnp.concatenate([x, c, d], axis=1)
    zs = (iz + jnp.array([0, -3, 3, -1, -4, 2, 1, -2], jnp.int32)) % nz
    ys = (iy + jnp.array([0, -1, 1, -2], jnp.int32)) % ny
    xs = jnp.stack([ix, 1 - ix])
    cell = (
        ((ys[:, None, None] * 2 + xs[None, None, :]) * nz + zs[None, :, None])[..., None] * coarse
        + jnp.arange(coarse, dtype=jnp.int32)
    ).reshape(1, -1)

    def over_y(part):
        parts = [part] + [shift(part, "y", s) for s in (1, -1, 2)]
        return jnp.concatenate(parts, axis=1).reshape(2, -1, part.shape[-1])

    lim = (ctx * coarse - 2).reshape(1).astype(jnp.int32)
    xl, core = lax.axis_index("xl"), lax.axis_index("core")
    swap = [(0, 1), (1, 0)]
    pairs = heads // CHUNK
    soon = 2
    step = soon * CHUNK * HD
    kv_first = over_y(x[..., :step])
    kv_first, x = lax.optimization_barrier((kv_first, x[..., step:]))
    kv_rest = over_y(x)

    here, there = xl * 2, (1 - xl) * 2
    last = pairs - 1
    own, across, beside, diagonal = [], [], [], []

    def place(kind, i):
        base = here if kind < 2 else there
        return (base + (core if kind % 2 == 0 else 1 - core)) * pairs + i

    def add(which, acc, dtype=jnp.float32):
        sets = (own, beside, across, diagonal)
        pieces, places = [], []
        for kind, i in which:
            pieces.append(sets[kind][i])
            places.append(place(kind, i))
        return project(pieces, places, out_weight, acc, dtype)

    hop = lambda axis, xs: [lax.ppermute(o, axis, swap) for o in xs]

    def attend(n, kv2, col):
        own.append(far(lim, part[2], part[0], part[1], kv2, col, cell, n))
        across.append(lax.ppermute(own[n], "xl", swap))

    attend(0, kv_first, 0)
    kv_first, own[0] = lax.optimization_barrier((kv_first, own[0]))
    attend(1, kv_first, 1)
    kv_rest, *both = lax.optimization_barrier((kv_rest, *own, across[0]))
    beside += hop("core", both[:2])
    diagonal += hop("core", both[2:])
    attend(2, kv_rest, 0)
    kv_rest, across[1], beside[0], beside[1], diagonal[0] = lax.optimization_barrier(
        (kv_rest, across[1], beside[0], beside[1], diagonal[0])
    )
    diagonal += hop("core", across[1:2])
    attend(3, kv_rest, 1)
    beside += hop("core", own[2:])
    acc = add([(0, 0), (0, 1), (1, 0), (1, 1), (2, 0), (3, 0)], None)
    acc = add([(2, 1), (3, 1), (0, 2), (1, 2), (0, 3), (1, 3)], acc)
    across[2], across[3], acc = lax.optimization_barrier((across[2], across[3], acc))
    diagonal += hop("core", across[2:])
    return add([(2, 2), (3, 2), (2, 3), (3, 3)], acc, jnp.bfloat16)


def solution(mesh):
    split = Mesh(mesh.devices.reshape(4, 2, 8, 2, 2), CTX + ("xl", "core"))
    rows, cols = CTX, ("xl", "core")
    in_specs = (P(rows, cols), P(rows, cols), P(rows, cols), P(rows), P(None, cols))
    return jax.shard_map(
        local, mesh=split, in_specs=in_specs, out_specs=P(rows, cols), check_vma=False
    )
```

time: 148 us -> 121 us (0.82)
  waiting for transfers between devices: 31.4 us -> 15.2 us
  local copies, waits for them, and re-layouts: 15.7 us -> 4.47 us
  starting transfers between devices: 32.8 us -> 39.6 us
  Pallas kernels: 62 us -> 57.5 us
    unnamed x53 -> x38, local copies, waits for them, and re-layouts: 14.5 us -> 2.48 us
    pallas_call x9 -> x7, Pallas kernels: 43.5 us -> 32 us  [the longest x4 15.7 us: far(): pl.pallas_call(functools.partial(far_kernel, pair), grid_spec=pltpu.Prefe...]
    ppermute x13, waiting for transfers between devices: 14.7 us -> 5.31 us  [the longest x4 3.65 us: attend(): across.append(lax.ppermute(own[n], 'xl', swap))]
    pallas_call x2 -> x3, Pallas kernels: 18.4 us -> 25.5 us  [project(): pl.pallas_call(functools.partial(project_kernel, n, acc is not None), gri...]
    ppermute x10, waiting for transfers between devices: 16.7 us -> 9.88 us  [shift(): return lax.ppermute(x, axis, [(i, (i + by) % n) for i in range(n)])]
    ppermute x13, starting transfers between devices: 15.6 us -> 20.4 us  [the longest x8 13.9 us: local(): hop = lambda axis, xs: [lax.ppermute(o, axis, swap) for o in xs]]
    ppermute x10, starting transfers between devices: 13.5 us -> 15.6 us  [shift(): return lax.ppermute(x, axis, [(i, (i + by) % n) for i in range(n)])]
    select_n x2 -> x1, other arithmetic: 1.71 us -> 0.01 us  [local(): zs = (iz + jnp.array([0, -3, 3, -1, -4, 2, 1, -2], jnp.int32)) % nz]
  transfers between devices with their start and end apart: 24 -> 24, of which waited for: 6 -> 9; matrix products, arithmetic and copies ran while one was open for 4% -> 4% of each run, Pallas kernels for 31% -> 35%
where the time goes in v2:
time: 121 us; the launch traced here: 120 us
  Pallas kernels  57.5 us (48%)
  starting transfers between devices  39.6 us (33%)
  waiting for transfers between devices  15.2 us (13%)
  local copies, waits for them, and re-layouts  4.47 us (4%)
  other arithmetic  3.34 us (3%)
    pallas_call x3, Pallas kernels, project(): pl.pallas_call(functools.partial(project_kernel, n, acc is not None), gri...  25.5 us
    pallas_call x4, Pallas kernels, far(): pl.pallas_call(functools.partial(far_kernel, pair), grid_spec=pltpu.Prefe...  15.7 us
    ppermute x10, starting transfers between devices, shift(): return lax.ppermute(x, axis, [(i, (i + by) % n) for i in range(n)])  15.6 us
    ppermute x8, starting transfers between devices, local(): hop = lambda axis, xs: [lax.ppermute(o, axis, swap) for o in xs]  13.9 us
    pallas_call x2, Pallas kernels, near(): pl.pallas_call(near_kernel, grid_spec=pltpu.PrefetchScalarGridSpec(num_sc...  12.7 us
    ppermute x10, waiting for transfers between devices, shift(): return lax.ppermute(x, axis, [(i, (i + by) % n) for i in range(n)])  9.88 us
    pallas_call x1, Pallas kernels, pool(): pl.pallas_call(pool_kernel, grid=(1,), in_specs=[spec(block, b) for b in...  3.66 us
    ppermute x4, waiting for transfers between devices, attend(): across.append(lax.ppermute(own[n], 'xl', swap))  3.65 us
  transfers between devices with their start and end apart: 24, of which 9 were waited for; matrix products, arithmetic and copies ran while one was open for 4% of the time, Pallas kernels for 35%

profile of v2, /device:TPU:1, one launch (start us, length us, event | category | flops | bytes accessed | tf_op | source)
XLA Modules:
  0.0 120.3 jit_solution(15935354723660786026)
XLA Ops:
  0.0 3.7 %pool.1 = (bf16[64,1024]{1,0:T(8,128)(2,1)}, bf16[64,1024]{1,0:T(8,128)(2,1)}, bf16[2,4,1024]{2,1,0:T(4,128)(2,1)}, bf16[160,1024]{1,0:T(8,128)(2,1)}) custom-call(bf16[1024,1024]{1,0:T(8,128)(2,1)} %k_ref.3, bf16[1024,1024]{1,0:T(8,128)(2,1)} %k_ref.3, bf16[1024,1024]{1,0:T(8,128)(2,1)} %k_ref.3, bf16[1024,1024]{1,0:T(8,128)(2,1)} %k_ref.3, ...), custom_call_target="tpu_custom_call" | custom-call | bytes 1000 | tf_op jit(solution)/shard_map/pool/pallas_call | solution.py:72
  3.7 3.6 %collective-permute-start = (bf16[2,4,1024]{2,1,0:T(4,128)(2,1)}, bf16[2,4,1024]{2,1,0:T(4,128)(2,1)S(1)}, u32[]{:S(2)}, u32[]{:S(2)}) collective-permute-start(bf16[2,4,1024]{2,1,0:T(4,128)(2,1)} %get-tuple-element.47), channel_id=1, source_target_pairs={{0,32},{32,0},{1,33},{33,1},{2,34},{34,2},{3,35},{35,3},{4,36},{36... | collective-permute-start | bytes 49160 | tf_op jit(solution)/shard_map/ppermute | solution.py:345
  7.2 3.5 %collective-permute-start.1 = (bf16[160,1024]{1,0:T(8,128)(2,1)}, bf16[160,1024]{1,0:T(8,128)(2,1)S(1)}, u32[]{:S(2)}, u32[]{:S(2)}) collective-permute-start(bf16[160,1024]{1,0:T(8,128)(2,1)} %get-tuple-element.48), channel_id=1, source_target_pairs={{0,4},{4,8},{8,12},{12,16},{16,20},{20,24},{24,28},{28,32},{32,36}... | collective-permute-start | bytes 983048 | tf_op jit(solution)/shard_map/ppermute | solution.py:349
  10.8 0.1 pad_add_fusion.1
  10.9 0.1 add_multiply_fusion.1
  11.0 0.1 add_multiply_fusion
  11.1 0.7 add_add_fusion.1
  11.7 6.4 %near.2 = (bf16[4,1024,256]{2,1,0:T(8,128)(2,1)}, f32[1024,128]{1,0:T(8,128)}, bf16[4,1024,256]{2,1,0:T(8,128)(2,1)}) custom-call(s32[66]{0:T(128)} %get-tuple-element.80.info_ref, bf16[1024,1024]{1,0:T(8,128)(2,1)} %q_ref.3, bf16[1024,1024]{1,0:T(8,128)(2,1)} %k_ref.3, bf16[1024,1024]{1,0:T(8,128)(2,1)} %v_ref.3, ...), custom_call_target="tpu_custom_call" | custom-call | bytes 1000 | tf_op jit(solution)/shard_map/near/pallas_call | solution.py:202
  18.2 0.0 collective-permute-done.1.pk_ref.pv_ref.pk1_ref.pv1_ref
  18.2 5.9 %collective-permute-start.3 = (bf16[2,1,8,1024]{3,2,0,1:T(8,128)(2,1)S(1)}, bf16[2,1,8,1024]{3,2,0,1:T(8,128)(2,1)S(1)}, u32[]{:S(2)}, u32[]{:S(2)}) collective-permute-start(bf16[2,1,8,1024]{3,2,0,1:T(8,128)(2,1)S(1)} %maximum_bitcast_fusion), channel_id=1, source_target_pairs={{0,20},{4,24},{8,28},{12,0},{16,4},{20,8},{24,12},{28,16},{1,21},{... | collective-permute-start | bytes 98312 | tf_op jit(solution)/shard_map/ppermute | solution.py:36
  24.1 0.0 collective-permute-start.2
  24.1 6.3 %near.3 = (bf16[4,1024,256]{2,1,0:T(8,128)(2,1)}, f32[1024,128]{1,0:T(8,128)}, bf16[4,1024,256]{2,1,0:T(8,128)(2,1)}) custom-call(s32[66]{0:T(128)} %get-tuple-element.79.info_ref, bf16[1024,1024]{1,0:T(8,128)(2,1)} %q_ref.3, bf16[1024,1024]{1,0:T(8,128)(2,1)} %k_ref.3, ...), custom_call_target="tpu_custom_call", output_to_operand_aliasing={{0}: (10, {}), {1}: (11, {}), {2}: (12, {})} | custom-call | bytes 1000 | tf_op jit(solution)/shard_map/near/pallas_call | solution.py:202
  30.4 0.0 collective-permute-done.2
  30.4 3.7 %collective-permute-start.5 = (bf16[2,2,8,1024]{3,2,0,1:T(8,128)(2,1)S(1)}, bf16[2,2,8,1024]{3,2,0,1:T(8,128)(2,1)S(1)}, u32[]{:S(2)}, u32[]{:S(2)}) collective-permute-start(bf16[2,2,8,1024]{3,2,0,1:T(8,128)(2,1)S(1)} %pad_maximum_fusion.3), channel_id=1, source_target_pairs={{0,28},{4,0},{8,4},{12,8},{16,12},{20,16},{24,20},{28,24},{1,29},{... | collective-permute-start | bytes 196616 | tf_op jit(solution)/shard_map/ppermute | solution.py:36
  34.1 0.1 collective-permute-start.4
  34.2 4.6 %collective-permute-done.4 = bf16[2,3,8,1024]{3,2,0,1:T(8,128)(2,1)S(1)} collective-permute-done((bf16[2,3,8,1024]{3,2,0,1:T(8,128)(2,1)S(1)}, bf16[2,3,8,1024]{3,2,0,1:T(8,128)(2,1)S(1)}, u32[]{:S(2)}, u32[]{:S(2)}) %collective-permute-start.4) | collective-permute-done | bytes 98336 | tf_op jit(solution)/shard_map/ppermute | solution.py:36
  38.9 0.0 collective-permute-done.5
  38.9 3.0 %collective-permute-start.8 = (bf16[2,8,8,512]{3,2,0,1:T(8,128)(2,1)S(1)}, bf16[2,8,8,512]{3,2,0,1:T(8,128)(2,1)S(1)}, u32[]{:S(2)}, u32[]{:S(2)}) collective-permute-start(bf16[2,8,8,512]{3,2,0,1:T(8,128)(2,1)S(1)} %get-tuple-element.78), channel_id=1, source_target_pairs={{0,128},{64,192},{128,0},{192,64},{1,129},{65,193},{129,1},{193,65... | collective-permute-start | bytes 393224 | tf_op jit(solution)/shard_map/ppermute | solution.py:36
  41.9 0.8 collective-permute-start.7
  42.7 0.7 collective-permute-start.6
  43.4 0.1 iota_add_fusion
  43.5 0.7 add.172.cell_ref
  44.2 0.1 collective-permute-done.8
  44.3 1.7 %collective-permute-done.7 = bf16[2,8,8,512]{3,2,0,1:T(8,128)(2,1)S(1)} collective-permute-done((bf16[2,8,8,512]{3,2,0,1:T(8,128)(2,1)S(1)}, bf16[2,8,8,512]{3,2,0,1:T(8,128)(2,1)S(1)}, u32[]{:S(2)}, u32[]{:S(2)}) %collective-permute-start.7) | collective-permute-done | bytes 131104 | tf_op jit(solution)/shard_map/ppermute | solution.py:36
  46.1 3.1 %collective-permute-done.6 = bf16[2,8,8,512]{3,2,0,1:T(8,128)(2,1)S(1)} collective-permute-done((bf16[2,8,8,512]{3,2,0,1:T(8,128)(2,1)S(1)}, bf16[2,8,8,512]{3,2,0,1:T(8,128)(2,1)S(1)}, u32[]{:S(2)}, u32[]{:S(2)}) %collective-permute-start.6) | collective-permute-done | bytes 131104 | tf_op jit(solution)/shard_map/ppermute | solution.py:36
  49.1 0.8 copy_bitcast_fusion.1.k2_ref.v2_ref
  49.9 3.7 %far.4.refs_0_ = bf16[1024,256]{1,0:T(8,128)(2,1)} custom-call(s32[1]{0:T(128)} %bitcast.4.lim_ref, bf16[4,1024,256]{2,1,0:T(8,128)(2,1)} %get-tuple-element.57.q_ref, bf16[4,1024,256]{2,1,0:T(8,128)(2,1)} %get-tuple-element.58.n_ref, f32[1024,128]{1,0:T(8,128)} %get-tuple-element.59.lse_ref, bf16[2,256,512]{2,1,0:T(8,128)(2,1)} %copy_bitcast_fusion.1.k2_ref.v2_ref, ...), custom_call_target="tpu_custom_call" | custom-call | bytes 1000 | tf_op jit(solution)/shard_map/far/pallas_call | solution.py:269
  53.7 0.3 collective-permute-start.12
  54.0 0.0 collective-permute-start.11
  54.0 0.5 collective-permute-start.10
  54.4 1.0 collective-permute-start.9
  55.5 3.8 %far.5.refs_1_ = bf16[1024,256]{1,0:T(8,128)(2,1)} custom-call(s32[1]{0:T(128)} %bitcast.4.lim_ref, bf16[4,1024,256]{2,1,0:T(8,128)(2,1)} %get-tuple-element.57.q_ref, bf16[4,1024,256]{2,1,0:T(8,128)(2,1)} %get-tuple-element.58.n_ref, f32[1024,128]{1,0:T(8,128)} %get-tuple-element.59.lse_ref, bf16[2,256,512]{2,1,0:T(8,128)(2,1)} %copy_bitcast_fusion.1.k2_ref.v2_ref, ...), custom_call_target="tpu_custom_call" | custom-call | bytes 1000 | tf_op jit(solution)/shard_map/far/pallas_call | solution.py:269
  59.3 1.1 collective-permute-start.14
  60.4 0.3 collective-permute-done.9
  60.7 0.8 copy_bitcast_fusion.k2_ref.v2_ref
  61.5 1.6 %collective-permute-done.12.refs_4_ = bf16[1024,256]{1,0:T(8,128)(2,1)S(1)} collective-permute-done((bf16[1024,256]{1,0:T(8,128)(2,1)}, bf16[1024,256]{1,0:T(8,128)(2,1)S(1)}, u32[]{:S(2)}, u32[]{:S(2)}) %collective-permute-start.12) | collective-permute-done | bytes 524320 | tf_op jit(solution)/shard_map/ppermute | solution.py:400
  63.1 9.8 %collective-permute-start.15 = (bf16[1024,256]{1,0:T(8,128)(2,1)S(1)}, bf16[1024,256]{1,0:T(8,128)(2,1)S(1)}, u32[]{:S(2)}, u32[]{:S(2)}) collective-permute-start(bf16[1024,256]{1,0:T(8,128)(2,1)S(1)} %copy-done.1), channel_id=1, source_target_pairs={{0,1},{1,0},{2,3},{3,2},{4,5},{5,4},{6,7},{7,6},{8,9},{9,8},{10,11... | collective-permute-start | bytes 1572872 | tf_op jit(solution)/shard_map/ppermute | solution.py:396
  72.9 0.1 collective-permute-start.16
  73.0 0.4 collective-permute-start.17
  73.4 3.8 %far.6.refs_2_ = bf16[1024,256]{1,0:T(8,128)(2,1)} custom-call(s32[1]{0:T(128)} %bitcast.4.lim_ref, bf16[4,1024,256]{2,1,0:T(8,128)(2,1)} %get-tuple-element.57.q_ref, bf16[4,1024,256]{2,1,0:T(8,128)(2,1)} %get-tuple-element.58.n_ref, f32[1024,128]{1,0:T(8,128)} %get-tuple-element.59.lse_ref, bf16[2,256,512]{2,1,0:T(8,128)(2,1)} %copy_bitcast_fusion.k2_ref.v2_ref, ...), custom_call_target="tpu_custom_call" | custom-call | bytes 1000 | tf_op jit(solution)/shard_map/far/pallas_call | solution.py:269
  77.2 0.2 collective-permute-start.20
  77.4 0.0 collective-permute-done.14.refs_0_
  77.4 0.0 collective-permute-done.15.refs_2_
  77.4 0.0 collective-permute-done.17.refs_5_
  77.4 4.3 %far.7.refs_4_ = bf16[1024,256]{1,0:T(8,128)(2,1)} custom-call(s32[1]{0:T(128)} %bitcast.4.lim_ref, bf16[4,1024,256]{2,1,0:T(8,128)(2,1)} %get-tuple-element.57.q_ref, bf16[4,1024,256]{2,1,0:T(8,128)(2,1)} %get-tuple-element.58.n_ref, f32[1024,128]{1,0:T(8,128)} %get-tuple-element.59.lse_ref, bf16[2,256,512]{2,1,0:T(8,128)(2,1)} %copy_bitcast_fusion.k2_ref.v2_ref, ...), custom_call_target="tpu_custom_call" | custom-call | bytes 1000 | tf_op jit(solution)/shard_map/far/pallas_call | solution.py:269
  81.8 2.1 %collective-permute-start.21 = (bf16[1024,256]{1,0:T(8,128)(2,1)}, bf16[1024,256]{1,0:T(8,128)(2,1)}, u32[]{:S(2)}, u32[]{:S(2)}) collective-permute-start(bf16[1024,256]{1,0:T(8,128)(2,1)} %far.7.refs_4_), channel_id=1, source_target_pairs={{0,1},{1,0},{2,3},{3,2},{4,5},{5,4},{6,7},{7,6},{8,9},{9,8},{10,11... | collective-permute-start | bytes 1572872 | tf_op jit(solution)/shard_map/ppermute | solution.py:396
  83.9 0.1 collective-permute-start.19
  84.0 0.3 collective-permute-start.13
  84.4 1.1 collective-permute-start.18
  85.5 0.7 stack.80.place_ref
  86.2 0.6 stack.87.place_ref
  86.8 8.6 %project.3.refs_12_ = f32[1024,1024]{1,0:T(8,128)} custom-call(s32[6]{0:T(128)} %stack.87.place_ref, bf16[1024,256]{1,0:T(8,128)(2,1)} %far.4.refs_0_, bf16[1024,256]{1,0:T(8,128)(2,1)} %far.5.refs_1_, bf16[1024,256]{1,0:T(8,128)(2,1)} %copy-done.8, bf16[1024,256]{1,0:T(8,128)(2,1)} %copy-done.9, bf16[1024,256]{1,0:T(8,128)(2,1)} %copy-done.3, ...), custom_call_target="tpu_custom_call" | custom-call | bytes 1000 | tf_op jit(solution)/shard_map/project/pallas_call | solution.py:312
  95.4 0.8 copy-done.7
  96.2 0.8 copy-done.10
  97.0 9.3 %project.4.refs_8_ = f32[1024,1024]{1,0:T(8,128)} custom-call(s32[6]{0:T(128)} %stack.80.place_ref, bf16[1024,256]{1,0:T(8,128)(2,1)} %copy-done.4, bf16[1024,256]{1,0:T(8,128)(2,1)} %copy-done.10, bf16[1024,256]{1,0:T(8,128)(2,1)} %far.6.refs_2_, bf16[1024,256]{1,0:T(8,128)(2,1)} %copy-done.7, bf16[1024,256]{1,0:T(8,128)(2,1)} %far.7.refs_4_, ...), custom_call_target="tpu_custom_call" | custom-call | bytes 1000 | tf_op jit(solution)/shard_map/project/pallas_call | solution.py:312
  106.3 2.1 %collective-permute-done.18.refs_2_ = bf16[1024,256]{1,0:T(8,128)(2,1)S(1)} collective-permute-done((bf16[1024,256]{1,0:T(8,128)(2,1)}, bf16[1024,256]{1,0:T(8,128)(2,1)S(1)}, u32[]{:S(2)}, u32[]{:S(2)}) %collective-permute-start.18) | collective-permute-done | bytes 524320 | tf_op jit(solution)/shard_map/ppermute | solution.py:400
  108.4 1.2 %collective-permute-start.22 = (bf16[1024,256]{1,0:T(8,128)(2,1)S(1)}, bf16[1024,256]{1,0:T(8,128)(2,1)S(1)}, u32[]{:S(2)}, u32[]{:S(2)}) collective-permute-start(bf16[1024,256]{1,0:T(8,128)(2,1)S(1)} %collective-permute-done.13.refs_0_), channel_id=1, source_target_pairs={{0,1},{1,0},{2,3},{3,2},{4,5},{5,4},{6,7},{7,6},{8,9},{9,8},{10,11... | collective-permute-start | bytes 1572872 | tf_op jit(solution)/shard_map/ppermute | solution.py:396
  109.6 0.0 collective-permute-start.23
  109.6 0.6 pad_add_fusion.place_ref
  110.3 0.9 collective-permute-done.22.refs_1_
  111.2 0.7 collective-permute-done.23.refs_3_
  111.9 0.0 copy-done.11
  112.0 0.8 copy-done.12
  112.8 7.6 %project.5 = bf16[1024,1024]{1,0:T(8,128)(2,1)} custom-call(s32[4]{0:T(128)} %pad_add_fusion.place_ref, bf16[1024,256]{1,0:T(8,128)(2,1)} %copy-done.5, bf16[1024,256]{1,0:T(8,128)(2,1)} %copy-done.11, bf16[1024,256]{1,0:T(8,128)(2,1)} %copy-done.6, bf16[1024,256]{1,0:T(8,128)(2,1)} %copy-done.12, bf16[4096,1024]{1,0:T(8,128)(2,1)} %refs_7_.7, ...), custom_call_target="tpu_custom_call" | custom-call | bytes 1000 | tf_op jit(solution)/shard_map/project/pallas_call | solution.py:312
  (50 shorter events, 0.2 us)
Async XLA Ops:
  0.0 10.9 %copy-start.16 = (s32[4]{0:T(128)S(1)}, s32[4]{0:T(128)}, u32[]{:S(2)}) copy-start(s32[4]{0:T(128)} %constant.73.clone) | copy-start | bytes 52
  0.0 10.9 %copy-start.15 = (s32[8]{0:T(128)S(1)}, s32[8]{0:T(128)}, u32[]{:S(2)}) copy-start(s32[8]{0:T(128)} %constant.72.clone) | copy-start | bytes 100
  0.0 11.1 %copy-start.14 = (s32[64]{0:T(128)S(1)}, s32[64]{0:T(128)}, u32[]{:S(2)}) copy-start(s32[64]{0:T(128)} %param.10) | copy-start | bytes 772
  3.7 14.4 %collective-permute-start = (bf16[2,4,1024]{2,1,0:T(4,128)(2,1)}, bf16[2,4,1024]{2,1,0:T(4,128)(2,1)S(1)}, u32[]{:S(2)}, u32[]{:S(2)}) collective-permute-start(bf16[2,4,1024]{2,1,0:T(4,128)(2,1)} %get-tuple-element.47), channel_id=1, source_target_pairs={{0,32},{32,0},{1,33},{33,1},{2,34},{34,2},{3,35},{35,3},{4,36},{36... | collective-permute-start | bytes 49160 | tf_op jit(solution)/shard_map/ppermute | solution.py:345
  7.2 10.9 %collective-permute-start.1 = (bf16[160,1024]{1,0:T(8,128)(2,1)}, bf16[160,1024]{1,0:T(8,128)(2,1)S(1)}, u32[]{:S(2)}, u32[]{:S(2)}) collective-permute-start(bf16[160,1024]{1,0:T(8,128)(2,1)} %get-tuple-element.48), channel_id=1, source_target_pairs={{0,4},{4,8},{8,12},{12,16},{16,20},{20,24},{24,28},{28,32},{32,36}... | collective-permute-start | bytes 983048 | tf_op jit(solution)/shard_map/ppermute | solution.py:349
  11.7 6.4 %copy-start.13 = (bf16[2,4,1024]{2,1,0:T(4,128)(2,1)S(1)}, bf16[2,4,1024]{2,1,0:T(4,128)(2,1)}, u32[]{:S(2)}) copy-start(bf16[2,4,1024]{2,1,0:T(4,128)(2,1)} %get-tuple-element.47) | copy-start | bytes 49156
  18.2 5.9 %copy-start = (bf16[160,1024]{1,0:T(8,128)(2,1)}, bf16[160,1024]{1,0:T(8,128)(2,1)S(1)}, u32[]{:S(2)}) copy-start(bf16[160,1024]{1,0:T(8,128)(2,1)S(1)} %collective-permute-done.1.pk_ref.pv_ref.pk1_ref.pv1_ref) | copy-start | bytes 983044
  18.2 15.9 %collective-permute-start.3 = (bf16[2,1,8,1024]{3,2,0,1:T(8,128)(2,1)S(1)}, bf16[2,1,8,1024]{3,2,0,1:T(8,128)(2,1)S(1)}, u32[]{:S(2)}, u32[]{:S(2)}) collective-permute-start(bf16[2,1,8,1024]{3,2,0,1:T(8,128)(2,1)S(1)} %maximum_bitcast_fusion), channel_id=1, source_target_pairs={{0,20},{4,24},{8,28},{12,0},{16,4},{20,8},{24,12},{28,16},{1,21},{... | collective-permute-start | bytes 98312 | tf_op jit(solution)/shard_map/ppermute | solution.py:36
  24.1 6.3 %collective-permute-start.2 = (bf16[2,1,8,1024]{3,2,0,1:T(8,128)(2,1)S(1)}, bf16[2,1,8,1024]{3,2,0,1:T(8,128)(2,1)S(1)}, u32[]{:S(2)}, u32[]{:S(2)}) collective-permute-start(bf16[2,1,8,1024]{3,2,0,1:T(8,128)(2,1)S(1)} %maximum_bitcast_fusion), channel_id=1, source_target_pairs={{0,12},{4,16},{8,20},{12,24},{16,28},{20,0},{24,4},{28,8},{1,13},{... | collective-permute-start | bytes 98312 | tf_op jit(solution)/shard_map/ppermute | solution.py:36
  30.4 8.5 %collective-permute-start.5 = (bf16[2,2,8,1024]{3,2,0,1:T(8,128)(2,1)S(1)}, bf16[2,2,8,1024]{3,2,0,1:T(8,128)(2,1)S(1)}, u32[]{:S(2)}, u32[]{:S(2)}) collective-permute-start(bf16[2,2,8,1024]{3,2,0,1:T(8,128)(2,1)S(1)} %pad_maximum_fusion.3), channel_id=1, source_target_pairs={{0,28},{4,0},{8,4},{12,8},{16,12},{20,16},{24,20},{28,24},{1,29},{... | collective-permute-start | bytes 196616 | tf_op jit(solution)/shard_map/ppermute | solution.py:36
  34.1 4.8 %collective-permute-start.4 = (bf16[2,3,8,1024]{3,2,0,1:T(8,128)(2,1)S(1)}, bf16[2,3,8,1024]{3,2,0,1:T(8,128)(2,1)S(1)}, u32[]{:S(2)}, u32[]{:S(2)}) collective-permute-start(bf16[2,3,8,1024]{3,2,0,1:T(8,128)(2,1)S(1)} %pad_maximum_fusion.2), channel_id=1, source_target_pairs={{0,4},{4,8},{8,12},{12,16},{16,20},{20,24},{24,28},{28,0},{1,5},{5... | collective-permute-start | bytes 294920 | tf_op jit(solution)/shard_map/ppermute | solution.py:36
  38.9 5.4 %collective-permute-start.8 = (bf16[2,8,8,512]{3,2,0,1:T(8,128)(2,1)S(1)}, bf16[2,8,8,512]{3,2,0,1:T(8,128)(2,1)S(1)}, u32[]{:S(2)}, u32[]{:S(2)}) collective-permute-start(bf16[2,8,8,512]{3,2,0,1:T(8,128)(2,1)S(1)} %get-tuple-element.78), channel_id=1, source_target_pairs={{0,128},{64,192},{128,0},{192,64},{1,129},{65,193},{129,1},{193,65... | collective-permute-start | bytes 393224 | tf_op jit(solution)/shard_map/ppermute | solution.py:36
  41.9 4.2 %collective-permute-start.7 = (bf16[2,8,8,512]{3,2,0,1:T(8,128)(2,1)S(1)}, bf16[2,8,8,512]{3,2,0,1:T(8,128)(2,1)S(1)}, u32[]{:S(2)}, u32[]{:S(2)}) collective-permute-start(bf16[2,8,8,512]{3,2,0,1:T(8,128)(2,1)S(1)} %get-tuple-element.78), channel_id=1, source_target_pairs={{0,192},{64,0},{128,64},{192,128},{1,193},{65,1},{129,65},{193,129... | collective-permute-start | bytes 393224 | tf_op jit(solution)/shard_map/ppermute | solution.py:36
  42.7 6.4 %collective-permute-start.6 = (bf16[2,8,8,512]{3,2,0,1:T(8,128)(2,1)S(1)}, bf16[2,8,8,512]{3,2,0,1:T(8,128)(2,1)S(1)}, u32[]{:S(2)}, u32[]{:S(2)}) collective-permute-start(bf16[2,8,8,512]{3,2,0,1:T(8,128)(2,1)S(1)} %get-tuple-element.78), channel_id=1, source_target_pairs={{0,64},{64,128},{128,192},{192,0},{1,65},{65,129},{129,193},{193,1... | collective-permute-start | bytes 393224 | tf_op jit(solution)/shard_map/ppermute | solution.py:36
  53.7 9.5 %copy-start.1 = (bf16[1024,256]{1,0:T(8,128)(2,1)S(1)}, bf16[1024,256]{1,0:T(8,128)(2,1)}, u32[]{:S(2)}) copy-start(bf16[1024,256]{1,0:T(8,128)(2,1)} %far.4.refs_0_) | copy-start | bytes 1572868
  53.7 9.5 %collective-permute-start.12 = (bf16[1024,256]{1,0:T(8,128)(2,1)}, bf16[1024,256]{1,0:T(8,128)(2,1)S(1)}, u32[]{:S(2)}, u32[]{:S(2)}) collective-permute-start(bf16[1024,256]{1,0:T(8,128)(2,1)} %far.4.refs_0_), channel_id=1, source_target_pairs={{0,2},{2,0},{1,3},{3,1},{4,6},{6,4},{5,7},{7,5},{8,10},{10,8},{9,1... | collective-permute-start | bytes 1572872 | tf_op jit(solution)/shard_map/ppermute | solution.py:400
  54.0 6.4 %collective-permute-start.11 = (bf16[2,8,8,512]{3,2,0,1:T(8,128)(2,1)S(1)}, bf16[2,8,8,512]{3,2,0,1:T(8,128)(2,1)S(1)}, u32[]{:S(2)}, u32[]{:S(2)}) collective-permute-start(bf16[2,8,8,512]{3,2,0,1:T(8,128)(2,1)S(1)} %get-tuple-element.61), channel_id=1, source_target_pairs={{0,128},{64,192},{128,0},{192,64},{1,129},{65,193},{129,1},{193,65... | collective-permute-start | bytes 393224 | tf_op jit(solution)/shard_map/ppermute | solution.py:36
  54.0 6.4 %collective-permute-start.10 = (bf16[2,8,8,512]{3,2,0,1:T(8,128)(2,1)S(1)}, bf16[2,8,8,512]{3,2,0,1:T(8,128)(2,1)S(1)}, u32[]{:S(2)}, u32[]{:S(2)}) collective-permute-start(bf16[2,8,8,512]{3,2,0,1:T(8,128)(2,1)S(1)} %get-tuple-element.61), channel_id=1, source_target_pairs={{0,192},{64,0},{128,64},{192,128},{1,193},{65,1},{129,65},{193,129... | collective-permute-start | bytes 393224 | tf_op jit(solution)/shard_map/ppermute | solution.py:36
  54.4 6.2 %collective-permute-start.9 = (bf16[2,8,8,512]{3,2,0,1:T(8,128)(2,1)S(1)}, bf16[2,8,8,512]{3,2,0,1:T(8,128)(2,1)S(1)}, u32[]{:S(2)}, u32[]{:S(2)}) collective-permute-start(bf16[2,8,8,512]{3,2,0,1:T(8,128)(2,1)S(1)} %get-tuple-element.61), channel_id=1, source_target_pairs={{0,64},{64,128},{128,192},{192,0},{1,65},{65,129},{129,193},{193,1... | collective-permute-start | bytes 393224 | tf_op jit(solution)/shard_map/ppermute | solution.py:36
  59.3 18.1 %collective-permute-start.14 = (bf16[1024,256]{1,0:T(8,128)(2,1)}, bf16[1024,256]{1,0:T(8,128)(2,1)S(1)}, u32[]{:S(2)}, u32[]{:S(2)}) collective-permute-start(bf16[1024,256]{1,0:T(8,128)(2,1)} %far.5.refs_1_), channel_id=1, source_target_pairs={{0,2},{2,0},{1,3},{3,1},{4,6},{6,4},{5,7},{7,5},{8,10},{10,8},{9,1... | collective-permute-start | bytes 1572872 | tf_op jit(solution)/shard_map/ppermute | solution.py:400
  63.1 14.1 %copy-start.3 = (bf16[1024,256]{1,0:T(8,128)(2,1)}, bf16[1024,256]{1,0:T(8,128)(2,1)S(1)}, u32[]{:S(2)}) copy-start(bf16[1024,256]{1,0:T(8,128)(2,1)S(1)} %collective-permute-done.12.refs_4_) | copy-start | bytes 1572868
  63.1 14.3 %collective-permute-start.15 = (bf16[1024,256]{1,0:T(8,128)(2,1)S(1)}, bf16[1024,256]{1,0:T(8,128)(2,1)S(1)}, u32[]{:S(2)}, u32[]{:S(2)}) collective-permute-start(bf16[1024,256]{1,0:T(8,128)(2,1)S(1)} %copy-done.1), channel_id=1, source_target_pairs={{0,1},{1,0},{2,3},{3,2},{4,5},{5,4},{6,7},{7,6},{8,9},{9,8},{10,11... | collective-permute-start | bytes 1572872 | tf_op jit(solution)/shard_map/ppermute | solution.py:396
  72.9 4.5 %collective-permute-start.16 = (bf16[1024,256]{1,0:T(8,128)(2,1)}, bf16[1024,256]{1,0:T(8,128)(2,1)S(1)}, u32[]{:S(2)}, u32[]{:S(2)}) collective-permute-start(bf16[1024,256]{1,0:T(8,128)(2,1)} %far.5.refs_1_), channel_id=1, source_target_pairs={{0,1},{1,0},{2,3},{3,2},{4,5},{5,4},{6,7},{7,6},{8,9},{9,8},{10,11... | collective-permute-start | bytes 1572872 | tf_op jit(solution)/shard_map/ppermute | solution.py:396
  73.0 4.4 %collective-permute-start.17 = (bf16[1024,256]{1,0:T(8,128)(2,1)S(1)}, bf16[1024,256]{1,0:T(8,128)(2,1)}, u32[]{:S(2)}, u32[]{:S(2)}) collective-permute-start(bf16[1024,256]{1,0:T(8,128)(2,1)S(1)} %collective-permute-done.12.refs_4_), channel_id=1, source_target_pairs={{0,1},{1,0},{2,3},{3,2},{4,5},{5,4},{6,7},{7,6},{8,9},{9,8},{10,11... | collective-permute-start | bytes 1572872 | tf_op jit(solution)/shard_map/ppermute | solution.py:396
  77.2 6.8 %copy-start.2 = (bf16[1024,256]{1,0:T(8,128)(2,1)S(1)}, bf16[1024,256]{1,0:T(8,128)(2,1)}, u32[]{:S(2)}) copy-start(bf16[1024,256]{1,0:T(8,128)(2,1)} %far.6.refs_2_) | copy-start | bytes 1572868
  77.2 18.2 %collective-permute-start.20 = (bf16[1024,256]{1,0:T(8,128)(2,1)}, bf16[1024,256]{1,0:T(8,128)(2,1)S(1)}, u32[]{:S(2)}, u32[]{:S(2)}) collective-permute-start(bf16[1024,256]{1,0:T(8,128)(2,1)} %far.6.refs_2_), channel_id=1, source_target_pairs={{0,1},{1,0},{2,3},{3,2},{4,5},{5,4},{6,7},{7,6},{8,9},{9,8},{10,11... | collective-permute-start | bytes 1572872 | tf_op jit(solution)/shard_map/ppermute | solution.py:396
  77.4 6.5 %copy-start.4 = (bf16[1024,256]{1,0:T(8,128)(2,1)}, bf16[1024,256]{1,0:T(8,128)(2,1)S(1)}, u32[]{:S(2)}) copy-start(bf16[1024,256]{1,0:T(8,128)(2,1)S(1)} %collective-permute-done.14.refs_0_) | copy-start | bytes 1572868
  77.4 4.4 %copy-start.8 = (bf16[1024,256]{1,0:T(8,128)(2,1)}, bf16[1024,256]{1,0:T(8,128)(2,1)S(1)}, u32[]{:S(2)}) copy-start(bf16[1024,256]{1,0:T(8,128)(2,1)S(1)} %collective-permute-done.15.refs_2_) | copy-start | bytes 1572868
  77.4 4.4 %copy-start.9 = (bf16[1024,256]{1,0:T(8,128)(2,1)}, bf16[1024,256]{1,0:T(8,128)(2,1)S(1)}, u32[]{:S(2)}) copy-start(bf16[1024,256]{1,0:T(8,128)(2,1)S(1)} %collective-permute-done.16.refs_3_) | copy-start | bytes 1572868
  81.8 13.6 %collective-permute-start.21 = (bf16[1024,256]{1,0:T(8,128)(2,1)}, bf16[1024,256]{1,0:T(8,128)(2,1)}, u32[]{:S(2)}, u32[]{:S(2)}) collective-permute-start(bf16[1024,256]{1,0:T(8,128)(2,1)} %far.7.refs_4_), channel_id=1, source_target_pairs={{0,1},{1,0},{2,3},{3,2},{4,5},{5,4},{6,7},{7,6},{8,9},{9,8},{10,11... | collective-permute-start | bytes 1572872 | tf_op jit(solution)/shard_map/ppermute | solution.py:396
  83.9 11.5 %collective-permute-start.19 = (bf16[1024,256]{1,0:T(8,128)(2,1)S(1)}, bf16[1024,256]{1,0:T(8,128)(2,1)S(1)}, u32[]{:S(2)}, u32[]{:S(2)}) collective-permute-start(bf16[1024,256]{1,0:T(8,128)(2,1)S(1)} %collective-permute-done.14.refs_0_), channel_id=1, source_target_pairs={{0,1},{1,0},{2,3},{3,2},{4,5},{5,4},{6,7},{7,6},{8,9},{9,8},{10,11... | collective-permute-start | bytes 1572872 | tf_op jit(solution)/shard_map/ppermute | solution.py:396
  84.0 22.3 %collective-permute-start.13 = (bf16[1024,256]{1,0:T(8,128)(2,1)S(1)}, bf16[1024,256]{1,0:T(8,128)(2,1)S(1)}, u32[]{:S(2)}, u32[]{:S(2)}) collective-permute-start(bf16[1024,256]{1,0:T(8,128)(2,1)S(1)} %copy-done.2), channel_id=1, source_target_pairs={{0,2},{2,0},{1,3},{3,1},{4,6},{6,4},{5,7},{7,5},{8,10},{10,8},{9,1... | collective-permute-start | bytes 1572872 | tf_op jit(solution)/shard_map/ppermute | solution.py:400
  84.4 24.0 %collective-permute-start.18 = (bf16[1024,256]{1,0:T(8,128)(2,1)}, bf16[1024,256]{1,0:T(8,128)(2,1)S(1)}, u32[]{:S(2)}, u32[]{:S(2)}) collective-permute-start(bf16[1024,256]{1,0:T(8,128)(2,1)} %far.7.refs_4_), channel_id=1, source_target_pairs={{0,2},{2,0},{1,3},{3,1},{4,6},{6,4},{5,7},{7,5},{8,10},{10,8},{9,1... | collective-permute-start | bytes 1572872 | tf_op jit(solution)/shard_map/ppermute | solution.py:400
  95.4 0.8 copy-start.7
  96.2 0.8 copy-start.10
  106.3 5.6 %copy-start.5 = (bf16[1024,256]{1,0:T(8,128)(2,1)}, bf16[1024,256]{1,0:T(8,128)(2,1)S(1)}, u32[]{:S(2)}) copy-start(bf16[1024,256]{1,0:T(8,128)(2,1)S(1)} %collective-permute-done.13.refs_0_) | copy-start | bytes 1572868
  108.4 3.5 %copy-start.6 = (bf16[1024,256]{1,0:T(8,128)(2,1)}, bf16[1024,256]{1,0:T(8,128)(2,1)S(1)}, u32[]{:S(2)}) copy-start(bf16[1024,256]{1,0:T(8,128)(2,1)S(1)} %collective-permute-done.18.refs_2_) | copy-start | bytes 1572868
  108.4 2.8 %collective-permute-start.22 = (bf16[1024,256]{1,0:T(8,128)(2,1)S(1)}, bf16[1024,256]{1,0:T(8,128)(2,1)S(1)}, u32[]{:S(2)}, u32[]{:S(2)}) collective-permute-start(bf16[1024,256]{1,0:T(8,128)(2,1)S(1)} %collective-permute-done.13.refs_0_), channel_id=1, source_target_pairs={{0,1},{1,0},{2,3},{3,2},{4,5},{5,4},{6,7},{7,6},{8,9},{9,8},{10,11... | collective-permute-start | bytes 1572872 | tf_op jit(solution)/shard_map/ppermute | solution.py:396
  109.6 2.3 %collective-permute-start.23 = (bf16[1024,256]{1,0:T(8,128)(2,1)S(1)}, bf16[1024,256]{1,0:T(8,128)(2,1)S(1)}, u32[]{:S(2)}, u32[]{:S(2)}) collective-permute-start(bf16[1024,256]{1,0:T(8,128)(2,1)S(1)} %collective-permute-done.18.refs_2_), channel_id=1, source_target_pairs={{0,1},{1,0},{2,3},{3,2},{4,5},{5,4},{6,7},{7,6},{8,9},{9,8},{10,11... | collective-permute-start | bytes 1572872 | tf_op jit(solution)/shard_map/ppermute | solution.py:396
  111.2 0.8 copy-start.11
  112.0 0.8 copy-start.12

commit v3 on v2

--- a/solution.py
+++ b/solution.py
@@ -222,27 +222,28 @@
     )(jnp.concatenate([jnp.full((1,), first, jnp.int32), info]), *args)
 
 
-def far_kernel(pair, lim_ref, q_ref, n_ref, lse_ref, k2_ref, v2_ref, cell_ref, out_ref):
-    rows = out_ref.shape[0]
-    heads = out_ref.shape[1] // HD
+def far_kernel(pair, lim_ref, q_ref, n_ref, lse_ref, k2_ref, v2_ref, cell_ref, *out_refs):
+    rows = q_ref.shape[1]
+    heads = CHUNK * len(out_refs)
     ones = jnp.ones((k2_ref.shape[1], HD), jnp.bfloat16)
     cell = cell_ref[...]
     limit = lim_ref[0] + pl.program_id(0) * (rows // (G * G))
 
     def where(job):
         t, h = job
-        return slice(t * TILE, (t + 1) * TILE), slice(h * HD, (h + 1) * HD)
+        part = h % CHUNK * HD
+        return h // CHUNK, slice(t * TILE, (t + 1) * TILE), slice(part, part + HD), slice(h * HD, (h + 1) * HD)
 
     def score(job, _):
-        at, cols = where(job)
+        p, at, cols, keys = where(job)
         return lax.dot_general(
-            q_ref[0, at, cols], k2_ref[0, :, cols], (((1,), (1,)), ((), ())),
+            q_ref[p, at, cols], k2_ref[0, :, keys], (((1,), (1,)), ((), ())),
             preferred_element_type=jnp.float32,
         )
 
     def weigh(job, s):
         t, h = job
-        at, _ = where(job)
+        _, at, _, _ = where(job)
         last = limit + t * TILE // (G * G)
         s = s * SCALE + jnp.where(cell <= last, 0.0, -jnp.inf)
         lse = lse_ref[at, pair * CHUNK + h : pair * CHUNK + h + 1]
@@ -250,18 +251,18 @@
         return jnp.exp2(lse - top), jnp.exp2(s - top).astype(jnp.bfloat16)
 
     def finish(job, kept):
-        at, cols = where(job)
+        p, at, cols, keys = where(job)
         part, w = kept
-        values = jnp.concatenate([v2_ref[0, :, cols], ones], axis=1)
+        values = jnp.concatenate([v2_ref[0, :, keys], ones], axis=1)
         both = jnp.dot(w, values, preferred_element_type=jnp.float32)
-        summed = both[:, :HD] + n_ref[0, at, cols].astype(jnp.float32) * part
+        summed = both[:, :HD] + n_ref[p, at, cols].astype(jnp.float32) * part
         done = (summed / (both[:, HD:] + part)).astype(jnp.bfloat16)
-        out_ref[at, cols] = done
+        out_refs[p][at, cols] = done
 
     staged([(t, h) for h in range(heads) for t in range(rows // TILE)], [score, weigh, finish])
 
 
-def far(lim, query, partial, lse, kv2, col, cell, pair):
+def far(lim, query, partial, lse, kv2, col, cell, pair, count=1):
     rows, cells = query.shape[1], kv2.shape[1]
     width = CHUNK * HD
     tile = 512
@@ -272,16 +273,16 @@
             num_scalar_prefetch=1,
             grid=(rows // tile,),
             in_specs=[
-                pl.BlockSpec((1, tile, width), lambda i, s: (pair, i, 0)),
-                pl.BlockSpec((1, tile, width), lambda i, s: (pair, i, 0)),
+                pl.BlockSpec((count, tile, width), lambda i, s: (pair // count, i, 0)),
+                pl.BlockSpec((count, tile, width), lambda i, s: (pair // count, i, 0)),
                 pl.BlockSpec((tile, HD), lambda i, s: (i, 0)),
-                pl.BlockSpec((1, cells, width), lambda i, s: (0, 0, col)),
-                pl.BlockSpec((1, cells, width), lambda i, s: (1, 0, col)),
+                pl.BlockSpec((1, cells, count * width), lambda i, s: (0, 0, col)),
+                pl.BlockSpec((1, cells, count * width), lambda i, s: (1, 0, col)),
                 pl.BlockSpec((1, cells), lambda i, s: (0, 0)),
             ],
-            out_specs=pl.BlockSpec((tile, width), lambda i, s: (i, 0)),
+            out_specs=[pl.BlockSpec((tile, width), lambda i, s: (i, 0))] * count,
         ),
-        out_shape=jax.ShapeDtypeStruct((rows, width), jnp.bfloat16),
+        out_shape=[jax.ShapeDtypeStruct((rows, width), jnp.bfloat16)] * count,
         compiler_params=params(60),
         cost_estimate=cost(0),
         name="far",
@@ -395,9 +396,9 @@
 
     hop = lambda axis, xs: [lax.ppermute(o, axis, swap) for o in xs]
 
-    def attend(n, kv2, col):
-        own.append(far(lim, part[2], part[0], part[1], kv2, col, cell, n))
-        across.append(lax.ppermute(own[n], "xl", swap))
+    def attend(n, kv2, col, count=1):
+        own.extend(far(lim, part[2], part[0], part[1], kv2, col, cell, n, count))
+        across.extend(hop("xl", own[n:]))
 
     attend(0, kv_first, 0)
     kv_first, own[0] = lax.optimization_barrier((kv_first, own[0]))
@@ -405,12 +406,9 @@
     kv_rest, *both = lax.optimization_barrier((kv_rest, *own, across[0]))
     beside += hop("core", both[:2])
     diagonal += hop("core", both[2:])
-    attend(2, kv_rest, 0)
-    kv_rest, across[1], beside[0], beside[1], diagonal[0] = lax.optimization_barrier(
-        (kv_rest, across[1], beside[0], beside[1], diagonal[0])
-    )
+    attend(2, kv_rest, 0, 2)
+    own[2], own[3], across[1] = lax.optimization_barrier((own[2], own[3], across[1]))
     diagonal += hop("core", across[1:2])
-    attend(3, kv_rest, 1)
     beside += hop("core", own[2:])
     acc = add([(0, 0), (0, 1), (1, 0), (1, 1), (2, 0), (3, 0)], None)
     acc = add([(2, 1), (3, 1), (0, 2), (1, 2), (0, 3), (1, 3)], acc)

time: 121 us -> 117 us (0.967)
  Pallas kernels: 57.5 us -> 54.9 us
  waiting for transfers between devices: 15.2 us -> 17.2 us
  starting transfers between devices: 39.6 us -> 37.8 us
  local copies, waits for them, and re-layouts: 4.47 us -> 2.99 us
    ppermute x8 -> x12, waiting for transfers between devices: 1.65 us -> 7.36 us  [local(): hop = lambda axis, xs: [lax.ppermute(o, axis, swap) for o in xs]]
    ppermute x4 -> x0, waiting for transfers between devices: 3.65 us -> none  [attend(): across.append(lax.ppermute(own[n], 'xl', swap))]
    ppermute x4 -> x0, starting transfers between devices: 2.88 us -> none  [attend(): across.append(lax.ppermute(own[n], 'xl', swap))]
    pallas_call x4 -> x3, Pallas kernels: 15.7 us -> 13 us  [far(): pl.pallas_call(functools.partial(far_kernel, pair), grid_spec=pltpu.Prefe...]
    unnamed x38 -> x34, local copies, waits for them, and re-layouts: 2.48 us -> 0.92 us
    ppermute x8 -> x12, starting transfers between devices: 13.9 us -> 15.1 us  [local(): hop = lambda axis, xs: [lax.ppermute(o, axis, swap) for o in xs]]
  transfers between devices with their start and end apart: 24 -> 24, of which waited for: 9 -> 9; matrix products, arithmetic and copies ran while one was open for 4% -> 4% of each run, Pallas kernels for 35% -> 34%
where the time goes in v3:
time: 117 us; the launch traced here: 116 us
  Pallas kernels  54.9 us (47%)
  starting transfers between devices  37.8 us (32%)
  waiting for transfers between devices  17.2 us (15%)
  other arithmetic  3.33 us (3%)
  local copies, waits for them, and re-layouts  2.99 us (3%)
    pallas_call x3, Pallas kernels, project(): pl.pallas_call(functools.partial(project_kernel, n, acc is not None), gri...  25.5 us
    ppermute x10, starting transfers between devices, shift(): return lax.ppermute(x, axis, [(i, (i + by) % n) for i in range(n)])  15.6 us
    ppermute x12, starting transfers between devices, local(): hop = lambda axis, xs: [lax.ppermute(o, axis, swap) for o in xs]  15.1 us
    pallas_call x3, Pallas kernels, far(): pl.pallas_call(functools.partial(far_kernel, pair), grid_spec=pltpu.Prefe...  13 us
    pallas_call x2, Pallas kernels, near(): pl.pallas_call(near_kernel, grid_spec=pltpu.PrefetchScalarGridSpec(num_sc...  12.7 us
    ppermute x10, waiting for transfers between devices, shift(): return lax.ppermute(x, axis, [(i, (i + by) % n) for i in range(n)])  9.86 us
    ppermute x12, waiting for transfers between devices, local(): hop = lambda axis, xs: [lax.ppermute(o, axis, swap) for o in xs]  7.36 us
    pallas_call x1, Pallas kernels, pool(): pl.pallas_call(pool_kernel, grid=(1,), in_specs=[spec(block, b) for b in...  3.64 us
  transfers between devices with their start and end apart: 24, of which 9 were waited for; matrix products, arithmetic and copies ran while one was open for 4% of the time, Pallas kernels for 34%

profile of v3, /device:TPU:1, one launch (start us, length us, event | category | flops | bytes accessed | tf_op | source)
XLA Modules:
  0.0 116.5 jit_solution(16475665493197339802)
XLA Ops:
  0.0 3.6 %pool.1 = (bf16[64,1024]{1,0:T(8,128)(2,1)}, bf16[64,1024]{1,0:T(8,128)(2,1)}, bf16[2,4,1024]{2,1,0:T(4,128)(2,1)}, bf16[160,1024]{1,0:T(8,128)(2,1)}) custom-call(bf16[1024,1024]{1,0:T(8,128)(2,1)} %k_ref.3, bf16[1024,1024]{1,0:T(8,128)(2,1)} %k_ref.3, bf16[1024,1024]{1,0:T(8,128)(2,1)} %k_ref.3, bf16[1024,1024]{1,0:T(8,128)(2,1)} %k_ref.3, ...), custom_call_target="tpu_custom_call" | custom-call | bytes 1000 | tf_op jit(solution)/shard_map/pool/pallas_call | solution.py:72
  3.7 3.6 %collective-permute-start = (bf16[2,4,1024]{2,1,0:T(4,128)(2,1)}, bf16[2,4,1024]{2,1,0:T(4,128)(2,1)S(1)}, u32[]{:S(2)}, u32[]{:S(2)}) collective-permute-start(bf16[2,4,1024]{2,1,0:T(4,128)(2,1)} %get-tuple-element.47), channel_id=1, source_target_pairs={{0,32},{32,0},{1,33},{33,1},{2,34},{34,2},{3,35},{35,3},{4,36},{36... | collective-permute-start | bytes 49160 | tf_op jit(solution)/shard_map/ppermute | solution.py:346
  7.2 3.5 %collective-permute-start.1 = (bf16[160,1024]{1,0:T(8,128)(2,1)}, bf16[160,1024]{1,0:T(8,128)(2,1)S(1)}, u32[]{:S(2)}, u32[]{:S(2)}) collective-permute-start(bf16[160,1024]{1,0:T(8,128)(2,1)} %get-tuple-element.48), channel_id=1, source_target_pairs={{0,4},{4,8},{8,12},{12,16},{16,20},{20,24},{24,28},{28,32},{32,36}... | collective-permute-start | bytes 983048 | tf_op jit(solution)/shard_map/ppermute | solution.py:350
  10.8 0.1 pad_add_fusion.1
  10.9 0.1 add_multiply_fusion.1
  11.0 0.1 add_multiply_fusion
  11.1 0.7 add_add_fusion.1
  11.7 6.4 %near.2 = (bf16[4,1024,256]{2,1,0:T(8,128)(2,1)}, f32[1024,128]{1,0:T(8,128)}, bf16[4,1024,256]{2,1,0:T(8,128)(2,1)}) custom-call(s32[66]{0:T(128)} %get-tuple-element.80.info_ref, bf16[1024,1024]{1,0:T(8,128)(2,1)} %q_ref.3, bf16[1024,1024]{1,0:T(8,128)(2,1)} %k_ref.3, bf16[1024,1024]{1,0:T(8,128)(2,1)} %v_ref.3, ...), custom_call_target="tpu_custom_call" | custom-call | bytes 1000 | tf_op jit(solution)/shard_map/near/pallas_call | solution.py:202
  18.2 0.0 collective-permute-done.1.pk_ref.pv_ref.pk1_ref.pv1_ref
  18.2 5.8 %collective-permute-start.3 = (bf16[2,1,8,1024]{3,2,0,1:T(8,128)(2,1)S(1)}, bf16[2,1,8,1024]{3,2,0,1:T(8,128)(2,1)S(1)}, u32[]{:S(2)}, u32[]{:S(2)}) collective-permute-start(bf16[2,1,8,1024]{3,2,0,1:T(8,128)(2,1)S(1)} %maximum_bitcast_fusion), channel_id=1, source_target_pairs={{0,20},{4,24},{8,28},{12,0},{16,4},{20,8},{24,12},{28,16},{1,21},{... | collective-permute-start | bytes 98312 | tf_op jit(solution)/shard_map/ppermute | solution.py:36
  24.0 0.0 collective-permute-start.2
  24.1 6.3 %near.3 = (bf16[4,1024,256]{2,1,0:T(8,128)(2,1)}, f32[1024,128]{1,0:T(8,128)}, bf16[4,1024,256]{2,1,0:T(8,128)(2,1)}) custom-call(s32[66]{0:T(128)} %get-tuple-element.79.info_ref, bf16[1024,1024]{1,0:T(8,128)(2,1)} %q_ref.3, bf16[1024,1024]{1,0:T(8,128)(2,1)} %k_ref.3, ...), custom_call_target="tpu_custom_call", output_to_operand_aliasing={{0}: (10, {}), {1}: (11, {}), {2}: (12, {})} | custom-call | bytes 1000 | tf_op jit(solution)/shard_map/near/pallas_call | solution.py:202
  30.3 0.0 collective-permute-done.2
  30.4 3.7 %collective-permute-start.5 = (bf16[2,2,8,1024]{3,2,0,1:T(8,128)(2,1)S(1)}, bf16[2,2,8,1024]{3,2,0,1:T(8,128)(2,1)S(1)}, u32[]{:S(2)}, u32[]{:S(2)}) collective-permute-start(bf16[2,2,8,1024]{3,2,0,1:T(8,128)(2,1)S(1)} %pad_maximum_fusion.3), channel_id=1, source_target_pairs={{0,28},{4,0},{8,4},{12,8},{16,12},{20,16},{24,20},{28,24},{1,29},{... | collective-permute-start | bytes 196616 | tf_op jit(solution)/shard_map/ppermute | solution.py:36
  34.1 0.1 collective-permute-start.4
  34.2 4.6 %collective-permute-done.4 = bf16[2,3,8,1024]{3,2,0,1:T(8,128)(2,1)S(1)} collective-permute-done((bf16[2,3,8,1024]{3,2,0,1:T(8,128)(2,1)S(1)}, bf16[2,3,8,1024]{3,2,0,1:T(8,128)(2,1)S(1)}, u32[]{:S(2)}, u32[]{:S(2)}) %collective-permute-start.4) | collective-permute-done | bytes 98336 | tf_op jit(solution)/shard_map/ppermute | solution.py:36
  38.8 0.0 collective-permute-done.5
  38.9 3.0 %collective-permute-start.8 = (bf16[2,8,8,512]{3,2,0,1:T(8,128)(2,1)S(1)}, bf16[2,8,8,512]{3,2,0,1:T(8,128)(2,1)S(1)}, u32[]{:S(2)}, u32[]{:S(2)}) collective-permute-start(bf16[2,8,8,512]{3,2,0,1:T(8,128)(2,1)S(1)} %get-tuple-element.78), channel_id=1, source_target_pairs={{0,128},{64,192},{128,0},{192,64},{1,129},{65,193},{129,1},{193,65... | collective-permute-start | bytes 393224 | tf_op jit(solution)/shard_map/ppermute | solution.py:36
  41.9 0.8 collective-permute-start.7
  42.7 0.7 collective-permute-start.6
  43.3 0.1 iota_add_fusion
  43.4 0.7 add.172.cell_ref
  44.1 0.1 collective-permute-done.8
  44.3 1.7 %collective-permute-done.7 = bf16[2,8,8,512]{3,2,0,1:T(8,128)(2,1)S(1)} collective-permute-done((bf16[2,8,8,512]{3,2,0,1:T(8,128)(2,1)S(1)}, bf16[2,8,8,512]{3,2,0,1:T(8,128)(2,1)S(1)}, u32[]{:S(2)}, u32[]{:S(2)}) %collective-permute-start.7) | collective-permute-done | bytes 131104 | tf_op jit(solution)/shard_map/ppermute | solution.py:36
  46.0 3.1 %collective-permute-done.6 = bf16[2,8,8,512]{3,2,0,1:T(8,128)(2,1)S(1)} collective-permute-done((bf16[2,8,8,512]{3,2,0,1:T(8,128)(2,1)S(1)}, bf16[2,8,8,512]{3,2,0,1:T(8,128)(2,1)S(1)}, u32[]{:S(2)}, u32[]{:S(2)}) %collective-permute-start.6) | collective-permute-done | bytes 131104 | tf_op jit(solution)/shard_map/ppermute | solution.py:36
  49.1 0.8 copy_bitcast_fusion.1.k2_ref.v2_ref
  49.9 3.7 %far.3.refs_0_ = bf16[1024,256]{1,0:T(8,128)(2,1)} custom-call(s32[1]{0:T(128)} %bitcast.4.lim_ref, bf16[4,1024,256]{2,1,0:T(8,128)(2,1)} %get-tuple-element.57.q_ref, bf16[4,1024,256]{2,1,0:T(8,128)(2,1)} %get-tuple-element.58.n_ref, f32[1024,128]{1,0:T(8,128)} %get-tuple-element.59.lse_ref, bf16[2,256,512]{2,1,0:T(8,128)(2,1)} %copy_bitcast_fusion.1.k2_ref.v2_ref, ...), custom_call_target="tpu_custom_call" | custom-call | bytes 1000 | tf_op jit(solution)/shard_map/far/pallas_call | solution.py:270
  53.6 0.3 collective-permute-start.12
  54.0 0.5 collective-permute-start.10
  54.4 1.1 collective-permute-start.9
  55.5 3.8 %far.4.refs_1_ = bf16[1024,256]{1,0:T(8,128)(2,1)} custom-call(s32[1]{0:T(128)} %bitcast.4.lim_ref, bf16[4,1024,256]{2,1,0:T(8,128)(2,1)} %get-tuple-element.57.q_ref, bf16[4,1024,256]{2,1,0:T(8,128)(2,1)} %get-tuple-element.58.n_ref, f32[1024,128]{1,0:T(8,128)} %get-tuple-element.59.lse_ref, bf16[2,256,512]{2,1,0:T(8,128)(2,1)} %copy_bitcast_fusion.1.k2_ref.v2_ref, ...), custom_call_target="tpu_custom_call" | custom-call | bytes 1000 | tf_op jit(solution)/shard_map/far/pallas_call | solution.py:270
  59.3 1.1 collective-permute-start.15
  60.4 0.0 collective-permute-done.11
  60.4 0.3 collective-permute-done.9
  60.7 0.8 copy_bitcast_fusion.k2_ref.v2_ref
  61.5 1.6 %collective-permute-done.12.refs_4_ = bf16[1024,256]{1,0:T(8,128)(2,1)S(1)} collective-permute-done((bf16[1024,256]{1,0:T(8,128)(2,1)}, bf16[1024,256]{1,0:T(8,128)(2,1)S(1)}, u32[]{:S(2)}, u32[]{:S(2)}) %collective-permute-start.12) | collective-permute-done | bytes 524320 | tf_op jit(solution)/shard_map/ppermute | solution.py:397
  63.1 9.8 %collective-permute-start.19 = (bf16[1024,256]{1,0:T(8,128)(2,1)S(1)}, bf16[1024,256]{1,0:T(8,128)(2,1)S(1)}, u32[]{:S(2)}, u32[]{:S(2)}) collective-permute-start(bf16[1024,256]{1,0:T(8,128)(2,1)S(1)} %copy-done.1), channel_id=1, source_target_pairs={{0,1},{1,0},{2,3},{3,2},{4,5},{5,4},{6,7},{7,6},{8,9},{9,8},{10,11... | collective-permute-start | bytes 1572872 | tf_op jit(solution)/shard_map/ppermute | solution.py:397
  72.9 0.1 collective-permute-start.20
  73.0 0.4 collective-permute-start.21
  73.4 5.5 %far.5 = (bf16[1024,256]{1,0:T(8,128)(2,1)}, bf16[1024,256]{1,0:T(8,128)(2,1)}) custom-call(s32[1]{0:T(128)} %bitcast.4.lim_ref, bf16[4,1024,256]{2,1,0:T(8,128)(2,1)} %get-tuple-element.57.q_ref, bf16[4,1024,256]{2,1,0:T(8,128)(2,1)} %get-tuple-element.58.n_ref, f32[1024,128]{1,0:T(8,128)} %get-tuple-element.59.lse_ref, ...), custom_call_target="tpu_custom_call" | custom-call | bytes 1000 | tf_op jit(solution)/shard_map/far/pallas_call | solution.py:270
  78.9 0.0 collective-permute-done.15.refs_0_
  78.9 0.0 copy-start.3
  78.9 0.5 collective-permute-start.16
  79.4 0.1 collective-permute-start.17
  79.5 0.4 collective-permute-start.18
  80.0 0.0 collective-permute-done.20.refs_3_
  80.0 0.3 collective-permute-start.13
  80.3 0.0 collective-permute-done.21.refs_5_
  80.3 1.2 collective-permute-start.14
  81.5 0.7 stack.80.place_ref
  82.1 0.7 stack.87.place_ref
  82.8 8.6 %project.3.refs_12_ = f32[1024,1024]{1,0:T(8,128)} custom-call(s32[6]{0:T(128)} %stack.87.place_ref, bf16[1024,256]{1,0:T(8,128)(2,1)} %far.3.refs_0_, bf16[1024,256]{1,0:T(8,128)(2,1)} %far.4.refs_1_, bf16[1024,256]{1,0:T(8,128)(2,1)} %copy-done.6, bf16[1024,256]{1,0:T(8,128)(2,1)} %copy-done.7, bf16[1024,256]{1,0:T(8,128)(2,1)} %copy-done.2, ...), custom_call_target="tpu_custom_call" | custom-call | bytes 1000 | tf_op jit(solution)/shard_map/project/pallas_call | solution.py:313
  91.5 0.0 collective-permute-done.17.refs_3_
  91.5 0.0 collective-permute-done.18.refs_5_
  91.5 9.3 %project.4.refs_8_ = f32[1024,1024]{1,0:T(8,128)} custom-call(s32[6]{0:T(128)} %stack.80.place_ref, bf16[1024,256]{1,0:T(8,128)(2,1)} %copy-done.3, bf16[1024,256]{1,0:T(8,128)(2,1)} %collective-permute-done.16.refs_1_, bf16[1024,256]{1,0:T(8,128)(2,1)} %get-tuple-element.69.refs_2_, bf16[1024,256]{1,0:T(8,128)(2,1)} %collective-permute-done.17.refs_3_, ...), custom_call_target="tpu_custom_call" | custom-call | bytes 1000 | tf_op jit(solution)/shard_map/project/pallas_call | solution.py:313
  100.8 4.1 %collective-permute-done.14.refs_2_ = bf16[1024,256]{1,0:T(8,128)(2,1)S(1)} collective-permute-done((bf16[1024,256]{1,0:T(8,128)(2,1)}, bf16[1024,256]{1,0:T(8,128)(2,1)S(1)}, u32[]{:S(2)}, u32[]{:S(2)}) %collective-permute-start.14) | collective-permute-done | bytes 524320 | tf_op jit(solution)/shard_map/ppermute | solution.py:397
  104.9 0.9 collective-permute-start.22
  105.8 0.0 collective-permute-start.23
  105.8 0.6 pad_add_fusion.place_ref
  106.4 0.9 collective-permute-done.22.refs_1_
  107.3 0.7 collective-permute-done.23.refs_3_
  108.1 0.0 copy-done.9
  108.1 0.8 copy-done.10
  108.9 7.6 %project.5 = bf16[1024,1024]{1,0:T(8,128)(2,1)} custom-call(s32[4]{0:T(128)} %pad_add_fusion.place_ref, bf16[1024,256]{1,0:T(8,128)(2,1)} %copy-done.4, bf16[1024,256]{1,0:T(8,128)(2,1)} %copy-done.9, bf16[1024,256]{1,0:T(8,128)(2,1)} %copy-done.5, bf16[1024,256]{1,0:T(8,128)(2,1)} %copy-done.10, bf16[4096,1024]{1,0:T(8,128)(2,1)} %refs_7_.7, ...), custom_call_target="tpu_custom_call" | custom-call | bytes 1000 | tf_op jit(solution)/shard_map/project/pallas_call | solution.py:313
  (45 shorter events, 0.2 us)
Async XLA Ops:
  0.0 10.9 %copy-start.14 = (s32[4]{0:T(128)S(1)}, s32[4]{0:T(128)}, u32[]{:S(2)}) copy-start(s32[4]{0:T(128)} %constant.73.clone) | copy-start | bytes 52
  0.0 10.9 %copy-start.13 = (s32[8]{0:T(128)S(1)}, s32[8]{0:T(128)}, u32[]{:S(2)}) copy-start(s32[8]{0:T(128)} %constant.72.clone) | copy-start | bytes 100
  0.0 11.1 %copy-start.12 = (s32[64]{0:T(128)S(1)}, s32[64]{0:T(128)}, u32[]{:S(2)}) copy-start(s32[64]{0:T(128)} %param.10) | copy-start | bytes 772
  3.7 14.5 %collective-permute-start = (bf16[2,4,1024]{2,1,0:T(4,128)(2,1)}, bf16[2,4,1024]{2,1,0:T(4,128)(2,1)S(1)}, u32[]{:S(2)}, u32[]{:S(2)}) collective-permute-start(bf16[2,4,1024]{2,1,0:T(4,128)(2,1)} %get-tuple-element.47), channel_id=1, source_target_pairs={{0,32},{32,0},{1,33},{33,1},{2,34},{34,2},{3,35},{35,3},{4,36},{36... | collective-permute-start | bytes 49160 | tf_op jit(solution)/shard_map/ppermute | solution.py:346
  7.2 11.0 %collective-permute-start.1 = (bf16[160,1024]{1,0:T(8,128)(2,1)}, bf16[160,1024]{1,0:T(8,128)(2,1)S(1)}, u32[]{:S(2)}, u32[]{:S(2)}) collective-permute-start(bf16[160,1024]{1,0:T(8,128)(2,1)} %get-tuple-element.48), channel_id=1, source_target_pairs={{0,4},{4,8},{8,12},{12,16},{16,20},{20,24},{24,28},{28,32},{32,36}... | collective-permute-start | bytes 983048 | tf_op jit(solution)/shard_map/ppermute | solution.py:350
  11.7 6.4 %copy-start.11 = (bf16[2,4,1024]{2,1,0:T(4,128)(2,1)S(1)}, bf16[2,4,1024]{2,1,0:T(4,128)(2,1)}, u32[]{:S(2)}) copy-start(bf16[2,4,1024]{2,1,0:T(4,128)(2,1)} %get-tuple-element.47) | copy-start | bytes 49156
  18.2 5.9 %copy-start = (bf16[160,1024]{1,0:T(8,128)(2,1)}, bf16[160,1024]{1,0:T(8,128)(2,1)S(1)}, u32[]{:S(2)}) copy-start(bf16[160,1024]{1,0:T(8,128)(2,1)S(1)} %collective-permute-done.1.pk_ref.pv_ref.pk1_ref.pv1_ref) | copy-start | bytes 983044
  18.2 15.8 %collective-permute-start.3 = (bf16[2,1,8,1024]{3,2,0,1:T(8,128)(2,1)S(1)}, bf16[2,1,8,1024]{3,2,0,1:T(8,128)(2,1)S(1)}, u32[]{:S(2)}, u32[]{:S(2)}) collective-permute-start(bf16[2,1,8,1024]{3,2,0,1:T(8,128)(2,1)S(1)} %maximum_bitcast_fusion), channel_id=1, source_target_pairs={{0,20},{4,24},{8,28},{12,0},{16,4},{20,8},{24,12},{28,16},{1,21},{... | collective-permute-start | bytes 98312 | tf_op jit(solution)/shard_map/ppermute | solution.py:36
  24.0 6.3 %collective-permute-start.2 = (bf16[2,1,8,1024]{3,2,0,1:T(8,128)(2,1)S(1)}, bf16[2,1,8,1024]{3,2,0,1:T(8,128)(2,1)S(1)}, u32[]{:S(2)}, u32[]{:S(2)}) collective-permute-start(bf16[2,1,8,1024]{3,2,0,1:T(8,128)(2,1)S(1)} %maximum_bitcast_fusion), channel_id=1, source_target_pairs={{0,12},{4,16},{8,20},{12,24},{16,28},{20,0},{24,4},{28,8},{1,13},{... | collective-permute-start | bytes 98312 | tf_op jit(solution)/shard_map/ppermute | solution.py:36
  30.4 8.5 %collective-permute-start.5 = (bf16[2,2,8,1024]{3,2,0,1:T(8,128)(2,1)S(1)}, bf16[2,2,8,1024]{3,2,0,1:T(8,128)(2,1)S(1)}, u32[]{:S(2)}, u32[]{:S(2)}) collective-permute-start(bf16[2,2,8,1024]{3,2,0,1:T(8,128)(2,1)S(1)} %pad_maximum_fusion.3), channel_id=1, source_target_pairs={{0,28},{4,0},{8,4},{12,8},{16,12},{20,16},{24,20},{28,24},{1,29},{... | collective-permute-start | bytes 196616 | tf_op jit(solution)/shard_map/ppermute | solution.py:36
  34.1 4.8 %collective-permute-start.4 = (bf16[2,3,8,1024]{3,2,0,1:T(8,128)(2,1)S(1)}, bf16[2,3,8,1024]{3,2,0,1:T(8,128)(2,1)S(1)}, u32[]{:S(2)}, u32[]{:S(2)}) collective-permute-start(bf16[2,3,8,1024]{3,2,0,1:T(8,128)(2,1)S(1)} %pad_maximum_fusion.2), channel_id=1, source_target_pairs={{0,4},{4,8},{8,12},{12,16},{16,20},{20,24},{24,28},{28,0},{1,5},{5... | collective-permute-start | bytes 294920 | tf_op jit(solution)/shard_map/ppermute | solution.py:36
  38.9 5.4 %collective-permute-start.8 = (bf16[2,8,8,512]{3,2,0,1:T(8,128)(2,1)S(1)}, bf16[2,8,8,512]{3,2,0,1:T(8,128)(2,1)S(1)}, u32[]{:S(2)}, u32[]{:S(2)}) collective-permute-start(bf16[2,8,8,512]{3,2,0,1:T(8,128)(2,1)S(1)} %get-tuple-element.78), channel_id=1, source_target_pairs={{0,128},{64,192},{128,0},{192,64},{1,129},{65,193},{129,1},{193,65... | collective-permute-start | bytes 393224 | tf_op jit(solution)/shard_map/ppermute | solution.py:36
  41.9 4.2 %collective-permute-start.7 = (bf16[2,8,8,512]{3,2,0,1:T(8,128)(2,1)S(1)}, bf16[2,8,8,512]{3,2,0,1:T(8,128)(2,1)S(1)}, u32[]{:S(2)}, u32[]{:S(2)}) collective-permute-start(bf16[2,8,8,512]{3,2,0,1:T(8,128)(2,1)S(1)} %get-tuple-element.78), channel_id=1, source_target_pairs={{0,192},{64,0},{128,64},{192,128},{1,193},{65,1},{129,65},{193,129... | collective-permute-start | bytes 393224 | tf_op jit(solution)/shard_map/ppermute | solution.py:36
  42.7 6.4 %collective-permute-start.6 = (bf16[2,8,8,512]{3,2,0,1:T(8,128)(2,1)S(1)}, bf16[2,8,8,512]{3,2,0,1:T(8,128)(2,1)S(1)}, u32[]{:S(2)}, u32[]{:S(2)}) collective-permute-start(bf16[2,8,8,512]{3,2,0,1:T(8,128)(2,1)S(1)} %get-tuple-element.78), channel_id=1, source_target_pairs={{0,64},{64,128},{128,192},{192,0},{1,65},{65,129},{129,193},{193,1... | collective-permute-start | bytes 393224 | tf_op jit(solution)/shard_map/ppermute | solution.py:36
  53.6 9.5 %copy-start.1 = (bf16[1024,256]{1,0:T(8,128)(2,1)S(1)}, bf16[1024,256]{1,0:T(8,128)(2,1)}, u32[]{:S(2)}) copy-start(bf16[1024,256]{1,0:T(8,128)(2,1)} %far.3.refs_0_) | copy-start | bytes 1572868
  53.6 9.5 %collective-permute-start.12 = (bf16[1024,256]{1,0:T(8,128)(2,1)}, bf16[1024,256]{1,0:T(8,128)(2,1)S(1)}, u32[]{:S(2)}, u32[]{:S(2)}) collective-permute-start(bf16[1024,256]{1,0:T(8,128)(2,1)} %far.3.refs_0_), channel_id=1, source_target_pairs={{0,2},{2,0},{1,3},{3,1},{4,6},{6,4},{5,7},{7,5},{8,10},{10,8},{9,1... | collective-permute-start | bytes 1572872 | tf_op jit(solution)/shard_map/ppermute | solution.py:397
  54.0 6.5 %collective-permute-start.11 = (bf16[2,8,8,512]{3,2,0,1:T(8,128)(2,1)S(1)}, bf16[2,8,8,512]{3,2,0,1:T(8,128)(2,1)S(1)}, u32[]{:S(2)}, u32[]{:S(2)}) collective-permute-start(bf16[2,8,8,512]{3,2,0,1:T(8,128)(2,1)S(1)} %get-tuple-element.61), channel_id=1, source_target_pairs={{0,128},{64,192},{128,0},{192,64},{1,129},{65,193},{129,1},{193,65... | collective-permute-start | bytes 393224 | tf_op jit(solution)/shard_map/ppermute | solution.py:36
  54.0 6.5 %collective-permute-start.10 = (bf16[2,8,8,512]{3,2,0,1:T(8,128)(2,1)S(1)}, bf16[2,8,8,512]{3,2,0,1:T(8,128)(2,1)S(1)}, u32[]{:S(2)}, u32[]{:S(2)}) collective-permute-start(bf16[2,8,8,512]{3,2,0,1:T(8,128)(2,1)S(1)} %get-tuple-element.61), channel_id=1, source_target_pairs={{0,192},{64,0},{128,64},{192,128},{1,193},{65,1},{129,65},{193,129... | collective-permute-start | bytes 393224 | tf_op jit(solution)/shard_map/ppermute | solution.py:36
  54.4 6.3 %collective-permute-start.9 = (bf16[2,8,8,512]{3,2,0,1:T(8,128)(2,1)S(1)}, bf16[2,8,8,512]{3,2,0,1:T(8,128)(2,1)S(1)}, u32[]{:S(2)}, u32[]{:S(2)}) collective-permute-start(bf16[2,8,8,512]{3,2,0,1:T(8,128)(2,1)S(1)} %get-tuple-element.61), channel_id=1, source_target_pairs={{0,64},{64,128},{128,192},{192,0},{1,65},{65,129},{129,193},{193,1... | collective-permute-start | bytes 393224 | tf_op jit(solution)/shard_map/ppermute | solution.py:36
  59.3 19.6 %collective-permute-start.15 = (bf16[1024,256]{1,0:T(8,128)(2,1)}, bf16[1024,256]{1,0:T(8,128)(2,1)S(1)}, u32[]{:S(2)}, u32[]{:S(2)}) collective-permute-start(bf16[1024,256]{1,0:T(8,128)(2,1)} %far.4.refs_1_), channel_id=1, source_target_pairs={{0,2},{2,0},{1,3},{3,1},{4,6},{6,4},{5,7},{7,5},{8,10},{10,8},{9,1... | collective-permute-start | bytes 1572872 | tf_op jit(solution)/shard_map/ppermute | solution.py:397
  63.1 15.8 %copy-start.2 = (bf16[1024,256]{1,0:T(8,128)(2,1)}, bf16[1024,256]{1,0:T(8,128)(2,1)S(1)}, u32[]{:S(2)}) copy-start(bf16[1024,256]{1,0:T(8,128)(2,1)S(1)} %collective-permute-done.12.refs_4_) | copy-start | bytes 1572868
  63.1 16.4 %collective-permute-start.19 = (bf16[1024,256]{1,0:T(8,128)(2,1)S(1)}, bf16[1024,256]{1,0:T(8,128)(2,1)S(1)}, u32[]{:S(2)}, u32[]{:S(2)}) collective-permute-start(bf16[1024,256]{1,0:T(8,128)(2,1)S(1)} %copy-done.1), channel_id=1, source_target_pairs={{0,1},{1,0},{2,3},{3,2},{4,5},{5,4},{6,7},{7,6},{8,9},{9,8},{10,11... | collective-permute-start | bytes 1572872 | tf_op jit(solution)/shard_map/ppermute | solution.py:397
  72.9 7.1 %collective-permute-start.20 = (bf16[1024,256]{1,0:T(8,128)(2,1)}, bf16[1024,256]{1,0:T(8,128)(2,1)S(1)}, u32[]{:S(2)}, u32[]{:S(2)}) collective-permute-start(bf16[1024,256]{1,0:T(8,128)(2,1)} %far.4.refs_1_), channel_id=1, source_target_pairs={{0,1},{1,0},{2,3},{3,2},{4,5},{5,4},{6,7},{7,6},{8,9},{9,8},{10,11... | collective-permute-start | bytes 1572872 | tf_op jit(solution)/shard_map/ppermute | solution.py:397
  73.0 7.3 %collective-permute-start.21 = (bf16[1024,256]{1,0:T(8,128)(2,1)S(1)}, bf16[1024,256]{1,0:T(8,128)(2,1)S(1)}, u32[]{:S(2)}, u32[]{:S(2)}) collective-permute-start(bf16[1024,256]{1,0:T(8,128)(2,1)S(1)} %collective-permute-done.12.refs_4_), channel_id=1, source_target_pairs={{0,1},{1,0},{2,3},{3,2},{4,5},{5,4},{6,7},{7,6},{8,9},{9,8},{10,11... | collective-permute-start | bytes 1572872 | tf_op jit(solution)/shard_map/ppermute | solution.py:397
  78.9 12.5 %copy-start.3 = (bf16[1024,256]{1,0:T(8,128)(2,1)}, bf16[1024,256]{1,0:T(8,128)(2,1)S(1)}, u32[]{:S(2)}) copy-start(bf16[1024,256]{1,0:T(8,128)(2,1)S(1)} %collective-permute-done.15.refs_0_) | copy-start | bytes 1572868
  78.9 12.5 %collective-permute-start.16 = (bf16[1024,256]{1,0:T(8,128)(2,1)S(1)}, bf16[1024,256]{1,0:T(8,128)(2,1)}, u32[]{:S(2)}, u32[]{:S(2)}) collective-permute-start(bf16[1024,256]{1,0:T(8,128)(2,1)S(1)} %collective-permute-done.15.refs_0_), channel_id=1, source_target_pairs={{0,1},{1,0},{2,3},{3,2},{4,5},{5,4},{6,7},{7,6},{8,9},{9,8},{10,11... | collective-permute-start | bytes 1572872 | tf_op jit(solution)/shard_map/ppermute | solution.py:397
  79.4 12.0 %collective-permute-start.17 = (bf16[1024,256]{1,0:T(8,128)(2,1)}, bf16[1024,256]{1,0:T(8,128)(2,1)}, u32[]{:S(2)}, u32[]{:S(2)}) collective-permute-start(bf16[1024,256]{1,0:T(8,128)(2,1)} %get-tuple-element.69.refs_2_), channel_id=1, source_target_pairs={{0,1},{1,0},{2,3},{3,2},{4,5},{5,4},{6,7},{7,6},{8,9},{9,8},{10,11... | collective-permute-start | bytes 1572872 | tf_op jit(solution)/shard_map/ppermute | solution.py:397
  79.5 3.3 %copy-start.6 = (bf16[1024,256]{1,0:T(8,128)(2,1)}, bf16[1024,256]{1,0:T(8,128)(2,1)S(1)}, u32[]{:S(2)}) copy-start(bf16[1024,256]{1,0:T(8,128)(2,1)S(1)} %collective-permute-done.19.refs_2_) | copy-start | bytes 1572868
  79.5 12.0 %collective-permute-start.18 = (bf16[1024,256]{1,0:T(8,128)(2,1)}, bf16[1024,256]{1,0:T(8,128)(2,1)}, u32[]{:S(2)}, u32[]{:S(2)}) collective-permute-start(bf16[1024,256]{1,0:T(8,128)(2,1)} %get-tuple-element.70.refs_4_), channel_id=1, source_target_pairs={{0,1},{1,0},{2,3},{3,2},{4,5},{5,4},{6,7},{7,6},{8,9},{9,8},{10,11... | collective-permute-start | bytes 1572872 | tf_op jit(solution)/shard_map/ppermute | solution.py:397
  80.0 2.9 %copy-start.7 = (bf16[1024,256]{1,0:T(8,128)(2,1)}, bf16[1024,256]{1,0:T(8,128)(2,1)S(1)}, u32[]{:S(2)}) copy-start(bf16[1024,256]{1,0:T(8,128)(2,1)S(1)} %collective-permute-done.20.refs_3_) | copy-start | bytes 1572868
  80.0 20.9 %collective-permute-start.13 = (bf16[1024,256]{1,0:T(8,128)(2,1)}, bf16[1024,256]{1,0:T(8,128)(2,1)S(1)}, u32[]{:S(2)}, u32[]{:S(2)}) collective-permute-start(bf16[1024,256]{1,0:T(8,128)(2,1)} %get-tuple-element.69.refs_2_), channel_id=1, source_target_pairs={{0,2},{2,0},{1,3},{3,1},{4,6},{6,4},{5,7},{7,5},{8,10},{10,8},{9,1... | collective-permute-start | bytes 1572872 | tf_op jit(solution)/shard_map/ppermute | solution.py:397
  80.3 2.5 %copy-start.8 = (bf16[1024,256]{1,0:T(8,128)(2,1)}, bf16[1024,256]{1,0:T(8,128)(2,1)S(1)}, u32[]{:S(2)}) copy-start(bf16[1024,256]{1,0:T(8,128)(2,1)S(1)} %collective-permute-done.21.refs_5_) | copy-start | bytes 1572868
  80.3 24.6 %collective-permute-start.14 = (bf16[1024,256]{1,0:T(8,128)(2,1)}, bf16[1024,256]{1,0:T(8,128)(2,1)S(1)}, u32[]{:S(2)}, u32[]{:S(2)}) collective-permute-start(bf16[1024,256]{1,0:T(8,128)(2,1)} %get-tuple-element.70.refs_4_), channel_id=1, source_target_pairs={{0,2},{2,0},{1,3},{3,1},{4,6},{6,4},{5,7},{7,5},{8,10},{10,8},{9,1... | collective-permute-start | bytes 1572872 | tf_op jit(solution)/shard_map/ppermute | solution.py:397
  100.8 7.2 %copy-start.4 = (bf16[1024,256]{1,0:T(8,128)(2,1)}, bf16[1024,256]{1,0:T(8,128)(2,1)S(1)}, u32[]{:S(2)}) copy-start(bf16[1024,256]{1,0:T(8,128)(2,1)S(1)} %collective-permute-done.13.refs_0_) | copy-start | bytes 1572868
  104.9 3.2 %copy-start.5 = (bf16[1024,256]{1,0:T(8,128)(2,1)}, bf16[1024,256]{1,0:T(8,128)(2,1)S(1)}, u32[]{:S(2)}) copy-start(bf16[1024,256]{1,0:T(8,128)(2,1)S(1)} %collective-permute-done.14.refs_2_) | copy-start | bytes 1572868
  104.9 2.4 %collective-permute-start.22 = (bf16[1024,256]{1,0:T(8,128)(2,1)S(1)}, bf16[1024,256]{1,0:T(8,128)(2,1)S(1)}, u32[]{:S(2)}, u32[]{:S(2)}) collective-permute-start(bf16[1024,256]{1,0:T(8,128)(2,1)S(1)} %collective-permute-done.13.refs_0_), channel_id=1, source_target_pairs={{0,1},{1,0},{2,3},{3,2},{4,5},{5,4},{6,7},{7,6},{8,9},{9,8},{10,11... | collective-permute-start | bytes 1572872 | tf_op jit(solution)/shard_map/ppermute | solution.py:397
  105.8 2.3 %collective-permute-start.23 = (bf16[1024,256]{1,0:T(8,128)(2,1)S(1)}, bf16[1024,256]{1,0:T(8,128)(2,1)S(1)}, u32[]{:S(2)}, u32[]{:S(2)}) collective-permute-start(bf16[1024,256]{1,0:T(8,128)(2,1)S(1)} %collective-permute-done.14.refs_2_), channel_id=1, source_target_pairs={{0,1},{1,0},{2,3},{3,2},{4,5},{5,4},{6,7},{7,6},{8,9},{9,8},{10,11... | collective-permute-start | bytes 1572872 | tf_op jit(solution)/shard_map/ppermute | solution.py:397
  107.3 0.8 copy-start.9
  108.1 0.8 copy-start.10

commit v4 on v3

--- a/solution.py
+++ b/solution.py
@@ -411,10 +411,12 @@
     diagonal += hop("core", across[1:2])
     beside += hop("core", own[2:])
     acc = add([(0, 0), (0, 1), (1, 0), (1, 1), (2, 0), (3, 0)], None)
-    acc = add([(2, 1), (3, 1), (0, 2), (1, 2), (0, 3), (1, 3)], acc)
-    across[2], across[3], acc = lax.optimization_barrier((across[2], across[3], acc))
-    diagonal += hop("core", across[2:])
-    return add([(2, 2), (3, 2), (2, 3), (3, 3)], acc, jnp.bfloat16)
+    across[2], acc = lax.optimization_barrier((across[2], acc))
+    diagonal += hop("core", across[2:3])
+    acc = add([(2, 1), (3, 1), (0, 2), (1, 2), (0, 3), (1, 3), (2, 2)], acc)
+    across[3], acc = lax.optimization_barrier((across[3], acc))
+    diagonal += hop("core", across[3:])
+    return add([(3, 2), (2, 3), (3, 3)], acc, jnp.bfloat16)
 
 
 def solution(mesh):

time: 117 us -> 113 us (0.966)
  waiting for transfers between devices: 17.2 us -> 12.3 us
  local copies, waits for them, and re-layouts: 2.99 us -> 4.24 us
    ppermute x12, waiting for transfers between devices: 7.36 us -> 3.41 us  [local(): hop = lambda axis, xs: [lax.ppermute(o, axis, swap) for o in xs]]
    unnamed x34, local copies, waits for them, and re-layouts: 0.92 us -> 2.21 us
  transfers between devices with their start and end apart: 24 -> 24, of which waited for: 9 -> 7; matrix products, arithmetic and copies ran while one was open for 4% -> 4% of each run, Pallas kernels for 34% -> 36%
where the time goes in v4:
time: 113 us; the launch traced here: 112 us
  Pallas kernels  54.9 us (49%)
  starting transfers between devices  37.1 us (33%)
  waiting for transfers between devices  12.3 us (11%)
  local copies, waits for them, and re-layouts  4.24 us (4%)
  other arithmetic  3.37 us (3%)
    pallas_call x3, Pallas kernels, project(): pl.pallas_call(functools.partial(project_kernel, n, acc is not None), gri...  25.6 us
    ppermute x10, starting transfers between devices, shift(): return lax.ppermute(x, axis, [(i, (i + by) % n) for i in range(n)])  15.9 us
    ppermute x12, starting transfers between devices, local(): hop = lambda axis, xs: [lax.ppermute(o, axis, swap) for o in xs]  14.1 us
    pallas_call x3, Pallas kernels, far(): pl.pallas_call(functools.partial(far_kernel, pair), grid_spec=pltpu.Prefe...  13 us
    pallas_call x2, Pallas kernels, near(): pl.pallas_call(near_kernel, grid_spec=pltpu.PrefetchScalarGridSpec(num_sc...  12.7 us
    ppermute x10, waiting for transfers between devices, shift(): return lax.ppermute(x, axis, [(i, (i + by) % n) for i in range(n)])  8.9 us
    pallas_call x1, Pallas kernels, pool(): pl.pallas_call(pool_kernel, grid=(1,), in_specs=[spec(block, b) for b in...  3.64 us
    ppermute x1, starting transfers between devices, local(): other = lax.ppermute(mine, 'xh', [(0, 1), (1, 0)])  3.57 us
  transfers between devices with their start and end apart: 24, of which 7 were waited for; matrix products, arithmetic and copies ran while one was open for 4% of the time, Pallas kernels for 36%

profile of v4, /device:TPU:1, one launch (start us, length us, event | category | flops | bytes accessed | tf_op | source)
XLA Modules:
  0.0 112.1 jit_solution(16106863880037935360)
XLA Ops:
  0.0 3.6 %pool.1 = (bf16[64,1024]{1,0:T(8,128)(2,1)}, bf16[64,1024]{1,0:T(8,128)(2,1)}, bf16[2,4,1024]{2,1,0:T(4,128)(2,1)}, bf16[160,1024]{1,0:T(8,128)(2,1)}) custom-call(bf16[1024,1024]{1,0:T(8,128)(2,1)} %k_ref.3, bf16[1024,1024]{1,0:T(8,128)(2,1)} %k_ref.3, bf16[1024,1024]{1,0:T(8,128)(2,1)} %k_ref.3, bf16[1024,1024]{1,0:T(8,128)(2,1)} %k_ref.3, ...), custom_call_target="tpu_custom_call" | custom-call | bytes 1000 | tf_op jit(solution)/shard_map/pool/pallas_call | solution.py:72
  3.7 3.6 %collective-permute-start = (bf16[2,4,1024]{2,1,0:T(4,128)(2,1)}, bf16[2,4,1024]{2,1,0:T(4,128)(2,1)S(1)}, u32[]{:S(2)}, u32[]{:S(2)}) collective-permute-start(bf16[2,4,1024]{2,1,0:T(4,128)(2,1)} %get-tuple-element.48), channel_id=1, source_target_pairs={{0,32},{32,0},{1,33},{33,1},{2,34},{34,2},{3,35},{35,3},{4,36},{36... | collective-permute-start | bytes 49160 | tf_op jit(solution)/shard_map/ppermute | solution.py:346
  7.2 3.5 %collective-permute-start.1 = (bf16[160,1024]{1,0:T(8,128)(2,1)}, bf16[160,1024]{1,0:T(8,128)(2,1)S(1)}, u32[]{:S(2)}, u32[]{:S(2)}) collective-permute-start(bf16[160,1024]{1,0:T(8,128)(2,1)} %get-tuple-element.49), channel_id=1, source_target_pairs={{0,4},{4,8},{8,12},{12,16},{16,20},{20,24},{24,28},{28,32},{32,36}... | collective-permute-start | bytes 983048 | tf_op jit(solution)/shard_map/ppermute | solution.py:350
  10.8 0.1 pad_add_fusion.1
  10.9 0.1 add_multiply_fusion.1
  11.0 0.1 add_multiply_fusion
  11.1 0.7 add_add_fusion.1
  11.7 6.4 %near.2 = (bf16[4,1024,256]{2,1,0:T(8,128)(2,1)}, f32[1024,128]{1,0:T(8,128)}, bf16[4,1024,256]{2,1,0:T(8,128)(2,1)}) custom-call(s32[66]{0:T(128)} %get-tuple-element.82.info_ref, bf16[1024,1024]{1,0:T(8,128)(2,1)} %q_ref.3, bf16[1024,1024]{1,0:T(8,128)(2,1)} %k_ref.3, bf16[1024,1024]{1,0:T(8,128)(2,1)} %v_ref.3, ...), custom_call_target="tpu_custom_call" | custom-call | bytes 1000 | tf_op jit(solution)/shard_map/near/pallas_call | solution.py:202
  18.1 0.0 collective-permute-done
  18.2 0.0 collective-permute-done.1.pk_ref.pv_ref.pk1_ref.pv1_ref
  18.2 5.6 %collective-permute-start.2 = (bf16[2,1,8,1024]{3,2,0,1:T(8,128)(2,1)S(1)}, bf16[2,1,8,1024]{3,2,0,1:T(8,128)(2,1)S(1)}, u32[]{:S(2)}, u32[]{:S(2)}) collective-permute-start(bf16[2,1,8,1024]{3,2,0,1:T(8,128)(2,1)S(1)} %maximum_bitcast_fusion), channel_id=1, source_target_pairs={{0,12},{4,16},{8,20},{12,24},{16,28},{20,0},{24,4},{28,8},{1,13},{... | collective-permute-start | bytes 98312 | tf_op jit(solution)/shard_map/ppermute | solution.py:36
  23.8 0.2 collective-permute-start.3
  24.1 6.3 %near.3 = (bf16[4,1024,256]{2,1,0:T(8,128)(2,1)}, f32[1024,128]{1,0:T(8,128)}, bf16[4,1024,256]{2,1,0:T(8,128)(2,1)}) custom-call(s32[66]{0:T(128)} %get-tuple-element.81.info_ref, bf16[1024,1024]{1,0:T(8,128)(2,1)} %q_ref.3, bf16[1024,1024]{1,0:T(8,128)(2,1)} %k_ref.3, ...), custom_call_target="tpu_custom_call", output_to_operand_aliasing={{0}: (10, {}), {1}: (11, {}), {2}: (12, {})} | custom-call | bytes 1000 | tf_op jit(solution)/shard_map/near/pallas_call | solution.py:202
  30.3 0.0 collective-permute-done.2
  30.4 2.4 %collective-permute-start.5 = (bf16[2,2,8,1024]{3,2,0,1:T(8,128)(2,1)S(1)}, bf16[2,2,8,1024]{3,2,0,1:T(8,128)(2,1)S(1)}, u32[]{:S(2)}, u32[]{:S(2)}) collective-permute-start(bf16[2,2,8,1024]{3,2,0,1:T(8,128)(2,1)S(1)} %pad_maximum_fusion.3), channel_id=1, source_target_pairs={{0,28},{4,0},{8,4},{12,8},{16,12},{20,16},{24,20},{28,24},{1,29},{... | collective-permute-start | bytes 196616 | tf_op jit(solution)/shard_map/ppermute | solution.py:36
  32.8 0.0 collective-permute-done.3
  32.8 0.1 collective-permute-start.4
  33.0 4.6 %collective-permute-done.4 = bf16[2,3,8,1024]{3,2,0,1:T(8,128)(2,1)S(1)} collective-permute-done((bf16[2,3,8,1024]{3,2,0,1:T(8,128)(2,1)S(1)}, bf16[2,3,8,1024]{3,2,0,1:T(8,128)(2,1)S(1)}, u32[]{:S(2)}, u32[]{:S(2)}) %collective-permute-start.4) | collective-permute-done | bytes 98336 | tf_op jit(solution)/shard_map/ppermute | solution.py:36
  37.6 0.0 collective-permute-done.5
  37.7 1.5 %collective-permute-start.6 = (bf16[2,8,8,512]{3,2,0,1:T(8,128)(2,1)S(1)}, bf16[2,8,8,512]{3,2,0,1:T(8,128)(2,1)S(1)}, u32[]{:S(2)}, u32[]{:S(2)}) collective-permute-start(bf16[2,8,8,512]{3,2,0,1:T(8,128)(2,1)S(1)} %get-tuple-element.80), channel_id=1, source_target_pairs={{0,64},{64,128},{128,192},{192,0},{1,65},{65,129},{129,193},{193,1... | collective-permute-start | bytes 393224 | tf_op jit(solution)/shard_map/ppermute | solution.py:36
  39.2 1.5 %collective-permute-start.7 = (bf16[2,8,8,512]{3,2,0,1:T(8,128)(2,1)S(1)}, bf16[2,8,8,512]{3,2,0,1:T(8,128)(2,1)S(1)}, u32[]{:S(2)}, u32[]{:S(2)}) collective-permute-start(bf16[2,8,8,512]{3,2,0,1:T(8,128)(2,1)S(1)} %get-tuple-element.80), channel_id=1, source_target_pairs={{0,192},{64,0},{128,64},{192,128},{1,193},{65,1},{129,65},{193,129... | collective-permute-start | bytes 393224 | tf_op jit(solution)/shard_map/ppermute | solution.py:36
  40.7 1.6 %collective-permute-start.8 = (bf16[2,8,8,512]{3,2,0,1:T(8,128)(2,1)S(1)}, bf16[2,8,8,512]{3,2,0,1:T(8,128)(2,1)S(1)}, u32[]{:S(2)}, u32[]{:S(2)}) collective-permute-start(bf16[2,8,8,512]{3,2,0,1:T(8,128)(2,1)S(1)} %get-tuple-element.80), channel_id=1, source_target_pairs={{0,128},{64,192},{128,0},{192,64},{1,129},{65,193},{129,1},{193,65... | collective-permute-start | bytes 393224 | tf_op jit(solution)/shard_map/ppermute | solution.py:36
  42.3 0.1 iota_add_fusion
  42.4 0.7 add.171.cell_ref
  43.1 3.0 %collective-permute-done.8 = bf16[2,8,8,512]{3,2,0,1:T(8,128)(2,1)S(1)} collective-permute-done((bf16[2,8,8,512]{3,2,0,1:T(8,128)(2,1)S(1)}, bf16[2,8,8,512]{3,2,0,1:T(8,128)(2,1)S(1)}, u32[]{:S(2)}, u32[]{:S(2)}) %collective-permute-start.8) | collective-permute-done | bytes 131104 | tf_op jit(solution)/shard_map/ppermute | solution.py:36
  46.1 0.8 copy_bitcast_fusion.1.k2_ref.v2_ref
  46.9 3.7 %far.3.refs_0_ = bf16[1024,256]{1,0:T(8,128)(2,1)} custom-call(s32[1]{0:T(128)} %bitcast.3.lim_ref, bf16[4,1024,256]{2,1,0:T(8,128)(2,1)} %get-tuple-element.58.q_ref, bf16[4,1024,256]{2,1,0:T(8,128)(2,1)} %get-tuple-element.59.n_ref, f32[1024,128]{1,0:T(8,128)} %get-tuple-element.60.lse_ref, bf16[2,256,512]{2,1,0:T(8,128)(2,1)} %copy_bitcast_fusion.1.k2_ref.v2_ref, ...), custom_call_target="tpu_custom_call" | custom-call | bytes 1000 | tf_op jit(solution)/shard_map/far/pallas_call | solution.py:270
  50.7 1.3 %collective-permute-start.12 = (bf16[1024,256]{1,0:T(8,128)(2,1)}, bf16[1024,256]{1,0:T(8,128)(2,1)S(1)}, u32[]{:S(2)}, u32[]{:S(2)}) collective-permute-start(bf16[1024,256]{1,0:T(8,128)(2,1)} %far.3.refs_0_), channel_id=1, source_target_pairs={{0,2},{2,0},{1,3},{3,1},{4,6},{6,4},{5,7},{7,5},{8,10},{10,8},{9,1... | collective-permute-start | bytes 1572872 | tf_op jit(solution)/shard_map/ppermute | solution.py:397
  52.0 1.3 %collective-permute-start.10 = (bf16[2,8,8,512]{3,2,0,1:T(8,128)(2,1)S(1)}, bf16[2,8,8,512]{3,2,0,1:T(8,128)(2,1)S(1)}, u32[]{:S(2)}, u32[]{:S(2)}) collective-permute-start(bf16[2,8,8,512]{3,2,0,1:T(8,128)(2,1)S(1)} %get-tuple-element.62), channel_id=1, source_target_pairs={{0,192},{64,0},{128,64},{192,128},{1,193},{65,1},{129,65},{193,129... | collective-permute-start | bytes 393224 | tf_op jit(solution)/shard_map/ppermute | solution.py:36
  53.3 0.8 collective-permute-start.11
  54.1 0.8 collective-permute-start.9
  54.8 3.8 %far.4.refs_1_ = bf16[1024,256]{1,0:T(8,128)(2,1)} custom-call(s32[1]{0:T(128)} %bitcast.3.lim_ref, bf16[4,1024,256]{2,1,0:T(8,128)(2,1)} %get-tuple-element.58.q_ref, bf16[4,1024,256]{2,1,0:T(8,128)(2,1)} %get-tuple-element.59.n_ref, f32[1024,128]{1,0:T(8,128)} %get-tuple-element.60.lse_ref, bf16[2,256,512]{2,1,0:T(8,128)(2,1)} %copy_bitcast_fusion.1.k2_ref.v2_ref, ...), custom_call_target="tpu_custom_call" | custom-call | bytes 1000 | tf_op jit(solution)/shard_map/far/pallas_call | solution.py:270
  58.7 0.1 collective-permute-start.19
  58.7 1.2 %collective-permute-done.9 = bf16[2,8,8,512]{3,2,0,1:T(8,128)(2,1)S(1)} collective-permute-done((bf16[2,8,8,512]{3,2,0,1:T(8,128)(2,1)S(1)}, bf16[2,8,8,512]{3,2,0,1:T(8,128)(2,1)S(1)}, u32[]{:S(2)}, u32[]{:S(2)}) %collective-permute-start.9) | collective-permute-done | bytes 131104 | tf_op jit(solution)/shard_map/ppermute | solution.py:36
  60.0 0.8 copy_bitcast_fusion.k2_ref.v2_ref
  60.8 0.0 collective-permute-done.12.refs_4_
  60.8 8.0 %collective-permute-start.14 = (bf16[1024,256]{1,0:T(8,128)(2,1)S(1)}, bf16[1024,256]{1,0:T(8,128)(2,1)S(1)}, u32[]{:S(2)}, u32[]{:S(2)}) collective-permute-start(bf16[1024,256]{1,0:T(8,128)(2,1)S(1)} %copy-done.1), channel_id=1, source_target_pairs={{0,1},{1,0},{2,3},{3,2},{4,5},{5,4},{6,7},{7,6},{8,9},{9,8},{10,11... | collective-permute-start | bytes 1572872 | tf_op jit(solution)/shard_map/ppermute | solution.py:397
  68.9 0.0 collective-permute-start.15
  68.9 0.5 collective-permute-start.16
  69.4 5.5 %far.5 = (bf16[1024,256]{1,0:T(8,128)(2,1)}, bf16[1024,256]{1,0:T(8,128)(2,1)}) custom-call(s32[1]{0:T(128)} %bitcast.3.lim_ref, bf16[4,1024,256]{2,1,0:T(8,128)(2,1)} %get-tuple-element.58.q_ref, bf16[4,1024,256]{2,1,0:T(8,128)(2,1)} %get-tuple-element.59.n_ref, f32[1024,128]{1,0:T(8,128)} %get-tuple-element.60.lse_ref, ...), custom_call_target="tpu_custom_call" | custom-call | bytes 1000 | tf_op jit(solution)/shard_map/far/pallas_call | solution.py:270
  74.9 2.1 %collective-permute-start.13 = (bf16[1024,256]{1,0:T(8,128)(2,1)}, bf16[1024,256]{1,0:T(8,128)(2,1)S(1)}, u32[]{:S(2)}, u32[]{:S(2)}) collective-permute-start(bf16[1024,256]{1,0:T(8,128)(2,1)} %get-tuple-element.74.refs_2_), channel_id=1, source_target_pairs={{0,2},{2,0},{1,3},{3,1},{4,6},{6,4},{5,7},{7,5},{8,10},{10,8},{9,1... | collective-permute-start | bytes 1572872 | tf_op jit(solution)/shard_map/ppermute | solution.py:397
  77.0 0.4 collective-permute-start.20
  77.3 0.2 collective-permute-start.21
  77.5 0.0 collective-permute-done.15.refs_3_
  77.5 0.4 collective-permute-start.22
  77.8 0.0 collective-permute-done.16.refs_5_
  77.9 0.5 collective-permute-start.18
  78.3 0.7 stack.79.place_ref
  79.0 0.6 stack.87.place_ref
  79.6 8.6 %project.3.refs_14_ = f32[1024,1024]{1,0:T(8,128)} custom-call(s32[6]{0:T(128)} %stack.79.place_ref, bf16[1024,256]{1,0:T(8,128)(2,1)} %far.3.refs_0_, bf16[1024,256]{1,0:T(8,128)(2,1)} %far.4.refs_1_, bf16[1024,256]{1,0:T(8,128)(2,1)} %copy-done.6, bf16[1024,256]{1,0:T(8,128)(2,1)} %copy-done.7, bf16[1024,256]{1,0:T(8,128)(2,1)} %copy-done.3, ...), custom_call_target="tpu_custom_call" | custom-call | bytes 1000 | tf_op jit(solution)/shard_map/project/pallas_call | solution.py:313
  88.3 1.1 collective-permute-done.13.refs_6_
  89.4 0.0 collective-permute-done.20.refs_1_
  89.4 0.0 collective-permute-done.21.refs_3_
  89.4 0.8 copy-done.4
  90.2 10.0 %project.4.refs_6_ = f32[1024,1024]{1,0:T(8,128)} custom-call(s32[7]{0:T(128)} %stack.87.place_ref, bf16[1024,256]{1,0:T(8,128)(2,1)} %copy-done.2, bf16[1024,256]{1,0:T(8,128)(2,1)} %collective-permute-done.20.refs_1_, bf16[1024,256]{1,0:T(8,128)(2,1)} %get-tuple-element.74.refs_2_, bf16[1024,256]{1,0:T(8,128)(2,1)} %collective-permute-done.21.refs_3_, ...), custom_call_target="tpu_custom_call" | custom-call | bytes 1000 | tf_op jit(solution)/shard_map/project/pallas_call | solution.py:313
  100.1 0.5 collective-permute-done.18.refs_1_
  100.6 0.7 collective-permute-start.23
  101.3 0.0 collective-permute-start.17
  101.3 0.7 pad_add_fusion.place_ref
  101.9 1.6 %collective-permute-done.23.refs_2_ = bf16[1024,256]{1,0:T(8,128)(2,1)S(1)} collective-permute-done((bf16[1024,256]{1,0:T(8,128)(2,1)S(1)}, bf16[1024,256]{1,0:T(8,128)(2,1)S(1)}, u32[]{:S(2)}, u32[]{:S(2)}) %collective-permute-start.23) | collective-permute-done | bytes 524320 | tf_op jit(solution)/shard_map/ppermute | solution.py:397
  103.5 0.3 collective-permute-done.17.refs_0_
  103.8 0.5 copy-done.9
  104.3 0.8 copy-done.10
  105.1 7.0 %project.5 = bf16[1024,1024]{1,0:T(8,128)(2,1)} custom-call(s32[3]{0:T(128)} %pad_add_fusion.place_ref, bf16[1024,256]{1,0:T(8,128)(2,1)} %copy-done.10, bf16[1024,256]{1,0:T(8,128)(2,1)} %copy-done.5, bf16[1024,256]{1,0:T(8,128)(2,1)} %copy-done.9, bf16[4096,1024]{1,0:T(8,128)(2,1)} %refs_5_.3, bf16[4096,1024]{1,0:T(8,128)(2,1)} %refs_5_.3, ...), custom_call_target="tpu_custom_call" | custom-call | bytes 1000 | tf_op jit(solution)/shard_map/project/pallas_call | solution.py:313
  (45 shorter events, 0.2 us)
Async XLA Ops:
  0.0 10.9 %copy-start.14 = (s32[4]{0:T(128)S(1)}, s32[4]{0:T(128)}, u32[]{:S(2)}) copy-start(s32[4]{0:T(128)} %constant.73.clone) | copy-start | bytes 52
  0.0 11.0 %copy-start.13 = (s32[8]{0:T(128)S(1)}, s32[8]{0:T(128)}, u32[]{:S(2)}) copy-start(s32[8]{0:T(128)} %constant.72.clone) | copy-start | bytes 100
  0.0 11.0 %copy-start.12 = (s32[64]{0:T(128)S(1)}, s32[64]{0:T(128)}, u32[]{:S(2)}) copy-start(s32[64]{0:T(128)} %param.10) | copy-start | bytes 772
  3.7 14.5 %collective-permute-start = (bf16[2,4,1024]{2,1,0:T(4,128)(2,1)}, bf16[2,4,1024]{2,1,0:T(4,128)(2,1)S(1)}, u32[]{:S(2)}, u32[]{:S(2)}) collective-permute-start(bf16[2,4,1024]{2,1,0:T(4,128)(2,1)} %get-tuple-element.48), channel_id=1, source_target_pairs={{0,32},{32,0},{1,33},{33,1},{2,34},{34,2},{3,35},{35,3},{4,36},{36... | collective-permute-start | bytes 49160 | tf_op jit(solution)/shard_map/ppermute | solution.py:346
  7.2 10.9 %collective-permute-start.1 = (bf16[160,1024]{1,0:T(8,128)(2,1)}, bf16[160,1024]{1,0:T(8,128)(2,1)S(1)}, u32[]{:S(2)}, u32[]{:S(2)}) collective-permute-start(bf16[160,1024]{1,0:T(8,128)(2,1)} %get-tuple-element.49), channel_id=1, source_target_pairs={{0,4},{4,8},{8,12},{12,16},{16,20},{20,24},{24,28},{28,32},{32,36}... | collective-permute-start | bytes 983048 | tf_op jit(solution)/shard_map/ppermute | solution.py:350
  11.7 6.4 %copy-start.11 = (bf16[2,4,1024]{2,1,0:T(4,128)(2,1)S(1)}, bf16[2,4,1024]{2,1,0:T(4,128)(2,1)}, u32[]{:S(2)}) copy-start(bf16[2,4,1024]{2,1,0:T(4,128)(2,1)} %get-tuple-element.48) | copy-start | bytes 49156
  18.2 5.9 %copy-start = (bf16[160,1024]{1,0:T(8,128)(2,1)}, bf16[160,1024]{1,0:T(8,128)(2,1)S(1)}, u32[]{:S(2)}) copy-start(bf16[160,1024]{1,0:T(8,128)(2,1)S(1)} %collective-permute-done.1.pk_ref.pv_ref.pk1_ref.pv1_ref) | copy-start | bytes 983044
  18.2 12.2 %collective-permute-start.2 = (bf16[2,1,8,1024]{3,2,0,1:T(8,128)(2,1)S(1)}, bf16[2,1,8,1024]{3,2,0,1:T(8,128)(2,1)S(1)}, u32[]{:S(2)}, u32[]{:S(2)}) collective-permute-start(bf16[2,1,8,1024]{3,2,0,1:T(8,128)(2,1)S(1)} %maximum_bitcast_fusion), channel_id=1, source_target_pairs={{0,12},{4,16},{8,20},{12,24},{16,28},{20,0},{24,4},{28,8},{1,13},{... | collective-permute-start | bytes 98312 | tf_op jit(solution)/shard_map/ppermute | solution.py:36
  23.8 9.0 %collective-permute-start.3 = (bf16[2,1,8,1024]{3,2,0,1:T(8,128)(2,1)S(1)}, bf16[2,1,8,1024]{3,2,0,1:T(8,128)(2,1)S(1)}, u32[]{:S(2)}, u32[]{:S(2)}) collective-permute-start(bf16[2,1,8,1024]{3,2,0,1:T(8,128)(2,1)S(1)} %maximum_bitcast_fusion), channel_id=1, source_target_pairs={{0,20},{4,24},{8,28},{12,0},{16,4},{20,8},{24,12},{28,16},{1,21},{... | collective-permute-start | bytes 98312 | tf_op jit(solution)/shard_map/ppermute | solution.py:36
  30.4 7.2 %collective-permute-start.5 = (bf16[2,2,8,1024]{3,2,0,1:T(8,128)(2,1)S(1)}, bf16[2,2,8,1024]{3,2,0,1:T(8,128)(2,1)S(1)}, u32[]{:S(2)}, u32[]{:S(2)}) collective-permute-start(bf16[2,2,8,1024]{3,2,0,1:T(8,128)(2,1)S(1)} %pad_maximum_fusion.3), channel_id=1, source_target_pairs={{0,28},{4,0},{8,4},{12,8},{16,12},{20,16},{24,20},{28,24},{1,29},{... | collective-permute-start | bytes 196616 | tf_op jit(solution)/shard_map/ppermute | solution.py:36
  32.8 4.8 %collective-permute-start.4 = (bf16[2,3,8,1024]{3,2,0,1:T(8,128)(2,1)S(1)}, bf16[2,3,8,1024]{3,2,0,1:T(8,128)(2,1)S(1)}, u32[]{:S(2)}, u32[]{:S(2)}) collective-permute-start(bf16[2,3,8,1024]{3,2,0,1:T(8,128)(2,1)S(1)} %pad_maximum_fusion.2), channel_id=1, source_target_pairs={{0,4},{4,8},{8,12},{12,16},{16,20},{20,24},{24,28},{28,0},{1,5},{5... | collective-permute-start | bytes 294920 | tf_op jit(solution)/shard_map/ppermute | solution.py:36
  37.7 5.4 %collective-permute-start.6 = (bf16[2,8,8,512]{3,2,0,1:T(8,128)(2,1)S(1)}, bf16[2,8,8,512]{3,2,0,1:T(8,128)(2,1)S(1)}, u32[]{:S(2)}, u32[]{:S(2)}) collective-permute-start(bf16[2,8,8,512]{3,2,0,1:T(8,128)(2,1)S(1)} %get-tuple-element.80), channel_id=1, source_target_pairs={{0,64},{64,128},{128,192},{192,0},{1,65},{65,129},{129,193},{193,1... | collective-permute-start | bytes 393224 | tf_op jit(solution)/shard_map/ppermute | solution.py:36
  39.2 3.9 %collective-permute-start.7 = (bf16[2,8,8,512]{3,2,0,1:T(8,128)(2,1)S(1)}, bf16[2,8,8,512]{3,2,0,1:T(8,128)(2,1)S(1)}, u32[]{:S(2)}, u32[]{:S(2)}) collective-permute-start(bf16[2,8,8,512]{3,2,0,1:T(8,128)(2,1)S(1)} %get-tuple-element.80), channel_id=1, source_target_pairs={{0,192},{64,0},{128,64},{192,128},{1,193},{65,1},{129,65},{193,129... | collective-permute-start | bytes 393224 | tf_op jit(solution)/shard_map/ppermute | solution.py:36
  40.7 5.4 %collective-permute-start.8 = (bf16[2,8,8,512]{3,2,0,1:T(8,128)(2,1)S(1)}, bf16[2,8,8,512]{3,2,0,1:T(8,128)(2,1)S(1)}, u32[]{:S(2)}, u32[]{:S(2)}) collective-permute-start(bf16[2,8,8,512]{3,2,0,1:T(8,128)(2,1)S(1)} %get-tuple-element.80), channel_id=1, source_target_pairs={{0,128},{64,192},{128,0},{192,64},{1,129},{65,193},{129,1},{193,65... | collective-permute-start | bytes 393224 | tf_op jit(solution)/shard_map/ppermute | solution.py:36
  50.7 10.2 %copy-start.1 = (bf16[1024,256]{1,0:T(8,128)(2,1)S(1)}, bf16[1024,256]{1,0:T(8,128)(2,1)}, u32[]{:S(2)}) copy-start(bf16[1024,256]{1,0:T(8,128)(2,1)} %far.3.refs_0_) | copy-start | bytes 1572868
  50.7 10.2 %collective-permute-start.12 = (bf16[1024,256]{1,0:T(8,128)(2,1)}, bf16[1024,256]{1,0:T(8,128)(2,1)S(1)}, u32[]{:S(2)}, u32[]{:S(2)}) collective-permute-start(bf16[1024,256]{1,0:T(8,128)(2,1)} %far.3.refs_0_), channel_id=1, source_target_pairs={{0,2},{2,0},{1,3},{3,1},{4,6},{6,4},{5,7},{7,5},{8,10},{10,8},{9,1... | collective-permute-start | bytes 1572872 | tf_op jit(solution)/shard_map/ppermute | solution.py:397
  52.0 6.8 %collective-permute-start.10 = (bf16[2,8,8,512]{3,2,0,1:T(8,128)(2,1)S(1)}, bf16[2,8,8,512]{3,2,0,1:T(8,128)(2,1)S(1)}, u32[]{:S(2)}, u32[]{:S(2)}) collective-permute-start(bf16[2,8,8,512]{3,2,0,1:T(8,128)(2,1)S(1)} %get-tuple-element.62), channel_id=1, source_target_pairs={{0,192},{64,0},{128,64},{192,128},{1,193},{65,1},{129,65},{193,129... | collective-permute-start | bytes 393224 | tf_op jit(solution)/shard_map/ppermute | solution.py:36
  53.3 5.5 %collective-permute-start.11 = (bf16[2,8,8,512]{3,2,0,1:T(8,128)(2,1)S(1)}, bf16[2,8,8,512]{3,2,0,1:T(8,128)(2,1)S(1)}, u32[]{:S(2)}, u32[]{:S(2)}) collective-permute-start(bf16[2,8,8,512]{3,2,0,1:T(8,128)(2,1)S(1)} %get-tuple-element.62), channel_id=1, source_target_pairs={{0,128},{64,192},{128,0},{192,64},{1,129},{65,193},{129,1},{193,65... | collective-permute-start | bytes 393224 | tf_op jit(solution)/shard_map/ppermute | solution.py:36
  54.1 5.9 %collective-permute-start.9 = (bf16[2,8,8,512]{3,2,0,1:T(8,128)(2,1)S(1)}, bf16[2,8,8,512]{3,2,0,1:T(8,128)(2,1)S(1)}, u32[]{:S(2)}, u32[]{:S(2)}) collective-permute-start(bf16[2,8,8,512]{3,2,0,1:T(8,128)(2,1)S(1)} %get-tuple-element.62), channel_id=1, source_target_pairs={{0,64},{64,128},{128,192},{192,0},{1,65},{65,129},{129,193},{193,1... | collective-permute-start | bytes 393224 | tf_op jit(solution)/shard_map/ppermute | solution.py:36
  58.7 18.3 %collective-permute-start.19 = (bf16[1024,256]{1,0:T(8,128)(2,1)}, bf16[1024,256]{1,0:T(8,128)(2,1)S(1)}, u32[]{:S(2)}, u32[]{:S(2)}) collective-permute-start(bf16[1024,256]{1,0:T(8,128)(2,1)} %far.4.refs_1_), channel_id=1, source_target_pairs={{0,2},{2,0},{1,3},{3,1},{4,6},{6,4},{5,7},{7,5},{8,10},{10,8},{9,1... | collective-permute-start | bytes 1572872 | tf_op jit(solution)/shard_map/ppermute | solution.py:397
  60.8 14.0 %copy-start.3 = (bf16[1024,256]{1,0:T(8,128)(2,1)}, bf16[1024,256]{1,0:T(8,128)(2,1)S(1)}, u32[]{:S(2)}) copy-start(bf16[1024,256]{1,0:T(8,128)(2,1)S(1)} %collective-permute-done.12.refs_4_) | copy-start | bytes 1572868
  60.8 16.5 %collective-permute-start.14 = (bf16[1024,256]{1,0:T(8,128)(2,1)S(1)}, bf16[1024,256]{1,0:T(8,128)(2,1)S(1)}, u32[]{:S(2)}, u32[]{:S(2)}) collective-permute-start(bf16[1024,256]{1,0:T(8,128)(2,1)S(1)} %copy-done.1), channel_id=1, source_target_pairs={{0,1},{1,0},{2,3},{3,2},{4,5},{5,4},{6,7},{7,6},{8,9},{9,8},{10,11... | collective-permute-start | bytes 1572872 | tf_op jit(solution)/shard_map/ppermute | solution.py:397
  68.9 8.6 %collective-permute-start.15 = (bf16[1024,256]{1,0:T(8,128)(2,1)}, bf16[1024,256]{1,0:T(8,128)(2,1)S(1)}, u32[]{:S(2)}, u32[]{:S(2)}) collective-permute-start(bf16[1024,256]{1,0:T(8,128)(2,1)} %far.4.refs_1_), channel_id=1, source_target_pairs={{0,1},{1,0},{2,3},{3,2},{4,5},{5,4},{6,7},{7,6},{8,9},{9,8},{10,11... | collective-permute-start | bytes 1572872 | tf_op jit(solution)/shard_map/ppermute | solution.py:397
  68.9 9.0 %collective-permute-start.16 = (bf16[1024,256]{1,0:T(8,128)(2,1)S(1)}, bf16[1024,256]{1,0:T(8,128)(2,1)S(1)}, u32[]{:S(2)}, u32[]{:S(2)}) collective-permute-start(bf16[1024,256]{1,0:T(8,128)(2,1)S(1)} %collective-permute-done.12.refs_4_), channel_id=1, source_target_pairs={{0,1},{1,0},{2,3},{3,2},{4,5},{5,4},{6,7},{7,6},{8,9},{9,8},{10,11... | collective-permute-start | bytes 1572872 | tf_op jit(solution)/shard_map/ppermute | solution.py:397
  74.9 14.5 %collective-permute-start.13 = (bf16[1024,256]{1,0:T(8,128)(2,1)}, bf16[1024,256]{1,0:T(8,128)(2,1)S(1)}, u32[]{:S(2)}, u32[]{:S(2)}) collective-permute-start(bf16[1024,256]{1,0:T(8,128)(2,1)} %get-tuple-element.74.refs_2_), channel_id=1, source_target_pairs={{0,2},{2,0},{1,3},{3,1},{4,6},{6,4},{5,7},{7,5},{8,10},{10,8},{9,1... | collective-permute-start | bytes 1572872 | tf_op jit(solution)/shard_map/ppermute | solution.py:397
  77.0 11.3 %copy-start.2 = (bf16[1024,256]{1,0:T(8,128)(2,1)}, bf16[1024,256]{1,0:T(8,128)(2,1)S(1)}, u32[]{:S(2)}) copy-start(bf16[1024,256]{1,0:T(8,128)(2,1)S(1)} %collective-permute-done.19.refs_0_) | copy-start | bytes 1572868
  77.0 12.4 %collective-permute-start.20 = (bf16[1024,256]{1,0:T(8,128)(2,1)S(1)}, bf16[1024,256]{1,0:T(8,128)(2,1)}, u32[]{:S(2)}, u32[]{:S(2)}) collective-permute-start(bf16[1024,256]{1,0:T(8,128)(2,1)S(1)} %collective-permute-done.19.refs_0_), channel_id=1, source_target_pairs={{0,1},{1,0},{2,3},{3,2},{4,5},{5,4},{6,7},{7,6},{8,9},{9,8},{10,11... | collective-permute-start | bytes 1572872 | tf_op jit(solution)/shard_map/ppermute | solution.py:397
  77.3 2.3 %copy-start.6 = (bf16[1024,256]{1,0:T(8,128)(2,1)}, bf16[1024,256]{1,0:T(8,128)(2,1)S(1)}, u32[]{:S(2)}) copy-start(bf16[1024,256]{1,0:T(8,128)(2,1)S(1)} %collective-permute-done.14.refs_2_) | copy-start | bytes 1572868
  77.3 12.0 %collective-permute-start.21 = (bf16[1024,256]{1,0:T(8,128)(2,1)}, bf16[1024,256]{1,0:T(8,128)(2,1)}, u32[]{:S(2)}, u32[]{:S(2)}) collective-permute-start(bf16[1024,256]{1,0:T(8,128)(2,1)} %get-tuple-element.74.refs_2_), channel_id=1, source_target_pairs={{0,1},{1,0},{2,3},{3,2},{4,5},{5,4},{6,7},{7,6},{8,9},{9,8},{10,11... | collective-permute-start | bytes 1572872 | tf_op jit(solution)/shard_map/ppermute | solution.py:397
  77.5 2.2 %copy-start.7 = (bf16[1024,256]{1,0:T(8,128)(2,1)}, bf16[1024,256]{1,0:T(8,128)(2,1)S(1)}, u32[]{:S(2)}) copy-start(bf16[1024,256]{1,0:T(8,128)(2,1)S(1)} %collective-permute-done.15.refs_3_) | copy-start | bytes 1572868
  77.5 11.9 %collective-permute-start.22 = (bf16[1024,256]{1,0:T(8,128)(2,1)}, bf16[1024,256]{1,0:T(8,128)(2,1)}, u32[]{:S(2)}, u32[]{:S(2)}) collective-permute-start(bf16[1024,256]{1,0:T(8,128)(2,1)} %get-tuple-element.75.refs_4_), channel_id=1, source_target_pairs={{0,1},{1,0},{2,3},{3,2},{4,5},{5,4},{6,7},{7,6},{8,9},{9,8},{10,11... | collective-permute-start | bytes 1572872 | tf_op jit(solution)/shard_map/ppermute | solution.py:397
  77.8 1.8 %copy-start.8 = (bf16[1024,256]{1,0:T(8,128)(2,1)}, bf16[1024,256]{1,0:T(8,128)(2,1)S(1)}, u32[]{:S(2)}) copy-start(bf16[1024,256]{1,0:T(8,128)(2,1)S(1)} %collective-permute-done.16.refs_5_) | copy-start | bytes 1572868
  77.9 22.7 %collective-permute-start.18 = (bf16[1024,256]{1,0:T(8,128)(2,1)}, bf16[1024,256]{1,0:T(8,128)(2,1)S(1)}, u32[]{:S(2)}, u32[]{:S(2)}) collective-permute-start(bf16[1024,256]{1,0:T(8,128)(2,1)} %get-tuple-element.75.refs_4_), channel_id=1, source_target_pairs={{0,2},{2,0},{1,3},{3,1},{4,6},{6,4},{5,7},{7,5},{8,10},{10,8},{9,1... | collective-permute-start | bytes 1572872 | tf_op jit(solution)/shard_map/ppermute | solution.py:397
  89.4 0.8 copy-start.4
  100.6 3.2 %copy-start.5 = (bf16[1024,256]{1,0:T(8,128)(2,1)}, bf16[1024,256]{1,0:T(8,128)(2,1)S(1)}, u32[]{:S(2)}) copy-start(bf16[1024,256]{1,0:T(8,128)(2,1)S(1)} %collective-permute-done.18.refs_1_) | copy-start | bytes 1572868
  100.6 2.9 %collective-permute-start.23 = (bf16[1024,256]{1,0:T(8,128)(2,1)S(1)}, bf16[1024,256]{1,0:T(8,128)(2,1)S(1)}, u32[]{:S(2)}, u32[]{:S(2)}) collective-permute-start(bf16[1024,256]{1,0:T(8,128)(2,1)S(1)} %collective-permute-done.18.refs_1_), channel_id=1, source_target_pairs={{0,1},{1,0},{2,3},{3,2},{4,5},{5,4},{6,7},{7,6},{8,9},{9,8},{10,11... | collective-permute-start | bytes 1572872 | tf_op jit(solution)/shard_map/ppermute | solution.py:397
  101.3 2.5 %collective-permute-start.17 = (bf16[1024,256]{1,0:T(8,128)(2,1)}, bf16[1024,256]{1,0:T(8,128)(2,1)S(1)}, u32[]{:S(2)}, u32[]{:S(2)}) collective-permute-start(bf16[1024,256]{1,0:T(8,128)(2,1)} %copy-done.4), channel_id=1, source_target_pairs={{0,1},{1,0},{2,3},{3,2},{4,5},{5,4},{6,7},{7,6},{8,9},{9,8},{10,11... | collective-permute-start | bytes 1572872 | tf_op jit(solution)/shard_map/ppermute | solution.py:397
  103.5 0.8 copy-start.9
  104.3 0.8 copy-start.10

commit v5 on v4

--- a/solution.py
+++ b/solution.py
@@ -298,14 +298,14 @@
     refs[-1][...] = total.astype(refs[-1].dtype)
 
 
-def project(pieces, places, weight, acc, dtype):
+def project(pieces, places, holders, pairs, weight, acc, dtype):
     n = len(pieces)
     rows, width = pieces[0].shape
     cols = weight.shape[1]
     tile = 256
     out_spec = pl.BlockSpec((tile, cols), lambda i, s: (i, 0))
     specs = [pl.BlockSpec((tile, width), lambda i, s: (i, 0)) for _ in pieces]
-    specs += [pl.BlockSpec((width, cols), lambda i, s, j=j: (s[j], 0)) for j in range(n)]
+    specs += [pl.BlockSpec((width, cols), lambda i, s, k=k, p=p: (s[k] * pairs + p, 0)) for k, p in places]
     args = list(pieces) + [weight] * n
     if acc is not None:
         specs.append(out_spec)
@@ -322,7 +322,7 @@
         compiler_params=params(60),
         cost_estimate=cost(0),
         name="project",
-    )(jnp.stack(places).astype(jnp.int32), *args)
+    )(holders, *args)
 
 
 def local(query, key, value, windows, out_weight):
@@ -382,17 +382,12 @@
     last = pairs - 1
     own, across, beside, diagonal = [], [], [], []
 
-    def place(kind, i):
-        base = here if kind < 2 else there
-        return (base + (core if kind % 2 == 0 else 1 - core)) * pairs + i
+    holders = jnp.stack([here + core, here + 1 - core, there + core, there + 1 - core]).astype(jnp.int32)
 
     def add(which, acc, dtype=jnp.float32):
         sets = (own, beside, across, diagonal)
-        pieces, places = [], []
-        for kind, i in which:
-            pieces.append(sets[kind][i])
-            places.append(place(kind, i))
-        return project(pieces, places, out_weight, acc, dtype)
+        pieces = [sets[kind][i] for kind, i in which]
+        return project(pieces, which, holders, pairs, out_weight, acc, dtype)
 
     hop = lambda axis, xs: [lax.ppermute(o, axis, swap) for o in xs]
 

time: 113 us -> 112 us (level)
  local copies, waits for them, and re-layouts: 4.24 us -> 2.31 us
  waiting for transfers between devices: 12.3 us -> 13.6 us
    another operation x2 -> x0, local copies, waits for them, and re-layouts: 1.31 us -> none  [project(): jnp.stack(places).astype(jnp.int32)]
    ppermute x12, waiting for transfers between devices: 3.41 us -> 4.65 us  [local(): hop = lambda axis, xs: [lax.ppermute(o, axis, swap) for o in xs]]
  transfers between devices with their start and end apart: 24 -> 24, of which waited for: 7 -> 7; matrix products, arithmetic and copies ran while one was open for 4% -> 3% of each run, Pallas kernels for 36% -> 36%
where the time goes in v5:
time: 112 us
  Pallas kernels  54.9 us (49%)
  starting transfers between devices  37.2 us (33%)
  waiting for transfers between devices  13.6 us (12%)
  other arithmetic  3.36 us (3%)
  local copies, waits for them, and re-layouts  2.31 us (2%)
    pallas_call x3, Pallas kernels, project(): pl.pallas_call(functools.partial(project_kernel, n, acc is not None), gri...  25.6 us
    ppermute x10, starting transfers between devices, shift(): return lax.ppermute(x, axis, [(i, (i + by) % n) for i in range(n)])  15.9 us
    ppermute x12, starting transfers between devices, local(): hop = lambda axis, xs: [lax.ppermute(o, axis, swap) for o in xs]  14.1 us
    pallas_call x3, Pallas kernels, far(): pl.pallas_call(functools.partial(far_kernel, pair), grid_spec=pltpu.Prefe...  13 us
    pallas_call x2, Pallas kernels, near(): pl.pallas_call(near_kernel, grid_spec=pltpu.PrefetchScalarGridSpec(num_sc...  12.7 us
    ppermute x10, waiting for transfers between devices, shift(): return lax.ppermute(x, axis, [(i, (i + by) % n) for i in range(n)])  8.97 us
    ppermute x12, waiting for transfers between devices, local(): hop = lambda axis, xs: [lax.ppermute(o, axis, swap) for o in xs]  4.65 us
    pallas_call x1, Pallas kernels, pool(): pl.pallas_call(pool_kernel, grid=(1,), in_specs=[spec(block, b) for b in...  3.62 us
  transfers between devices with their start and end apart: 24, of which 7 were waited for; matrix products, arithmetic and copies ran while one was open for 3% of the time, Pallas kernels for 36%

profile of v5, /device:TPU:1, one launch (start us, length us, event | category | flops | bytes accessed | tf_op | source)
XLA Modules:
  0.0 111.6 jit_solution(15146728620944181474)
XLA Ops:
  0.0 3.6 %pool.1 = (bf16[64,1024]{1,0:T(8,128)(2,1)}, bf16[64,1024]{1,0:T(8,128)(2,1)}, bf16[2,4,1024]{2,1,0:T(4,128)(2,1)}, bf16[160,1024]{1,0:T(8,128)(2,1)}) custom-call(bf16[1024,1024]{1,0:T(8,128)(2,1)} %k_ref.3, bf16[1024,1024]{1,0:T(8,128)(2,1)} %k_ref.3, bf16[1024,1024]{1,0:T(8,128)(2,1)} %k_ref.3, bf16[1024,1024]{1,0:T(8,128)(2,1)} %k_ref.3, ...), custom_call_target="tpu_custom_call" | custom-call | bytes 1000 | tf_op jit(solution)/shard_map/pool/pallas_call | solution.py:72
  3.6 3.6 %collective-permute-start = (bf16[2,4,1024]{2,1,0:T(4,128)(2,1)}, bf16[2,4,1024]{2,1,0:T(4,128)(2,1)S(1)}, u32[]{:S(2)}, u32[]{:S(2)}) collective-permute-start(bf16[2,4,1024]{2,1,0:T(4,128)(2,1)} %get-tuple-element.48), channel_id=1, source_target_pairs={{0,32},{32,0},{1,33},{33,1},{2,34},{34,2},{3,35},{35,3},{4,36},{36... | collective-permute-start | bytes 49160 | tf_op jit(solution)/shard_map/ppermute | solution.py:346
  7.2 3.5 %collective-permute-start.1 = (bf16[160,1024]{1,0:T(8,128)(2,1)}, bf16[160,1024]{1,0:T(8,128)(2,1)S(1)}, u32[]{:S(2)}, u32[]{:S(2)}) collective-permute-start(bf16[160,1024]{1,0:T(8,128)(2,1)} %get-tuple-element.49), channel_id=1, source_target_pairs={{0,4},{4,8},{8,12},{12,16},{16,20},{20,24},{24,28},{28,32},{32,36}... | collective-permute-start | bytes 983048 | tf_op jit(solution)/shard_map/ppermute | solution.py:350
  10.8 0.1 pad_add_fusion.1
  10.9 0.1 add_multiply_fusion.1
  11.0 0.1 add_multiply_fusion
  11.0 0.6 add_add_fusion.1
  11.7 6.4 %near.2 = (bf16[4,1024,256]{2,1,0:T(8,128)(2,1)}, f32[1024,128]{1,0:T(8,128)}, bf16[4,1024,256]{2,1,0:T(8,128)(2,1)}) custom-call(s32[66]{0:T(128)} %get-tuple-element.82.info_ref, bf16[1024,1024]{1,0:T(8,128)(2,1)} %q_ref.3, bf16[1024,1024]{1,0:T(8,128)(2,1)} %k_ref.3, bf16[1024,1024]{1,0:T(8,128)(2,1)} %v_ref.3, ...), custom_call_target="tpu_custom_call" | custom-call | bytes 1000 | tf_op jit(solution)/shard_map/near/pallas_call | solution.py:202
  18.1 0.0 collective-permute-done
  18.1 0.0 collective-permute-done.1.pk_ref.pv_ref.pk1_ref.pv1_ref
  18.1 5.6 %collective-permute-start.2 = (bf16[2,1,8,1024]{3,2,0,1:T(8,128)(2,1)S(1)}, bf16[2,1,8,1024]{3,2,0,1:T(8,128)(2,1)S(1)}, u32[]{:S(2)}, u32[]{:S(2)}) collective-permute-start(bf16[2,1,8,1024]{3,2,0,1:T(8,128)(2,1)S(1)} %maximum_bitcast_fusion), channel_id=1, source_target_pairs={{0,12},{4,16},{8,20},{12,24},{16,28},{20,0},{24,4},{28,8},{1,13},{... | collective-permute-start | bytes 98312 | tf_op jit(solution)/shard_map/ppermute | solution.py:36
  23.7 0.3 collective-permute-start.3
  24.0 6.3 %near.3 = (bf16[4,1024,256]{2,1,0:T(8,128)(2,1)}, f32[1024,128]{1,0:T(8,128)}, bf16[4,1024,256]{2,1,0:T(8,128)(2,1)}) custom-call(s32[66]{0:T(128)} %get-tuple-element.81.info_ref, bf16[1024,1024]{1,0:T(8,128)(2,1)} %q_ref.3, bf16[1024,1024]{1,0:T(8,128)(2,1)} %k_ref.3, ...), custom_call_target="tpu_custom_call", output_to_operand_aliasing={{0}: (10, {}), {1}: (11, {}), {2}: (12, {})} | custom-call | bytes 1000 | tf_op jit(solution)/shard_map/near/pallas_call | solution.py:202
  30.3 0.0 collective-permute-done.2
  30.4 2.5 %collective-permute-start.5 = (bf16[2,2,8,1024]{3,2,0,1:T(8,128)(2,1)S(1)}, bf16[2,2,8,1024]{3,2,0,1:T(8,128)(2,1)S(1)}, u32[]{:S(2)}, u32[]{:S(2)}) collective-permute-start(bf16[2,2,8,1024]{3,2,0,1:T(8,128)(2,1)S(1)} %pad_maximum_fusion.3), channel_id=1, source_target_pairs={{0,28},{4,0},{8,4},{12,8},{16,12},{20,16},{24,20},{28,24},{1,29},{... | collective-permute-start | bytes 196616 | tf_op jit(solution)/shard_map/ppermute | solution.py:36
  32.8 0.1 collective-permute-start.4
  32.9 4.6 %collective-permute-done.4 = bf16[2,3,8,1024]{3,2,0,1:T(8,128)(2,1)S(1)} collective-permute-done((bf16[2,3,8,1024]{3,2,0,1:T(8,128)(2,1)S(1)}, bf16[2,3,8,1024]{3,2,0,1:T(8,128)(2,1)S(1)}, u32[]{:S(2)}, u32[]{:S(2)}) %collective-permute-start.4) | collective-permute-done | bytes 98336 | tf_op jit(solution)/shard_map/ppermute | solution.py:36
  37.6 0.0 collective-permute-done.5
  37.6 1.5 %collective-permute-start.6 = (bf16[2,8,8,512]{3,2,0,1:T(8,128)(2,1)S(1)}, bf16[2,8,8,512]{3,2,0,1:T(8,128)(2,1)S(1)}, u32[]{:S(2)}, u32[]{:S(2)}) collective-permute-start(bf16[2,8,8,512]{3,2,0,1:T(8,128)(2,1)S(1)} %get-tuple-element.80), channel_id=1, source_target_pairs={{0,64},{64,128},{128,192},{192,0},{1,65},{65,129},{129,193},{193,1... | collective-permute-start | bytes 393224 | tf_op jit(solution)/shard_map/ppermute | solution.py:36
  39.2 1.5 %collective-permute-start.7 = (bf16[2,8,8,512]{3,2,0,1:T(8,128)(2,1)S(1)}, bf16[2,8,8,512]{3,2,0,1:T(8,128)(2,1)S(1)}, u32[]{:S(2)}, u32[]{:S(2)}) collective-permute-start(bf16[2,8,8,512]{3,2,0,1:T(8,128)(2,1)S(1)} %get-tuple-element.80), channel_id=1, source_target_pairs={{0,192},{64,0},{128,64},{192,128},{1,193},{65,1},{129,65},{193,129... | collective-permute-start | bytes 393224 | tf_op jit(solution)/shard_map/ppermute | solution.py:36
  40.7 1.6 %collective-permute-start.8 = (bf16[2,8,8,512]{3,2,0,1:T(8,128)(2,1)S(1)}, bf16[2,8,8,512]{3,2,0,1:T(8,128)(2,1)S(1)}, u32[]{:S(2)}, u32[]{:S(2)}) collective-permute-start(bf16[2,8,8,512]{3,2,0,1:T(8,128)(2,1)S(1)} %get-tuple-element.80), channel_id=1, source_target_pairs={{0,128},{64,192},{128,0},{192,64},{1,129},{65,193},{129,1},{193,65... | collective-permute-start | bytes 393224 | tf_op jit(solution)/shard_map/ppermute | solution.py:36
  42.3 0.1 iota_add_fusion
  42.4 0.6 add.122.cell_ref
  43.0 0.0 collective-permute-done.6
  43.0 0.0 collective-permute-done.7
  43.0 3.1 %collective-permute-done.8 = bf16[2,8,8,512]{3,2,0,1:T(8,128)(2,1)S(1)} collective-permute-done((bf16[2,8,8,512]{3,2,0,1:T(8,128)(2,1)S(1)}, bf16[2,8,8,512]{3,2,0,1:T(8,128)(2,1)S(1)}, u32[]{:S(2)}, u32[]{:S(2)}) %collective-permute-start.8) | collective-permute-done | bytes 131104 | tf_op jit(solution)/shard_map/ppermute | solution.py:36
  46.1 0.9 copy_bitcast_fusion.1.k2_ref.v2_ref
  46.9 3.7 %far.3.refs_0_ = bf16[1024,256]{1,0:T(8,128)(2,1)} custom-call(s32[1]{0:T(128)} %bitcast.4.lim_ref, bf16[4,1024,256]{2,1,0:T(8,128)(2,1)} %get-tuple-element.58.q_ref, bf16[4,1024,256]{2,1,0:T(8,128)(2,1)} %get-tuple-element.59.n_ref, f32[1024,128]{1,0:T(8,128)} %get-tuple-element.60.lse_ref, bf16[2,256,512]{2,1,0:T(8,128)(2,1)} %copy_bitcast_fusion.1.k2_ref.v2_ref, ...), custom_call_target="tpu_custom_call" | custom-call | bytes 1000 | tf_op jit(solution)/shard_map/far/pallas_call | solution.py:270
  50.7 1.3 %collective-permute-start.12 = (bf16[1024,256]{1,0:T(8,128)(2,1)}, bf16[1024,256]{1,0:T(8,128)(2,1)S(1)}, u32[]{:S(2)}, u32[]{:S(2)}) collective-permute-start(bf16[1024,256]{1,0:T(8,128)(2,1)} %far.3.refs_0_), channel_id=1, source_target_pairs={{0,2},{2,0},{1,3},{3,1},{4,6},{6,4},{5,7},{7,5},{8,10},{10,8},{9,1... | collective-permute-start | bytes 1572872 | tf_op jit(solution)/shard_map/ppermute | solution.py:392
  52.0 1.3 %collective-permute-start.10 = (bf16[2,8,8,512]{3,2,0,1:T(8,128)(2,1)S(1)}, bf16[2,8,8,512]{3,2,0,1:T(8,128)(2,1)S(1)}, u32[]{:S(2)}, u32[]{:S(2)}) collective-permute-start(bf16[2,8,8,512]{3,2,0,1:T(8,128)(2,1)S(1)} %get-tuple-element.62), channel_id=1, source_target_pairs={{0,192},{64,0},{128,64},{192,128},{1,193},{65,1},{129,65},{193,129... | collective-permute-start | bytes 393224 | tf_op jit(solution)/shard_map/ppermute | solution.py:36
  53.3 0.8 collective-permute-start.11
  54.1 0.8 collective-permute-start.9
  54.9 3.8 %far.4.refs_1_ = bf16[1024,256]{1,0:T(8,128)(2,1)} custom-call(s32[1]{0:T(128)} %bitcast.4.lim_ref, bf16[4,1024,256]{2,1,0:T(8,128)(2,1)} %get-tuple-element.58.q_ref, bf16[4,1024,256]{2,1,0:T(8,128)(2,1)} %get-tuple-element.59.n_ref, f32[1024,128]{1,0:T(8,128)} %get-tuple-element.60.lse_ref, bf16[2,256,512]{2,1,0:T(8,128)(2,1)} %copy_bitcast_fusion.1.k2_ref.v2_ref, ...), custom_call_target="tpu_custom_call" | custom-call | bytes 1000 | tf_op jit(solution)/shard_map/far/pallas_call | solution.py:270
  58.7 0.1 collective-permute-start.19
  58.7 0.0 collective-permute-done.10
  58.7 0.0 collective-permute-done.11
  58.7 1.3 %collective-permute-done.9 = bf16[2,8,8,512]{3,2,0,1:T(8,128)(2,1)S(1)} collective-permute-done((bf16[2,8,8,512]{3,2,0,1:T(8,128)(2,1)S(1)}, bf16[2,8,8,512]{3,2,0,1:T(8,128)(2,1)S(1)}, u32[]{:S(2)}, u32[]{:S(2)}) %collective-permute-start.9) | collective-permute-done | bytes 131104 | tf_op jit(solution)/shard_map/ppermute | solution.py:36
  60.0 0.9 copy_bitcast_fusion.k2_ref.v2_ref
  60.9 0.0 collective-permute-done.12.refs_4_
  60.9 8.0 %collective-permute-start.14 = (bf16[1024,256]{1,0:T(8,128)(2,1)S(1)}, bf16[1024,256]{1,0:T(8,128)(2,1)S(1)}, u32[]{:S(2)}, u32[]{:S(2)}) collective-permute-start(bf16[1024,256]{1,0:T(8,128)(2,1)S(1)} %copy-done.1), channel_id=1, source_target_pairs={{0,1},{1,0},{2,3},{3,2},{4,5},{5,4},{6,7},{7,6},{8,9},{9,8},{10,11... | collective-permute-start | bytes 1572872 | tf_op jit(solution)/shard_map/ppermute | solution.py:392
  68.9 0.0 collective-permute-start.15
  68.9 0.5 collective-permute-start.16
  69.4 5.5 %far.5 = (bf16[1024,256]{1,0:T(8,128)(2,1)}, bf16[1024,256]{1,0:T(8,128)(2,1)}) custom-call(s32[1]{0:T(128)} %bitcast.4.lim_ref, bf16[4,1024,256]{2,1,0:T(8,128)(2,1)} %get-tuple-element.58.q_ref, bf16[4,1024,256]{2,1,0:T(8,128)(2,1)} %get-tuple-element.59.n_ref, f32[1024,128]{1,0:T(8,128)} %get-tuple-element.60.lse_ref, ...), custom_call_target="tpu_custom_call" | custom-call | bytes 1000 | tf_op jit(solution)/shard_map/far/pallas_call | solution.py:270
  74.9 2.1 %collective-permute-start.13 = (bf16[1024,256]{1,0:T(8,128)(2,1)}, bf16[1024,256]{1,0:T(8,128)(2,1)S(1)}, u32[]{:S(2)}, u32[]{:S(2)}) collective-permute-start(bf16[1024,256]{1,0:T(8,128)(2,1)} %get-tuple-element.74.refs_2_), channel_id=1, source_target_pairs={{0,2},{2,0},{1,3},{3,1},{4,6},{6,4},{5,7},{7,5},{8,10},{10,8},{9,1... | collective-permute-start | bytes 1572872 | tf_op jit(solution)/shard_map/ppermute | solution.py:392
  77.0 0.0 collective-permute-done.19.refs_0_
  77.0 0.4 collective-permute-start.20
  77.4 0.2 collective-permute-start.21
  77.5 0.4 collective-permute-start.22
  77.9 0.0 collective-permute-done.16.refs_5_
  77.9 0.5 collective-permute-start.18
  78.3 0.6 pad_add_fusion.place_ref
  79.0 8.6 %project.3.refs_14_ = f32[1024,1024]{1,0:T(8,128)} custom-call(s32[4]{0:T(128)} %pad_add_fusion.place_ref, bf16[1024,256]{1,0:T(8,128)(2,1)} %far.3.refs_0_, bf16[1024,256]{1,0:T(8,128)(2,1)} %far.4.refs_1_, bf16[1024,256]{1,0:T(8,128)(2,1)} %copy-done.5, bf16[1024,256]{1,0:T(8,128)(2,1)} %copy-done.6, bf16[1024,256]{1,0:T(8,128)(2,1)} %copy-done.2, ...), custom_call_target="tpu_custom_call" | custom-call | bytes 1000 | tf_op jit(solution)/shard_map/project/pallas_call | solution.py:313
  87.6 1.8 %collective-permute-done.13.refs_6_ = bf16[1024,256]{1,0:T(8,128)(2,1)S(1)} collective-permute-done((bf16[1024,256]{1,0:T(8,128)(2,1)}, bf16[1024,256]{1,0:T(8,128)(2,1)S(1)}, u32[]{:S(2)}, u32[]{:S(2)}) %collective-permute-start.13) | collective-permute-done | bytes 524320 | tf_op jit(solution)/shard_map/ppermute | solution.py:392
  89.4 0.0 collective-permute-done.20.refs_1_
  89.4 0.0 collective-permute-done.21.refs_3_
  89.4 0.8 copy-done.4
  90.2 10.1 %project.4.refs_6_ = f32[1024,1024]{1,0:T(8,128)} custom-call(s32[4]{0:T(128)} %pad_add_fusion.place_ref, bf16[1024,256]{1,0:T(8,128)(2,1)} %copy-done.3, bf16[1024,256]{1,0:T(8,128)(2,1)} %collective-permute-done.20.refs_1_, bf16[1024,256]{1,0:T(8,128)(2,1)} %get-tuple-element.74.refs_2_, bf16[1024,256]{1,0:T(8,128)(2,1)} %collective-permute-done.21.refs_3_, ...), custom_call_target="tpu_custom_call" | custom-call | bytes 1000 | tf_op jit(solution)/shard_map/project/pallas_call | solution.py:313
  100.3 0.4 collective-permute-done.18.refs_1_
  100.6 0.7 collective-permute-start.23
  101.3 0.1 collective-permute-start.17
  101.4 1.4 %collective-permute-done.23.refs_2_ = bf16[1024,256]{1,0:T(8,128)(2,1)S(1)} collective-permute-done((bf16[1024,256]{1,0:T(8,128)(2,1)S(1)}, bf16[1024,256]{1,0:T(8,128)(2,1)S(1)}, u32[]{:S(2)}, u32[]{:S(2)}) %collective-permute-start.23) | collective-permute-done | bytes 524320 | tf_op jit(solution)/shard_map/ppermute | solution.py:392
  102.8 1.0 collective-permute-done.17.refs_0_
  103.8 0.8 copy-done.10
  104.6 7.0 %project.5 = bf16[1024,1024]{1,0:T(8,128)(2,1)} custom-call(s32[4]{0:T(128)} %pad_add_fusion.place_ref, bf16[1024,256]{1,0:T(8,128)(2,1)} %copy-done.10, bf16[1024,256]{1,0:T(8,128)(2,1)} %copy-done.8, bf16[1024,256]{1,0:T(8,128)(2,1)} %copy-done.9, bf16[4096,1024]{1,0:T(8,128)(2,1)} %refs_5_.3, bf16[4096,1024]{1,0:T(8,128)(2,1)} %refs_5_.3, ...), custom_call_target="tpu_custom_call" | custom-call | bytes 1000 | tf_op jit(solution)/shard_map/project/pallas_call | solution.py:313
  (43 shorter events, 0.2 us)
Async XLA Ops:
  0.0 10.8 %copy-start.14 = (s32[4]{0:T(128)S(1)}, s32[4]{0:T(128)}, u32[]{:S(2)}) copy-start(s32[4]{0:T(128)} %constant.72.clone) | copy-start | bytes 52
  0.0 10.9 %copy-start.13 = (s32[8]{0:T(128)S(1)}, s32[8]{0:T(128)}, u32[]{:S(2)}) copy-start(s32[8]{0:T(128)} %constant.71.clone) | copy-start | bytes 100
  0.0 11.0 %copy-start.12 = (s32[64]{0:T(128)S(1)}, s32[64]{0:T(128)}, u32[]{:S(2)}) copy-start(s32[64]{0:T(128)} %param.10) | copy-start | bytes 772
  3.6 14.4 %collective-permute-start = (bf16[2,4,1024]{2,1,0:T(4,128)(2,1)}, bf16[2,4,1024]{2,1,0:T(4,128)(2,1)S(1)}, u32[]{:S(2)}, u32[]{:S(2)}) collective-permute-start(bf16[2,4,1024]{2,1,0:T(4,128)(2,1)} %get-tuple-element.48), channel_id=1, source_target_pairs={{0,32},{32,0},{1,33},{33,1},{2,34},{34,2},{3,35},{35,3},{4,36},{36... | collective-permute-start | bytes 49160 | tf_op jit(solution)/shard_map/ppermute | solution.py:346
  7.2 10.9 %collective-permute-start.1 = (bf16[160,1024]{1,0:T(8,128)(2,1)}, bf16[160,1024]{1,0:T(8,128)(2,1)S(1)}, u32[]{:S(2)}, u32[]{:S(2)}) collective-permute-start(bf16[160,1024]{1,0:T(8,128)(2,1)} %get-tuple-element.49), channel_id=1, source_target_pairs={{0,4},{4,8},{8,12},{12,16},{16,20},{20,24},{24,28},{28,32},{32,36}... | collective-permute-start | bytes 983048 | tf_op jit(solution)/shard_map/ppermute | solution.py:350
  11.7 6.4 %copy-start.11 = (bf16[2,4,1024]{2,1,0:T(4,128)(2,1)S(1)}, bf16[2,4,1024]{2,1,0:T(4,128)(2,1)}, u32[]{:S(2)}) copy-start(bf16[2,4,1024]{2,1,0:T(4,128)(2,1)} %get-tuple-element.48) | copy-start | bytes 49156
  18.1 5.9 %copy-start = (bf16[160,1024]{1,0:T(8,128)(2,1)}, bf16[160,1024]{1,0:T(8,128)(2,1)S(1)}, u32[]{:S(2)}) copy-start(bf16[160,1024]{1,0:T(8,128)(2,1)S(1)} %collective-permute-done.1.pk_ref.pv_ref.pk1_ref.pv1_ref) | copy-start | bytes 983044
  18.1 12.2 %collective-permute-start.2 = (bf16[2,1,8,1024]{3,2,0,1:T(8,128)(2,1)S(1)}, bf16[2,1,8,1024]{3,2,0,1:T(8,128)(2,1)S(1)}, u32[]{:S(2)}, u32[]{:S(2)}) collective-permute-start(bf16[2,1,8,1024]{3,2,0,1:T(8,128)(2,1)S(1)} %maximum_bitcast_fusion), channel_id=1, source_target_pairs={{0,12},{4,16},{8,20},{12,24},{16,28},{20,0},{24,4},{28,8},{1,13},{... | collective-permute-start | bytes 98312 | tf_op jit(solution)/shard_map/ppermute | solution.py:36
  23.7 9.1 %collective-permute-start.3 = (bf16[2,1,8,1024]{3,2,0,1:T(8,128)(2,1)S(1)}, bf16[2,1,8,1024]{3,2,0,1:T(8,128)(2,1)S(1)}, u32[]{:S(2)}, u32[]{:S(2)}) collective-permute-start(bf16[2,1,8,1024]{3,2,0,1:T(8,128)(2,1)S(1)} %maximum_bitcast_fusion), channel_id=1, source_target_pairs={{0,20},{4,24},{8,28},{12,0},{16,4},{20,8},{24,12},{28,16},{1,21},{... | collective-permute-start | bytes 98312 | tf_op jit(solution)/shard_map/ppermute | solution.py:36
  30.4 7.2 %collective-permute-start.5 = (bf16[2,2,8,1024]{3,2,0,1:T(8,128)(2,1)S(1)}, bf16[2,2,8,1024]{3,2,0,1:T(8,128)(2,1)S(1)}, u32[]{:S(2)}, u32[]{:S(2)}) collective-permute-start(bf16[2,2,8,1024]{3,2,0,1:T(8,128)(2,1)S(1)} %pad_maximum_fusion.3), channel_id=1, source_target_pairs={{0,28},{4,0},{8,4},{12,8},{16,12},{20,16},{24,20},{28,24},{1,29},{... | collective-permute-start | bytes 196616 | tf_op jit(solution)/shard_map/ppermute | solution.py:36
  32.8 4.8 %collective-permute-start.4 = (bf16[2,3,8,1024]{3,2,0,1:T(8,128)(2,1)S(1)}, bf16[2,3,8,1024]{3,2,0,1:T(8,128)(2,1)S(1)}, u32[]{:S(2)}, u32[]{:S(2)}) collective-permute-start(bf16[2,3,8,1024]{3,2,0,1:T(8,128)(2,1)S(1)} %pad_maximum_fusion.2), channel_id=1, source_target_pairs={{0,4},{4,8},{8,12},{12,16},{16,20},{20,24},{24,28},{28,0},{1,5},{5... | collective-permute-start | bytes 294920 | tf_op jit(solution)/shard_map/ppermute | solution.py:36
  37.6 5.4 %collective-permute-start.6 = (bf16[2,8,8,512]{3,2,0,1:T(8,128)(2,1)S(1)}, bf16[2,8,8,512]{3,2,0,1:T(8,128)(2,1)S(1)}, u32[]{:S(2)}, u32[]{:S(2)}) collective-permute-start(bf16[2,8,8,512]{3,2,0,1:T(8,128)(2,1)S(1)} %get-tuple-element.80), channel_id=1, source_target_pairs={{0,64},{64,128},{128,192},{192,0},{1,65},{65,129},{129,193},{193,1... | collective-permute-start | bytes 393224 | tf_op jit(solution)/shard_map/ppermute | solution.py:36
  39.2 3.8 %collective-permute-start.7 = (bf16[2,8,8,512]{3,2,0,1:T(8,128)(2,1)S(1)}, bf16[2,8,8,512]{3,2,0,1:T(8,128)(2,1)S(1)}, u32[]{:S(2)}, u32[]{:S(2)}) collective-permute-start(bf16[2,8,8,512]{3,2,0,1:T(8,128)(2,1)S(1)} %get-tuple-element.80), channel_id=1, source_target_pairs={{0,192},{64,0},{128,64},{192,128},{1,193},{65,1},{129,65},{193,129... | collective-permute-start | bytes 393224 | tf_op jit(solution)/shard_map/ppermute | solution.py:36
  40.7 5.4 %collective-permute-start.8 = (bf16[2,8,8,512]{3,2,0,1:T(8,128)(2,1)S(1)}, bf16[2,8,8,512]{3,2,0,1:T(8,128)(2,1)S(1)}, u32[]{:S(2)}, u32[]{:S(2)}) collective-permute-start(bf16[2,8,8,512]{3,2,0,1:T(8,128)(2,1)S(1)} %get-tuple-element.80), channel_id=1, source_target_pairs={{0,128},{64,192},{128,0},{192,64},{1,129},{65,193},{129,1},{193,65... | collective-permute-start | bytes 393224 | tf_op jit(solution)/shard_map/ppermute | solution.py:36
  50.7 10.2 %copy-start.1 = (bf16[1024,256]{1,0:T(8,128)(2,1)S(1)}, bf16[1024,256]{1,0:T(8,128)(2,1)}, u32[]{:S(2)}) copy-start(bf16[1024,256]{1,0:T(8,128)(2,1)} %far.3.refs_0_) | copy-start | bytes 1572868
  50.7 10.2 %collective-permute-start.12 = (bf16[1024,256]{1,0:T(8,128)(2,1)}, bf16[1024,256]{1,0:T(8,128)(2,1)S(1)}, u32[]{:S(2)}, u32[]{:S(2)}) collective-permute-start(bf16[1024,256]{1,0:T(8,128)(2,1)} %far.3.refs_0_), channel_id=1, source_target_pairs={{0,2},{2,0},{1,3},{3,1},{4,6},{6,4},{5,7},{7,5},{8,10},{10,8},{9,1... | collective-permute-start | bytes 1572872 | tf_op jit(solution)/shard_map/ppermute | solution.py:392
  52.0 6.7 %collective-permute-start.10 = (bf16[2,8,8,512]{3,2,0,1:T(8,128)(2,1)S(1)}, bf16[2,8,8,512]{3,2,0,1:T(8,128)(2,1)S(1)}, u32[]{:S(2)}, u32[]{:S(2)}) collective-permute-start(bf16[2,8,8,512]{3,2,0,1:T(8,128)(2,1)S(1)} %get-tuple-element.62), channel_id=1, source_target_pairs={{0,192},{64,0},{128,64},{192,128},{1,193},{65,1},{129,65},{193,129... | collective-permute-start | bytes 393224 | tf_op jit(solution)/shard_map/ppermute | solution.py:36
  53.3 5.5 %collective-permute-start.11 = (bf16[2,8,8,512]{3,2,0,1:T(8,128)(2,1)S(1)}, bf16[2,8,8,512]{3,2,0,1:T(8,128)(2,1)S(1)}, u32[]{:S(2)}, u32[]{:S(2)}) collective-permute-start(bf16[2,8,8,512]{3,2,0,1:T(8,128)(2,1)S(1)} %get-tuple-element.62), channel_id=1, source_target_pairs={{0,128},{64,192},{128,0},{192,64},{1,129},{65,193},{129,1},{193,65... | collective-permute-start | bytes 393224 | tf_op jit(solution)/shard_map/ppermute | solution.py:36
  54.1 5.9 %collective-permute-start.9 = (bf16[2,8,8,512]{3,2,0,1:T(8,128)(2,1)S(1)}, bf16[2,8,8,512]{3,2,0,1:T(8,128)(2,1)S(1)}, u32[]{:S(2)}, u32[]{:S(2)}) collective-permute-start(bf16[2,8,8,512]{3,2,0,1:T(8,128)(2,1)S(1)} %get-tuple-element.62), channel_id=1, source_target_pairs={{0,64},{64,128},{128,192},{192,0},{1,65},{65,129},{129,193},{193,1... | collective-permute-start | bytes 393224 | tf_op jit(solution)/shard_map/ppermute | solution.py:36
  58.7 18.3 %collective-permute-start.19 = (bf16[1024,256]{1,0:T(8,128)(2,1)}, bf16[1024,256]{1,0:T(8,128)(2,1)S(1)}, u32[]{:S(2)}, u32[]{:S(2)}) collective-permute-start(bf16[1024,256]{1,0:T(8,128)(2,1)} %far.4.refs_1_), channel_id=1, source_target_pairs={{0,2},{2,0},{1,3},{3,1},{4,6},{6,4},{5,7},{7,5},{8,10},{10,8},{9,1... | collective-permute-start | bytes 1572872 | tf_op jit(solution)/shard_map/ppermute | solution.py:392
  60.9 14.0 %copy-start.2 = (bf16[1024,256]{1,0:T(8,128)(2,1)}, bf16[1024,256]{1,0:T(8,128)(2,1)S(1)}, u32[]{:S(2)}) copy-start(bf16[1024,256]{1,0:T(8,128)(2,1)S(1)} %collective-permute-done.12.refs_4_) | copy-start | bytes 1572868
  60.9 16.5 %collective-permute-start.14 = (bf16[1024,256]{1,0:T(8,128)(2,1)S(1)}, bf16[1024,256]{1,0:T(8,128)(2,1)S(1)}, u32[]{:S(2)}, u32[]{:S(2)}) collective-permute-start(bf16[1024,256]{1,0:T(8,128)(2,1)S(1)} %copy-done.1), channel_id=1, source_target_pairs={{0,1},{1,0},{2,3},{3,2},{4,5},{5,4},{6,7},{7,6},{8,9},{9,8},{10,11... | collective-permute-start | bytes 1572872 | tf_op jit(solution)/shard_map/ppermute | solution.py:392
  68.9 8.6 %collective-permute-start.15 = (bf16[1024,256]{1,0:T(8,128)(2,1)}, bf16[1024,256]{1,0:T(8,128)(2,1)S(1)}, u32[]{:S(2)}, u32[]{:S(2)}) collective-permute-start(bf16[1024,256]{1,0:T(8,128)(2,1)} %far.4.refs_1_), channel_id=1, source_target_pairs={{0,1},{1,0},{2,3},{3,2},{4,5},{5,4},{6,7},{7,6},{8,9},{9,8},{10,11... | collective-permute-start | bytes 1572872 | tf_op jit(solution)/shard_map/ppermute | solution.py:392
  68.9 9.0 %collective-permute-start.16 = (bf16[1024,256]{1,0:T(8,128)(2,1)S(1)}, bf16[1024,256]{1,0:T(8,128)(2,1)S(1)}, u32[]{:S(2)}, u32[]{:S(2)}) collective-permute-start(bf16[1024,256]{1,0:T(8,128)(2,1)S(1)} %collective-permute-done.12.refs_4_), channel_id=1, source_target_pairs={{0,1},{1,0},{2,3},{3,2},{4,5},{5,4},{6,7},{7,6},{8,9},{9,8},{10,11... | collective-permute-start | bytes 1572872 | tf_op jit(solution)/shard_map/ppermute | solution.py:392
  74.9 14.5 %collective-permute-start.13 = (bf16[1024,256]{1,0:T(8,128)(2,1)}, bf16[1024,256]{1,0:T(8,128)(2,1)S(1)}, u32[]{:S(2)}, u32[]{:S(2)}) collective-permute-start(bf16[1024,256]{1,0:T(8,128)(2,1)} %get-tuple-element.74.refs_2_), channel_id=1, source_target_pairs={{0,2},{2,0},{1,3},{3,1},{4,6},{6,4},{5,7},{7,5},{8,10},{10,8},{9,1... | collective-permute-start | bytes 1572872 | tf_op jit(solution)/shard_map/ppermute | solution.py:392
  77.0 10.5 %copy-start.3 = (bf16[1024,256]{1,0:T(8,128)(2,1)}, bf16[1024,256]{1,0:T(8,128)(2,1)S(1)}, u32[]{:S(2)}) copy-start(bf16[1024,256]{1,0:T(8,128)(2,1)S(1)} %collective-permute-done.19.refs_0_) | copy-start | bytes 1572868
  77.0 12.4 %collective-permute-start.20 = (bf16[1024,256]{1,0:T(8,128)(2,1)S(1)}, bf16[1024,256]{1,0:T(8,128)(2,1)}, u32[]{:S(2)}, u32[]{:S(2)}) collective-permute-start(bf16[1024,256]{1,0:T(8,128)(2,1)S(1)} %collective-permute-done.19.refs_0_), channel_id=1, source_target_pairs={{0,1},{1,0},{2,3},{3,2},{4,5},{5,4},{6,7},{7,6},{8,9},{9,8},{10,11... | collective-permute-start | bytes 1572872 | tf_op jit(solution)/shard_map/ppermute | solution.py:392
  77.4 1.6 %copy-start.5 = (bf16[1024,256]{1,0:T(8,128)(2,1)}, bf16[1024,256]{1,0:T(8,128)(2,1)S(1)}, u32[]{:S(2)}) copy-start(bf16[1024,256]{1,0:T(8,128)(2,1)S(1)} %collective-permute-done.14.refs_2_) | copy-start | bytes 1572868
  77.4 12.0 %collective-permute-start.21 = (bf16[1024,256]{1,0:T(8,128)(2,1)}, bf16[1024,256]{1,0:T(8,128)(2,1)}, u32[]{:S(2)}, u32[]{:S(2)}) collective-permute-start(bf16[1024,256]{1,0:T(8,128)(2,1)} %get-tuple-element.74.refs_2_), channel_id=1, source_target_pairs={{0,1},{1,0},{2,3},{3,2},{4,5},{5,4},{6,7},{7,6},{8,9},{9,8},{10,11... | collective-permute-start | bytes 1572872 | tf_op jit(solution)/shard_map/ppermute | solution.py:392
  77.5 1.5 %copy-start.6 = (bf16[1024,256]{1,0:T(8,128)(2,1)}, bf16[1024,256]{1,0:T(8,128)(2,1)S(1)}, u32[]{:S(2)}) copy-start(bf16[1024,256]{1,0:T(8,128)(2,1)S(1)} %collective-permute-done.15.refs_3_) | copy-start | bytes 1572868
  77.5 11.9 %collective-permute-start.22 = (bf16[1024,256]{1,0:T(8,128)(2,1)}, bf16[1024,256]{1,0:T(8,128)(2,1)}, u32[]{:S(2)}, u32[]{:S(2)}) collective-permute-start(bf16[1024,256]{1,0:T(8,128)(2,1)} %get-tuple-element.75.refs_4_), channel_id=1, source_target_pairs={{0,1},{1,0},{2,3},{3,2},{4,5},{5,4},{6,7},{7,6},{8,9},{9,8},{10,11... | collective-permute-start | bytes 1572872 | tf_op jit(solution)/shard_map/ppermute | solution.py:392
  77.9 1.1 copy-start.7
  77.9 22.7 %collective-permute-start.18 = (bf16[1024,256]{1,0:T(8,128)(2,1)}, bf16[1024,256]{1,0:T(8,128)(2,1)S(1)}, u32[]{:S(2)}, u32[]{:S(2)}) collective-permute-start(bf16[1024,256]{1,0:T(8,128)(2,1)} %get-tuple-element.75.refs_4_), channel_id=1, source_target_pairs={{0,2},{2,0},{1,3},{3,1},{4,6},{6,4},{5,7},{7,5},{8,10},{10,8},{9,1... | collective-permute-start | bytes 1572872 | tf_op jit(solution)/shard_map/ppermute | solution.py:392
  89.4 0.8 copy-start.4
  100.6 3.2 %copy-start.8 = (bf16[1024,256]{1,0:T(8,128)(2,1)}, bf16[1024,256]{1,0:T(8,128)(2,1)S(1)}, u32[]{:S(2)}) copy-start(bf16[1024,256]{1,0:T(8,128)(2,1)S(1)} %collective-permute-done.18.refs_1_) | copy-start | bytes 1572868
  100.6 2.2 %collective-permute-start.23 = (bf16[1024,256]{1,0:T(8,128)(2,1)S(1)}, bf16[1024,256]{1,0:T(8,128)(2,1)S(1)}, u32[]{:S(2)}, u32[]{:S(2)}) collective-permute-start(bf16[1024,256]{1,0:T(8,128)(2,1)S(1)} %collective-permute-done.18.refs_1_), channel_id=1, source_target_pairs={{0,1},{1,0},{2,3},{3,2},{4,5},{5,4},{6,7},{7,6},{8,9},{9,8},{10,11... | collective-permute-start | bytes 1572872 | tf_op jit(solution)/shard_map/ppermute | solution.py:392
  101.3 2.5 %collective-permute-start.17 = (bf16[1024,256]{1,0:T(8,128)(2,1)}, bf16[1024,256]{1,0:T(8,128)(2,1)S(1)}, u32[]{:S(2)}, u32[]{:S(2)}) collective-permute-start(bf16[1024,256]{1,0:T(8,128)(2,1)} %copy-done.4), channel_id=1, source_target_pairs={{0,1},{1,0},{2,3},{3,2},{4,5},{5,4},{6,7},{7,6},{8,9},{9,8},{10,11... | collective-permute-start | bytes 1572872 | tf_op jit(solution)/shard_map/ppermute | solution.py:392
  102.8 1.0 copy-start.9
  103.8 0.8 copy-start.10
